TPU v7x, 128 devices: a whole 4x4x4 slice. The times are simulated.
128 devices in a mesh: grp: 8 (over y, core), seq: 16 (over z, x).
Axes of the slice: x: 4, y: 4, z: 4, core: 2. Of those that a mesh axis runs over, the one named last changes fastest.
Arguments:
- queries: bfloat16 [32, 2, 8192], P('grp', None, 'seq'), may hold values from -12 to 12
- new_kv: bfloat16 [32, 2, 2, 1024], P('grp'), may hold values from -64 to 64
- prefix_keys: bfloat16 [131072, 1024], P(('grp', 'seq')), may hold values from -64 to 64
- prefix_values: bfloat16 [131072, 1024], P(('grp', 'seq')), may hold values from -6 to 6
- suffix_keys: bfloat16 [32, 4096, 1024], P('grp', 'seq'), may hold values from -64 to 64
- suffix_values: bfloat16 [32, 4096, 1024], P('grp', 'seq'), may hold values from -6 to 6
- suffix_lengths: int32 [32], P('grp'), may hold values from 16 to 4096, as said below
- row_slot: int32 [32], replicated, may hold values from 0 to 31, as said below
Outputs:
- attended: bfloat16 [32, 2, 8192], P('grp', None, 'seq')
Inputs may be any that keep to these rules, and one draw needn't show every extreme that they name: Row r's continuation is held in cache slot row_slot[r]; every slot belongs to exactly one row. Slot s holds its first suffix_lengths[s] positions live; at least one slot holds exactly 4096.
All inputs are finite; a program needn't handle non-finite values.
Results may differ from a plain program's by a relative error of at most 0.0095.
Values may be sent and summed in bfloat16 or wider, within the bound.
No kernel may reach another device: no remote copies, remote signals or barrier semaphores. Data moves between devices by JAX's collectives and lax.ppermute only.
A program may use at most 512 MiB of HBM per device.

v0:
```python
import math

import jax
import jax.numpy as jnp
from jax import lax
from jax.sharding import PartitionSpec as P

H = 64
KVH = 8
HEAD = 128


lowest = -1e30


def online_update(state, scores, valid, weigh):
    maximum, denominator, numerator = state
    if valid is not None:
        scores = jnp.where(valid, scores, lowest)
    raised = jnp.maximum(maximum, jnp.max(scores, axis=-1))
    weights = jnp.exp(scores - raised[..., None])
    if valid is not None:
        weights = jnp.where(valid, weights, 0.0)
    shrink = jnp.exp(maximum - raised)
    denominator = denominator * shrink + jnp.sum(weights, axis=-1)
    numerator = numerator * shrink[..., None] + weigh(weights.astype(jnp.bfloat16))
    return (raised, denominator, numerator)


def join_partials(first_part, second_part):
    upper = jnp.maximum(first_part[0], second_part[0])
    first_factor = jnp.exp(first_part[0] - upper)
    second_factor = jnp.exp(second_part[0] - upper)
    denominator = first_part[1] * first_factor + second_part[1] * second_factor
    numerator = first_part[2] * first_factor[..., None] + second_part[2] * second_factor[..., None]
    return (upper, denominator, numerator)


def empty_state(shape):
    return (
        jnp.full(shape, lowest, jnp.float32),
        jnp.zeros(shape, jnp.float32),
        jnp.zeros(shape + (HEAD,), jnp.float32),
    )


def arrange(values, groups, members):
    per_group = values.shape[0] // groups
    own_heads = values.shape[2] // members
    shaped = values.reshape(
        (groups, per_group, values.shape[1], members, own_heads) + values.shape[3:]
    )
    order = (0, 3, 1, 2, 4) + tuple(range(5, shaped.ndim))
    return shaped.transpose(order).reshape(
        (groups * members * per_group, values.shape[1], own_heads) + values.shape[3:]
    )


def per_device(
    queries,
    new_kv,
    prefix_keys,
    prefix_values,
    suffix_keys,
    suffix_values,
    suffix_lengths,
    row_slot,
):
    groups = lax.axis_size("grp")
    members = lax.axis_size("seq")
    group_index = lax.axis_index("grp")
    member_index = lax.axis_index("seq")
    per_group = queries.shape[0]
    steps = queries.shape[1]
    sharing = H // KVH
    own_heads = H // members
    all_rows = per_group * groups
    scale_factor = HEAD ** (-0.5)
    with_heads = lax.all_gather(queries, "seq", axis=2, tiled=True)
    gathered = lax.all_gather(with_heads, "grp", axis=0, tiled=True)
    grouped = gathered.reshape(all_rows, steps, KVH, sharing, HEAD)
    prefix_length = prefix_keys.shape[0]
    prefix_block = math.gcd(prefix_length, 512)

    def prefix_step(number, state):
        key_block = lax.dynamic_slice_in_dim(
            prefix_keys, number * prefix_block, prefix_block, 0
        ).reshape(prefix_block, KVH, HEAD)
        value_block = lax.dynamic_slice_in_dim(
            prefix_values, number * prefix_block, prefix_block, 0
        ).reshape(prefix_block, KVH, HEAD)
        scores = (
            jnp.einsum("rtkgd,jkd->rtkgj", grouped, key_block, preferred_element_type=jnp.float32)
            * scale_factor
        )
        return online_update(
            state,
            scores,
            None,
            lambda weights: jnp.einsum(
                "rtkgj,jkd->rtkgd", weights, value_block, preferred_element_type=jnp.float32
            ),
        )

    prefix_state = lax.fori_loop(
        0, prefix_length // prefix_block, prefix_step, empty_state((all_rows, steps, KVH, sharing))
    )
    slot_ids = group_index * per_group + jnp.arange(per_group, dtype=jnp.int32)
    belongs = row_slot[None, :] == slot_ids[:, None]
    slot_queries = jnp.einsum(
        "jr,rtc->jtc", belongs.astype(jnp.bfloat16), gathered, preferred_element_type=jnp.float32
    )
    slot_queries = slot_queries.astype(jnp.bfloat16).reshape(per_group, steps, KVH, sharing, HEAD)
    span = suffix_keys.shape[1]
    suffix_block = math.gcd(span, 512)
    live_here = jnp.clip(suffix_lengths - member_index * span, 0, span)

    def suffix_step(number, state):
        key_block = suffix_keys.reshape(per_group, suffix_block, KVH, HEAD)
        value_block = suffix_values.reshape(per_group, suffix_block, KVH, HEAD)
        scores = (
            jnp.einsum(
                "jtkgd,jukd->jtkgu", slot_queries, key_block, preferred_element_type=jnp.float32
            )
            * scale_factor
        )
        positions = number * suffix_block + jnp.arange(suffix_block, dtype=jnp.int32)
        valid = (positions[None, :] < live_here[:, None])[:, None, None, None, :]
        return online_update(
            state,
            scores,
            valid,
            lambda weights: jnp.einsum(
                "jtkgu,jukd->jtkgd", weights, value_block, preferred_element_type=jnp.float32
            ),
        )

    block_count = span // suffix_block
    slot_state = lax.fori_loop(
        0, block_count, suffix_step, empty_state((per_group, steps, KVH, sharing))
    )
    placement = belongs.astype(jnp.float32)
    in_group = jnp.any(belongs, axis=0)
    highest = lax.Precision.HIGHEST
    spread_max = jnp.einsum("jr,jtkg->rtkg", placement, slot_state[0], precision=highest)
    rows_max = jnp.where(in_group[:, None, None, None], spread_max, lowest)
    rows_den = jnp.einsum("jr,jtkg->rtkg", placement, slot_state[1], precision=highest)
    rows_num = jnp.einsum("jr,jtkgd->rtkgd", placement, slot_state[2], precision=highest)
    local = join_partials(prefix_state, (rows_max, rows_den, rows_num))
    flat_max = local[0].reshape(all_rows, steps, H)
    flat_den = local[1].reshape(all_rows, steps, H)
    flat_num = local[2].reshape(all_rows, steps, H, HEAD)
    received = (
        lax.all_to_all(
            arrange(flat_max, groups, members),
            ("grp", "seq"),
            split_axis=0,
            concat_axis=0,
            tiled=True,
        ),
        lax.all_to_all(
            arrange(flat_den, groups, members),
            ("grp", "seq"),
            split_axis=0,
            concat_axis=0,
            tiled=True,
        ),
        lax.all_to_all(
            arrange(flat_num, groups, members),
            ("grp", "seq"),
            split_axis=0,
            concat_axis=0,
            tiled=True,
        ),
    )
    sources = groups * members
    pieces = tuple(
        (
            member_part.reshape((sources, per_group) + member_part.shape[1:])
            for member_part in received
        )
    )
    upper = jnp.max(pieces[0], axis=0)
    factor = jnp.exp(pieces[0] - upper[None])
    owned = (
        upper,
        jnp.sum(pieces[1] * factor, axis=0),
        jnp.sum(pieces[2] * factor[..., None], axis=0),
    )
    own_queries = queries.reshape(per_group, steps, own_heads, HEAD)
    new_keys = jnp.repeat(new_kv[:, :, 0].reshape(per_group, steps, KVH, HEAD), sharing, axis=2)
    new_keys = lax.dynamic_slice_in_dim(new_keys, member_index * own_heads, own_heads, 2)
    new_values = jnp.repeat(new_kv[:, :, 1].reshape(per_group, steps, KVH, HEAD), sharing, axis=2)
    new_values = lax.dynamic_slice_in_dim(new_values, member_index * own_heads, own_heads, 2)
    new_scores = (
        jnp.einsum("rthd,ruhd->rthu", own_queries, new_keys, preferred_element_type=jnp.float32)
        * scale_factor
    )
    causal = (jnp.arange(steps)[None, :] <= jnp.arange(steps)[:, None])[None, :, None, :]
    new_state = online_update(
        empty_state((per_group, steps, own_heads)),
        new_scores,
        causal,
        lambda weights: jnp.einsum(
            "rthu,ruhd->rthd", weights, new_values, preferred_element_type=jnp.float32
        ),
    )
    final = join_partials(owned, new_state)
    result = final[2] / final[1][..., None]
    return result.reshape(per_group, steps, own_heads * HEAD).astype(jnp.bfloat16)


def solution(mesh):
    placed = (
        P("grp", None, "seq"),
        P("grp", None, None, None),
        P(("grp", "seq"), None),
        P(("grp", "seq"), None),
        P("grp", "seq", None),
        P("grp", "seq", None),
        P("grp"),
        P(),
    )
    return jax.shard_map(
        per_device, mesh=mesh, in_specs=placed, out_specs=P("grp", None, "seq"), check_vma=False
    )
```

profile of v0, /device:TPU:0, one launch (start us, length us, event | category | flops | bytes accessed | tf_op | source)
XLA Modules:
  0.0 177.5 jit_solution(5764073923974659053)
XLA Ops:
  6.5 27.4 %all_gather.6 = bf16[4,2,8192]{2,1,0:T(2,128)(2,1)} all-gather(bf16[4,2,512]{2,1,0:T(2,128)(2,1)} %param.10), channel_id=1, replica_groups=mesh['grp'=8,'seq'=16] {'seq'}, dimensions={2}, use_global_device_ids=true | all-gather | bytes 139264 | tf_op jit(solution)/shard_map/all_gather | solution.py:79
  34.0 3.7 %copy.213 = bf16[128,8,8,128]{3,2,1,0:T(8,128)(2,1)} copy(bf16[128,8,8,128]{3,1,2,0:T(8,128)(2,1)} %bitcast.147) | data formatting | bytes 4194304
  37.7 2.0 %copy.214 = bf16[128,8,8,128]{3,2,1,0:T(8,128)(2,1)} copy(bf16[128,8,8,128]{3,1,2,0:T(8,128)(2,1)S(1)} %bitcast.148) | data formatting | bytes 4194304
  39.9 1.9 %bitcast_bitcast_fusion.1 = bf16[4,256,8,128,1]{3,2,1,0,4:T(8,128)(2,1)S(1)} fusion(bf16[4,256,8,128]{3,2,1,0:T(8,128)(2,1)} %bitcast.143), kind=kLoop, calls=%fused_computation.19 | loop fusion | bytes 4194304 | tf_op jit(solution)/shard_map/while/body/eval_jaxpr/reshape | solution.py:119
  41.8 0.4 copy-done.3
  42.1 1.5 bitcast_bitcast_fusion
  43.6 12.8 %all-gather.2.cloned.1.call-done = bf16[32,2,8192]{2,1,0:T(2,128)(2,1)} async-done(((bf16[4,2,8192]{2,1,0:T(2,128)(2,1)}), bf16[32,2,8192]{2,1,0:T(2,128)(2,1)}) %all-gather.2.cloned.1.call-update) | async-done | bytes 1048592 | tf_op jit(solution)/shard_map/all_gather | solution.py:80
  56.5 2.7 %reshape.143 = bf16[32,2,8,8,128]{4,3,2,1,0:T(8,128)(2,1)} reshape(bf16[32,2,8192]{2,1,0:T(2,128)(2,1)} %all-gather.2.cloned.1.call-done) | data formatting | bytes 2097152 | tf_op jit(solution)/shard_map/reshape | solution.py:81
  59.2 2.9 %copy.145 = bf16[32,2,8,8,128]{4,0,3,1,2:T(8,128)(2,1)} copy(bf16[32,2,8,8,128]{4,3,2,1,0:T(8,128)(2,1)} %reshape.143) | data formatting | bytes 2097152
  62.1 1.2 convolution_convert_fusion
  63.3 0.2 reshape.144
  63.5 0.8 fusion.68
  64.3 0.3 fusion.40
  64.6 0.6 copy_add_fusion
  65.2 0.6 copy.155
  65.8 24.1 %while.5 = (s32[]{:T(128)}, f32[32,2,8,8]{0,3,1,2:T(8,128)S(1)}, f32[32,2,8,8]{0,3,1,2:T(8,128)S(1)}, f32[32,2,8,8,128]{4,0,3,1,2:T(8,128)}, bf16[1024,1024]{1,0...) while((s32[]{:T(128)}, f32[32,2,8,8]{0,3,1,2:T(8,128)S(1)}, ...), condition=%wide.region_3.0_spmd.clone, body=%wide.region_0.0_spmd.clone.sunk | while | flops 1092112384 | bytes 57934056 | solution.py:105
  65.8 1.7 constant_dynamic-slice_fusion.3
  67.5 0.5 copy.271
  68.1 0.5 copy.272
  68.6 2.5 %bitcast_reduce_fusion.2 = (f32[32,2,8,8]{0,3,1,2:T(8,128)S(1)}, f32[8,512,32,2,8]{1,2,4,3,0:T(8,128)S(1)}) fusion(bf16[512,8,128,1,1]{0,2,4,3,1:T(8,128)(2,1)S(1)} %bitcast.138, bf16[32,2,8,8,128]{4,0,3,1,2:T(8,128)(2,1)} %get-tuple-element.346), kind=kOutput, calls=%fused_computation.1.clone.1 | convolution fusion | flops 541061120 | bytes 10502144 | tf_op jit(solution)/shard_map/while/body/eval_jaxpr/rtkgd,jkd->rtkgj/dot_general | solution.py:93
  71.2 2.2 %fusion.83 = f32[32,2,8,8]{0,3,1,2:T(8,128)S(1)} fusion(f32[8,512,32,2,8]{1,2,4,3,0:T(8,128)S(1)} %get-tuple-element.315, f32[32,2,8,8]{0,3,1,2:T(8,128)S(1)} %select_maximum_fusion.2), kind=kLoop, calls=%fused_computation.4.clone.1 | loop fusion | flops 6287360 | bytes 8421376 | tf_op jit(solution)/shard_map/while/body/eval_jaxpr/reduce_sum | solution.py:25
  73.4 3.1 %bitcast_add_fusion.2 = f32[32,2,8,8,128]{4,0,3,1,2:T(8,128)S(1)} fusion(f32[32,2,8,8,128]{4,0,3,1,2:T(8,128)S(1)} %copy-done, bf16[512,8,128,1,1]{0,2,4,3,1:T(8,128)(2,1)S(1)} %bitcast.139, f32[8,512,32,2,8]{1,2,4,3,0:T(8,128)S(1)} %get-tuple-element.315, f32[32,2,8,8]{0,3,1,2:T(8,128)S(1)} %select_maximum_fusion.2, ...), kind=kOutput, calls=%fused_computation.8.clone.1 | convolution fusion | flops 544735232 | bytes 13664257 | tf_op jit(solution)/shard_map/while/body/eval_jaxpr/rtkgj,jkd->rtkgd/dot_general | solution.py:100
  76.6 1.3 copy-done.1
  77.9 1.7 constant_dynamic-slice_fusion.3
  79.6 0.5 copy.271
  80.1 0.5 copy.272
  80.7 2.5 %bitcast_reduce_fusion.2 = (f32[32,2,8,8]{0,3,1,2:T(8,128)S(1)}, f32[8,512,32,2,8]{1,2,4,3,0:T(8,128)S(1)}) fusion(bf16[512,8,128,1,1]{0,2,4,3,1:T(8,128)(2,1)S(1)} %bitcast.138, bf16[32,2,8,8,128]{4,0,3,1,2:T(8,128)(2,1)} %get-tuple-element.346), kind=kOutput, calls=%fused_computation.1.clone.1 | convolution fusion | flops 541061120 | bytes 10502144 | tf_op jit(solution)/shard_map/while/body/eval_jaxpr/rtkgd,jkd->rtkgj/dot_general | solution.py:93
  83.3 2.2 %fusion.83 = f32[32,2,8,8]{0,3,1,2:T(8,128)S(1)} fusion(f32[8,512,32,2,8]{1,2,4,3,0:T(8,128)S(1)} %get-tuple-element.315, f32[32,2,8,8]{0,3,1,2:T(8,128)S(1)} %select_maximum_fusion.2), kind=kLoop, calls=%fused_computation.4.clone.1 | loop fusion | flops 6287360 | bytes 8421376 | tf_op jit(solution)/shard_map/while/body/eval_jaxpr/reduce_sum | solution.py:25
  85.5 3.1 %bitcast_add_fusion.2 = f32[32,2,8,8,128]{4,0,3,1,2:T(8,128)S(1)} fusion(f32[32,2,8,8,128]{4,0,3,1,2:T(8,128)S(1)} %copy-done, bf16[512,8,128,1,1]{0,2,4,3,1:T(8,128)(2,1)S(1)} %bitcast.139, f32[8,512,32,2,8]{1,2,4,3,0:T(8,128)S(1)} %get-tuple-element.315, f32[32,2,8,8]{0,3,1,2:T(8,128)S(1)} %select_maximum_fusion.2, ...), kind=kOutput, calls=%fused_computation.8.clone.1 | convolution fusion | flops 544735232 | bytes 13664257 | tf_op jit(solution)/shard_map/while/body/eval_jaxpr/rtkgj,jkd->rtkgd/dot_general | solution.py:100
  88.6 1.3 copy-done.1
  89.9 0.3 copy_maximum_fusion
  90.2 0.2 reshape_reshape.10
  90.4 2.4 %copy.196 = f32[8,16,4,2,4]{4,3,2,1,0:T(2,128)} copy(f32[8,16,4,2,4]{2,0,4,1,3:T(8,128)S(1)} %bitcast.152) | data formatting | bytes 32768 | tf_op jit(solution)/shard_map/reshape | solution.py:54
  92.8 8.5 %all-to-all-start.1 = ((f32[512,2,4]{2,1,0:T(2,128)}), f32[512,2,4]{2,1,0:T(2,128)S(1)}, u32[]{:S(2)}, u32[]{:S(2)}) async-start(f32[512,2,4]{2,1,0:T(2,128)} %bitcast.151), calls=%async_computation.1 | async-start | bytes 1048576 | tf_op jit(solution)/shard_map/all_to_all | solution.py:154
  101.3 1.9 %fusion.29 = f32[4,2,8,8,128]{4,3,1,2,0:T(8,128)} fusion(bf16[4,256,8,128,1]{3,2,1,0,4:T(8,128)(2,1)S(1)} %copy-done.8, f32[4,2,8,8,256]{4,3,1,2,0:T(8,128)S(1)} %copy-done.6, f32[4,2,8,8]{3,1,2,0:T(2,128)S(1)} %copy.156, pred[4,256]{1,0:T(4,128)(4,1)S(1)} %iota_compare_fusion, f32[4,2,8,8]{3,1,2,0:T(2,128)} %copy.155), kind=kOutput, calls=%fused_computation.32 | convolution fusion | flops 34013184 | bytes 2888704 | tf_op jit(solution)/shard_map/while/body/eval_jaxpr/jtkgu,jukd->jtkgd/dot_general | solution.py:133
  103.3 0.3 fusion.32
  103.5 0.2 reshape_reshape.11
  103.7 2.4 %copy.198 = f32[8,16,4,2,4]{4,3,2,1,0:T(2,128)} copy(f32[8,16,4,2,4]{2,0,4,1,3:T(8,128)S(1)} %bitcast.153) | data formatting | bytes 32768 | tf_op jit(solution)/shard_map/reshape | solution.py:54
  106.2 8.8 %all-to-all-done.1 = f32[512,2,4]{2,1,0:T(2,128)S(1)} async-done(((f32[512,2,4]{2,1,0:T(2,128)}), f32[512,2,4]{2,1,0:T(2,128)S(1)}, u32[]{:S(2)}, u32[]{:S(2)}) %all-to-all-start.1) | async-done | bytes 16416 | tf_op jit(solution)/shard_map/all_to_all | solution.py:154
  114.9 4.8 %all-to-all-start.2 = ((f32[512,2,4]{2,1,0:T(2,128)}), f32[512,2,4]{2,1,0:T(2,128)S(1)}, u32[]{:S(2)}, u32[]{:S(2)}) async-start(f32[512,2,4]{2,1,0:T(2,128)} %bitcast.150), calls=%async_computation.2 | async-start | bytes 1048576 | tf_op jit(solution)/shard_map/all_to_all | solution.py:161
  119.7 3.8 %fusion.16 = f32[32,2,8,8,128]{4,0,3,2,1:T(8,128)S(1)} fusion(f32[32,2,8,8,128]{4,0,3,1,2:T(8,128)S(1)} %copy-done.2, f32[32,2,8,8]{0,3,2,1:T(8,128)S(1)} %get-tuple-element.256, f32[32,2,8,8]{0,3,2,1:T(8,128)S(1)} %get-tuple-element.255, f32[4,2,8,8,128]{4,3,1,2,0:T(8,128)} %fusion.29, s32[32]{0:T(128)S(1)} %copy-done.12, s32[4]{0:T(128)S(1)} %iota_add_fusion), kind=kOutput, calls=%fused_computation.27 | convolution fusion | flops 26738816 | bytes 4489360 | tf_op jit(solution)/shard_map/jr,jtkgd->rtkgd/dot_general | solution.py:148
  123.5 0.6 copy.159
  124.1 2.7 %copy.160 = f32[512,2,4,128]{3,2,1,0:T(4,128)} copy(f32[512,2,4,128]{3,0,2,1:T(8,128)S(1)} %bitcast.144) | data formatting | bytes 4194304 | tf_op jit(solution)/shard_map/reshape | solution.py:54
  126.8 6.5 %all-to-all-done.2 = f32[512,2,4]{2,1,0:T(2,128)S(1)} async-done(((f32[512,2,4]{2,1,0:T(2,128)}), f32[512,2,4]{2,1,0:T(2,128)S(1)}, u32[]{:S(2)}, u32[]{:S(2)}) %all-to-all-start.2) | async-done | bytes 16416 | tf_op jit(solution)/shard_map/all_to_all | solution.py:161
  133.3 0.8 copy-done.9
  134.1 4.6 %all-to-all-start = ((f32[512,2,4,128]{3,2,1,0:T(4,128)}), f32[512,2,4,128]{3,2,1,0:T(4,128)S(1)}, u32[]{:S(2)}, u32[]{:S(2)}) async-start(f32[512,2,4,128]{3,2,1,0:T(4,128)} %copy.160), calls=%async_computation | async-start | bytes 4194304 | tf_op jit(solution)/shard_map/all_to_all | solution.py:168
  138.8 0.2 slice_reduce_fusion
  139.0 0.1 fusion.50
  139.2 0.1 copy.167
  139.4 0.1 copy.169
  139.5 0.1 copy.174
  139.8 0.1 copy.175
  140.0 2.0 %copy.197 = f32[128,4,2,4]{1,0,3,2:T(8,128)S(1)} copy(f32[128,4,2,4]{3,2,1,0:T(2,128)S(1)} %bitcast.145) | data formatting | bytes 32768 | tf_op jit(solution)/shard_map/reshape | solution.py:179
  141.9 0.3 reduce_max.42
  142.2 0.1 copy.208
  142.3 3.7 %copy.199 = f32[128,4,2,4]{1,0,3,2:T(8,128)} copy(f32[128,4,2,4]{3,2,1,0:T(2,128)} %bitcast.149) | data formatting | bytes 32768 | tf_op jit(solution)/shard_map/reshape | solution.py:179
  146.0 1.2 multiply_reduce_fusion
  147.2 0.1 copy.185
  147.3 0.1 copy.170
  147.5 0.1 copy.176
  147.6 0.1 copy.172
  147.7 20.8 %all-to-all-done = f32[512,2,4,128]{3,2,1,0:T(4,128)S(1)} async-done(((f32[512,2,4,128]{3,2,1,0:T(4,128)}), f32[512,2,4,128]{3,2,1,0:T(4,128)S(1)}, u32[]{:S(2)}, u32[]{:S(2)}) %all-to-all-start) | async-done | bytes 2097184 | tf_op jit(solution)/shard_map/all_to_all | solution.py:168
  168.5 1.3 fusion.15
  169.9 0.8 fusion.38
  (55 shorter events, 0.9 us)
Async XLA Ops:
  6.5 49.9 %all-gather.2.cloned.1.call-start = ((), (), s32[]{:S(2)}) async-start(), calls=%async_computation.3 | async-start | bytes 1179648 | tf_op jit(solution)/shard_map/all_gather | solution.py:80
  34.0 3.7 %copy-start.7 = (bf16[4,256,1024]{2,1,0:T(8,128)(2,1)S(1)}, bf16[4,256,1024]{2,1,0:T(8,128)(2,1)}, u32[]{:S(2)}) copy-start(bf16[4,256,1024]{2,1,0:T(8,128)(2,1)} %param.15) | copy-start | bytes 6291460
  37.7 2.0 %copy-start.12 = (s32[32]{0:T(128)S(1)}, s32[32]{0:T(128)}, u32[]{:S(2)}) copy-start(s32[32]{0:T(128)} %param.17) | copy-start | bytes 388
  37.7 2.1 %copy-start.14 = (s32[4]{0:T(128)S(1)}, s32[4]{0:T(128)}, u32[]{:S(2)}) copy-start(s32[4]{0:T(128)} %param.16) | copy-start | bytes 52
  39.9 2.3 %copy-start.3 = (bf16[128,8,8,128]{3,2,1,0:T(8,128)(2,1)S(1)}, bf16[128,8,8,128]{3,2,1,0:T(8,128)(2,1)}, u32[]{:S(2)}) copy-start(bf16[128,8,8,128]{3,2,1,0:T(8,128)(2,1)} %copy.214) | copy-start | bytes 6291460
  56.5 5.6 %copy-start.4 = (bf16[32,2,8192]{2,1,0:T(2,128)(2,1)S(1)}, bf16[32,2,8192]{2,1,0:T(2,128)(2,1)}, u32[]{:S(2)}) copy-start(bf16[32,2,8192]{2,1,0:T(2,128)(2,1)} %all-gather.2.cloned.1.call-done) | copy-start | bytes 3145732
  64.2 1.6 copy-start.5
  71.2 2.2 %copy-start = (f32[32,2,8,8,128]{4,0,3,1,2:T(8,128)S(1)}, f32[32,2,8,8,128]{4,0,3,1,2:T(8,128)}, u32[]{:S(2)}) copy-start(f32[32,2,8,8,128]{4,0,3,1,2:T(8,128)} %get-tuple-element.333) | copy-start | bytes 6291460 | tf_op jit(solution)/shard_map/while
  76.6 1.3 copy-start.1
  83.2 2.2 %copy-start = (f32[32,2,8,8,128]{4,0,3,1,2:T(8,128)S(1)}, f32[32,2,8,8,128]{4,0,3,1,2:T(8,128)}, u32[]{:S(2)}) copy-start(f32[32,2,8,8,128]{4,0,3,1,2:T(8,128)} %get-tuple-element.333) | copy-start | bytes 6291460 | tf_op jit(solution)/shard_map/while
  88.6 1.3 copy-start.1
  89.9 11.4 %copy-start.6 = (f32[4,2,8,8,256]{4,3,1,2,0:T(8,128)S(1)}, f32[4,2,8,8,256]{4,3,1,2,0:T(8,128)}, u32[]{:S(2)}) copy-start(f32[4,2,8,8,256]{4,3,1,2,0:T(8,128)} %copy-done.5) | copy-start | bytes 1572868
  89.9 11.4 %copy-start.8 = (bf16[4,256,8,128,1]{3,2,1,0,4:T(8,128)(2,1)S(1)}, bf16[4,256,8,128,1]{3,2,1,0,4:T(8,128)(2,1)}, u32[]{:S(2)}) copy-start(bf16[4,256,8,128,1]{3,2,1,0,4:T(8,128)(2,1)} %bitcast_bitcast_fusion) | copy-start | bytes 6291460
  92.8 22.1 %all-to-all-start.1 = ((f32[512,2,4]{2,1,0:T(2,128)}), f32[512,2,4]{2,1,0:T(2,128)S(1)}, u32[]{:S(2)}, u32[]{:S(2)}) async-start(f32[512,2,4]{2,1,0:T(2,128)} %bitcast.151), calls=%async_computation.1 | async-start | bytes 1048576 | tf_op jit(solution)/shard_map/all_to_all | solution.py:154
  101.3 1.9 %copy-start.11 = (f32[4,2,8,8]{3,2,1,0:T(8,128)S(1)}, f32[4,2,8,8]{3,2,1,0:T(8,128)}, u32[]{:S(2)}) copy-start(f32[4,2,8,8]{3,2,1,0:T(8,128)} %get-tuple-element.257) | copy-start | bytes 6148
  103.3 16.5 %copy-start.2 = (f32[32,2,8,8,128]{4,0,3,1,2:T(8,128)S(1)}, f32[32,2,8,8,128]{4,0,3,1,2:T(8,128)}, u32[]{:S(2)}) copy-start(f32[32,2,8,8,128]{4,0,3,1,2:T(8,128)} %get-tuple-element.158) | copy-start | bytes 6291460
  114.9 18.4 %all-to-all-start.2 = ((f32[512,2,4]{2,1,0:T(2,128)}), f32[512,2,4]{2,1,0:T(2,128)S(1)}, u32[]{:S(2)}, u32[]{:S(2)}) async-start(f32[512,2,4]{2,1,0:T(2,128)} %bitcast.150), calls=%async_computation.2 | async-start | bytes 1048576 | tf_op jit(solution)/shard_map/all_to_all | solution.py:161
  126.8 12.0 %copy-start.10 = (bf16[4,2,2,1024]{3,2,1,0:T(2,128)(2,1)S(1)}, bf16[4,2,2,1024]{3,2,1,0:T(2,128)(2,1)}, u32[]{:S(2)}) copy-start(bf16[4,2,2,1024]{3,2,1,0:T(2,128)(2,1)} %param.11) | copy-start | bytes 98308
  126.8 12.2 %copy-start.13 = (bf16[4,2,512]{2,1,0:T(2,128)(2,1)S(1)}, bf16[4,2,512]{2,1,0:T(2,128)(2,1)}, u32[]{:S(2)}) copy-start(bf16[4,2,512]{2,1,0:T(2,128)(2,1)} %param.10) | copy-start | bytes 24580
  133.3 0.8 copy-start.9
  134.1 34.4 %all-to-all-start = ((f32[512,2,4,128]{3,2,1,0:T(4,128)}), f32[512,2,4,128]{3,2,1,0:T(4,128)S(1)}, u32[]{:S(2)}, u32[]{:S(2)}) async-start(f32[512,2,4,128]{3,2,1,0:T(4,128)} %copy.160), calls=%async_computation | async-start | bytes 4194304 | tf_op jit(solution)/shard_map/all_to_all | solution.py:168
Sparse Core Ops, SparseCore 0:
  34.1 22.3 all-gather.1
where the time goes:
time: 178 us
  waiting for transfers between devices  49 us (28%)
  local copies, waits for them, and re-layouts  40.4 us (23%)
  blocking collectives  27.4 us (15%)
  matrix products  20.4 us (11%)
  starting transfers between devices  18 us (10%)
  between operations  13.7 us (8%)
  other arithmetic  8.55 us (5%)
    all_gather x1, blocking collectives, per_device(): with_heads = lax.all_gather(queries, 'seq', axis=2, tiled=True)  27.4 us
    all_to_all x1, waiting for transfers between devices, per_device(): lax.all_to_all(arrange(flat_num, groups, members), ('grp', 'seq'), split_...  20.8 us
    all_gather x1, waiting for transfers between devices, per_device(): gathered = lax.all_gather(with_heads, 'grp', axis=0, tiled=True)  12.8 us
    unnamed x30, local copies, waits for them, and re-layouts  9.86 us
    all_to_all x1, waiting for transfers between devices, per_device(): lax.all_to_all(arrange(flat_max, groups, members), ('grp', 'seq'), split_...  8.77 us
    all_to_all x1, starting transfers between devices, per_device(): lax.all_to_all(arrange(flat_max, groups, members), ('grp', 'seq'), split_...  8.52 us
    reshape x3, local copies, waits for them, and re-layouts, arrange(): shaped.transpose(order)  7.56 us
    all_to_all x1, waiting for transfers between devices, per_device(): lax.all_to_all(arrange(flat_den, groups, members), ('grp', 'seq'), split_...  6.53 us
  transfers between devices with their start and end apart: 4, of which 4 were waited for; matrix products, arithmetic and copies ran while one was open for 17% of the time, Pallas kernels for 0%

commit v1 on v0

v1 whole, which is shorter than its diff:
```python
import functools
import math

import jax
import jax.numpy as jnp
from jax import lax
from jax.experimental import pallas as pl
from jax.experimental.pallas import tpu as pltpu
from jax.sharding import PartitionSpec as P

H = 64
KVH = 8
HEAD = 128
LOWEST = -(2.0**100)
SCALE = HEAD ** (-0.5) * math.log2(math.e)
NUM_ROWS = 32
ALL_ROWS = 40
HEADS = NUM_ROWS // 8
PARAMS = pltpu.CompilerParams(vmem_limit_bytes=32 << 20)

NT = (((1,), (1,)), ((), ()))
NN = (((1,), (0,)), ((), ()))


def dot(a, b, dims):
    return lax.dot_general(a, b, dims, preferred_element_type=jnp.float32)


def iota(shape, axis):
    return lax.broadcasted_iota(jnp.int32, shape, axis)


def as_bf16(x):
    return x.astype(jnp.bfloat16).astype(jnp.float32)


def columns(x):
    return [x[:, a * HEAD : (a + 1) * HEAD] for a in range(x.shape[1] // HEAD)]


def pack(tops, totals):
    lane = iota((8, HEAD), 1)
    piece = lax.rem(lane, 32) // 8
    packed = None
    for a in range(HEADS):
        high = as_bf16(totals[a])
        mixed = jnp.where(piece == 1, high, totals[a] - high)
        mixed = jnp.where(piece == 0, tops[a], mixed)
        packed = mixed if a == 0 else jnp.where(lane // 32 == a, mixed, packed)
    return packed.astype(jnp.bfloat16)


def unpack(tails):
    shape = (HEAD, HEADS * HEAD)
    start = iota(shape, 0) - 32 * (iota(shape, 1) // HEAD)
    first = (start == 0).astype(jnp.float32).astype(jnp.bfloat16)
    second = ((start == 8) | (start == 16)).astype(jnp.float32).astype(jnp.bfloat16)
    return dot(tails, first, NN), dot(tails, second, NN)


def combine(tops, totals, numerators):
    upper = functools.reduce(jnp.maximum, tops)
    factors = [jnp.exp2(top - upper) for top in tops]
    total = sum(x * f for x, f in zip(totals, factors))
    return upper, total, sum(x * f for x, f in zip(numerators, factors))


def spread_kernel(q_ref, out_ref):
    held = [q_ref[r].astype(jnp.float32) for r in range(q_ref.shape[0])]
    heads = range(q_ref.shape[2] // HEAD)
    block = [x[:, h * HEAD : (h + 1) * HEAD] for h in heads for x in held]
    block = jnp.concatenate(block, axis=0).astype(jnp.bfloat16)
    for d in range(out_ref.shape[0]):
        out_ref[d] = block


def spread(queries, copies):
    return pl.pallas_call(
        spread_kernel,
        out_shape=jax.ShapeDtypeStruct((copies, NUM_ROWS, HEAD), jnp.bfloat16),
        compiler_params=PARAMS,
        name="spread",
    )(queries)


def stage_kernel(*refs):
    sources, outs, sems = refs[:4], refs[4:8], refs[8]
    copies = []
    for n, (source, out) in enumerate(zip(sources, outs)):
        for k in range(KVH):
            at = pl.ds(k * HEAD, HEAD)
            part = source.at[:, at] if n < 2 else source.at[:, :, at]
            copies.append(pltpu.make_async_copy(part, out.at[k], sems.at[n, k]))
    for copy in copies:
        copy.start()
    for copy in copies:
        copy.wait()


def stage(*arrays):
    outs = [pltpu.VMEM((KVH,) + x.shape[:-1] + (HEAD,), x.dtype) for x in arrays]
    size = sum(2 * x.size * x.dtype.itemsize for x in arrays)
    return pl.pallas_call(
        stage_kernel,
        in_specs=[pl.BlockSpec(memory_space=pl.ANY)] * len(arrays),
        out_specs=[pl.BlockSpec(memory_space=pl.ANY)] * len(arrays),
        out_shape=outs,
        scratch_shapes=[pltpu.SemaphoreType.DMA((len(arrays), KVH))],
        compiler_params=PARAMS,
        cost_estimate=pl.CostEstimate(flops=0, bytes_accessed=size, transcendentals=0),
        name="stage",
    )(*[pltpu.with_memory_space_constraint(x, pltpu.HBM) for x in arrays])


def attend_kernel(info, *refs, heads, chunk):
    near_ref, far_ref, k_ref, v_ref, sk_ref, sv_ref, near_out, far_out = refs[:8]
    q_ref, own_top, own_acc = refs[8:]
    pieces, _, rows, _ = q_ref.shape
    near = near_out.shape[0]
    halves = rows // NUM_ROWS
    per_chunk = chunk // rows
    length = k_ref.shape[1]
    _, slots, span, _ = sk_ref.shape
    ones = jnp.ones((length, HEAD), jnp.bfloat16)

    @pl.when(pl.program_id(0) == 0)
    def _():
        own_top[...] = jnp.full(own_top.shape, LOWEST, jnp.float32)
        own_acc[...] = jnp.zeros(own_acc.shape, jnp.float32)

    q_ref[:near] = near_ref[...]
    q_ref[near:] = far_ref[...]

    def scored(i, c):
        q = q_ref[c * per_chunk : (c + 1) * per_chunk, i].reshape(chunk, HEAD)
        return dot(q, k_ref[i], NT)

    items = [(i, c) for i in range(heads) for c in range(pieces // per_chunk)]
    scores = scored(*items[0])

    row_id = lax.rem(iota((rows, HEAD), 0), 8) // 2
    row_ids = lax.rem(iota((rows, span), 0), 8) // 2
    position = iota((rows, span), 1)
    found = []
    for j in range(slots):
        group, row, live = info[j], info[slots + j], info[2 * slots + j]
        kept = (row_ids == row) & (position < live)
        for i in range(heads):
            own = dot(q_ref[group, i], sk_ref[i, j], NT) * SCALE
            own = jnp.where(kept, own, LOWEST)
            peak = jnp.max(own, axis=1, keepdims=True)
            peak = jnp.broadcast_to(as_bf16(peak), (rows, HEAD))
            shift = jnp.concatenate([peak] * (span // HEAD), axis=1)
            weights = jnp.exp2(own - shift).astype(jnp.bfloat16)
            values = jnp.concatenate([sv_ref[i, j], ones[:span]], axis=1)
            found.append((group, i, row_id == row, peak, dot(weights, values, NN)))
    for group, i, here, peak, summed in found:
        own_top[group, i] = jnp.where(here, peak, own_top[group, i])
        both = jnp.concatenate([here, here], axis=1)
        own_acc[group, i] = jnp.where(both, summed, own_acc[group, i])

    for number, (i, c) in enumerate(items):
        later = scored(*items[number + 1]) if number + 1 < len(items) else None
        at = slice(c * per_chunk, (c + 1) * per_chunk)
        before = own_top[at, i].reshape(chunk, HEAD)
        carried = own_acc[at, i].reshape(chunk, 2 * HEAD)
        peak = jnp.max(scores, axis=1, keepdims=True) * SCALE
        top = jnp.maximum(jnp.broadcast_to(as_bf16(peak), (chunk, HEAD)), before)
        shift = jnp.concatenate([top] * (length // HEAD), axis=1)
        weights = jnp.exp2(scores * SCALE - shift).astype(jnp.bfloat16)
        values = jnp.concatenate([v_ref[i], ones], axis=1)
        keep = jnp.exp2(before - top)
        summed = dot(weights, values, NN) + carried * jnp.concatenate([keep, keep], axis=1)
        results = []
        for b in range(chunk // NUM_ROWS):
            low = b * NUM_ROWS
            parts = [slice(low + 8 * a, low + 8 * a + 8) for a in range(HEADS)]
            tail = pack([top[p] for p in parts], [summed[p, HEAD:] for p in parts])
            results.append((summed[low : low + NUM_ROWS, :HEAD].astype(jnp.bfloat16), tail))
        for b, (block, tail) in enumerate(results):
            g = c * per_chunk + b // halves
            out_ref = (near_out if g < near else far_out).at[g % near, i * halves + b % halves]
            out_ref[:NUM_ROWS] = block
            out_ref[NUM_ROWS:] = tail
        scores = later


def attend(info, near, far, keys, values, suffix_keys, suffix_values, heads, chunk):
    layers, members = near.shape[:2]
    rows = members // KVH * NUM_ROWS
    near, far = (x.reshape(layers, KVH, rows, HEAD) for x in (near, far))
    length = keys.shape[1]
    _, slots, span, _ = suffix_keys.shape
    by_head = pl.BlockSpec((layers, heads, rows, HEAD), lambda k: (0, k, 0, 0))
    prompt = pl.BlockSpec((heads, length, HEAD), lambda k: (k, 0, 0))
    own = pl.BlockSpec((heads, slots, span, HEAD), lambda k: (k, 0, 0, 0))
    out_block = (layers, heads * rows // NUM_ROWS, ALL_ROWS, HEAD)
    out_spec = pl.BlockSpec(out_block, lambda k: (0, k, 0, 0))
    out = jax.ShapeDtypeStruct((layers, members, ALL_ROWS, HEAD), jnp.bfloat16)
    return pl.pallas_call(
        functools.partial(attend_kernel, heads=heads, chunk=chunk),
        grid=(KVH // heads,),
        in_specs=[pl.BlockSpec(memory_space=pltpu.SMEM)]
        + [by_head, by_head, prompt, prompt, own, own],
        out_specs=[out_spec, out_spec],
        out_shape=[out, out],
        scratch_shapes=[
            pltpu.VMEM((2 * layers, heads, rows, HEAD), jnp.bfloat16),
            pltpu.VMEM((2 * layers, heads, rows, HEAD), jnp.float32),
            pltpu.VMEM((2 * layers, heads, rows, 2 * HEAD), jnp.float32),
        ],
        compiler_params=PARAMS,
        name="attend",
    )(info, near, far, keys, values, suffix_keys, suffix_values)


def join_parts(parts):
    count = len(parts[0])
    opened = []
    for blocks in parts:
        tails = [x[NUM_ROWS:].astype(jnp.float32) for x in blocks]
        opened.append(unpack(jnp.concatenate(tails, axis=0).astype(jnp.bfloat16)))
    joined = []
    for b in range(count):
        tops, totals, numerators = [], [], []
        for blocks, (top, total) in zip(parts, opened):
            tops.append(columns(top[b * 8 : b * 8 + 8]))
            totals.append(columns(total[b * 8 : b * 8 + 8]))
            numerator = blocks[b][:NUM_ROWS].astype(jnp.float32)
            numerators.append([numerator[a * 8 : a * 8 + 8] for a in range(HEADS)])
        rows = [
            combine([x[a] for x in tops], [x[a] for x in totals], [x[a] for x in numerators])
            for a in range(HEADS)
        ]
        block = jnp.concatenate([x[2] for x in rows], axis=0).astype(jnp.bfloat16)
        joined.append((block, pack([x[0] for x in rows], [x[1] for x in rows])))
    return joined


def join_cores_kernel(a_ref, b_ref, out_ref):
    layers, members = a_ref.shape[:2]
    for y in range(layers):
        parts = [[ref[y, m] for m in range(members)] for ref in (a_ref, b_ref)]
        for m, (block, tail) in enumerate(join_parts(parts)):
            out_ref[y, m, :NUM_ROWS] = block
            out_ref[y, m, NUM_ROWS:] = tail


def join_cores(a, b):
    return pl.pallas_call(
        join_cores_kernel,
        out_shape=jax.ShapeDtypeStruct(a.shape, a.dtype),
        compiler_params=PARAMS,
        name="join_cores",
    )(a, b)


def new_kernel(q_ref, new_ref, score_ref, value_ref):
    rows, steps, _ = q_ref.shape
    member = lax.axis_index("z") * lax.axis_size("x") + lax.axis_index("x")
    kv_head = member * HEADS // (H // KVH)
    at_head = pl.ds(pl.multiple_of(kv_head * HEAD, HEAD), HEAD)

    def new_rows(u, which):
        found = [new_ref[r, u, which : which + 1, at_head].astype(jnp.float32) for r in range(rows)]
        return jnp.concatenate([jnp.broadcast_to(x, (steps, HEAD)) for x in found], axis=0)

    held = [q_ref[r].astype(jnp.float32) for r in range(rows)]
    step = lax.rem(iota((8, HEAD), 0), steps)
    for u in range(steps):
        keys = new_rows(u, 0)
        value_ref[u] = new_rows(u, 1)
        for a in range(HEADS):
            q = jnp.concatenate([x[:, a * HEAD : (a + 1) * HEAD] for x in held], axis=0)
            score = jnp.sum(q * keys, axis=1, keepdims=True) * SCALE
            score = jnp.broadcast_to(score, (8, HEAD))
            score_ref[u, a] = jnp.where(step >= u, score, LOWEST)


def new_tokens(queries, new_kv):
    steps = queries.shape[1]
    return pl.pallas_call(
        new_kernel,
        out_shape=[
            jax.ShapeDtypeStruct((steps, HEADS, 8, HEAD), jnp.float32),
            jax.ShapeDtypeStruct((steps, 8, HEAD), jnp.float32),
        ],
        compiler_params=PARAMS,
        name="new_tokens",
    )(queries, new_kv)


def merge_kernel(parts_ref, score_ref, value_ref, out_ref):
    rows, steps, _ = out_ref.shape
    blocks = [parts_ref[s] for s in range(parts_ref.shape[0])]
    tails = [x[NUM_ROWS:].astype(jnp.float32) for x in blocks]
    opened = unpack(jnp.concatenate(tails, axis=0).astype(jnp.bfloat16))
    opened = [columns(x) for x in opened]
    one = jnp.ones((8, HEAD), jnp.float32)
    results = []
    for a in range(HEADS):
        pieces = [slice(s * 8, s * 8 + 8) for s in range(len(blocks))]
        tops = [opened[0][a][p] for p in pieces]
        totals = [opened[1][a][p] for p in pieces]
        sums = [x[a * 8 : a * 8 + 8].astype(jnp.float32) for x in blocks]
        for u in range(steps):
            tops.append(score_ref[u, a])
            totals.append(one)
            sums.append(value_ref[u])
        _, total, summed = combine(tops, totals, sums)
        results.append(summed / total)
    for a, result in enumerate(results):
        for r in range(rows):
            out_ref[r, :, a * HEAD : (a + 1) * HEAD] = result[r * steps : (r + 1) * steps].astype(
                jnp.bfloat16
            )


def merge(parts, scores, values, shape):
    return pl.pallas_call(
        merge_kernel,
        out_shape=jax.ShapeDtypeStruct(shape, jnp.bfloat16),
        compiler_params=PARAMS,
        name="merge",
    )(parts, scores, values)


CHIPS = ("y", "z", "x")


def exchange(x, axes):
    return lax.all_to_all(x, axes, split_axis=0, concat_axis=0, tiled=True)


def per_device(
    queries,
    new_kv,
    prefix_keys,
    prefix_values,
    suffix_keys,
    suffix_values,
    suffix_lengths,
    row_slot,
):
    layers = lax.axis_size("y")
    cores = lax.axis_size("core")
    members = lax.axis_size("z") * lax.axis_size("x")
    layer = lax.axis_index("y")
    core = lax.axis_index("core")
    member_index = lax.axis_index("z") * lax.axis_size("x") + lax.axis_index("x")
    per_group = queries.shape[0]
    swap = [(i, (i + 1) % cores) for i in range(cores)]

    chips = layers * members
    block = (layers, members)

    copies = spread(queries, chips)
    copies, *cached = lax.optimization_barrier(
        (copies, prefix_keys, prefix_values, suffix_keys, suffix_values)
    )
    near = exchange(copies, CHIPS).reshape(block + (NUM_ROWS, HEAD))
    near, *cached = lax.optimization_barrier((near, *stage(*cached)))
    far = lax.ppermute(near, "core", swap)

    slot_ids = (layer * cores + core) * per_group + jnp.arange(per_group, dtype=jnp.int32)
    belongs = row_slot[None, :] == slot_ids[:, None]
    row_ids = jnp.arange(row_slot.shape[0], dtype=jnp.int32)
    row_of = jnp.sum(jnp.where(belongs, row_ids[None, :], 0), axis=1)
    row_group = row_of // per_group
    place = row_group // cores + jnp.where(row_group % cores == core, 0, layers)
    span = suffix_keys.shape[1]
    live = jnp.clip(suffix_lengths - member_index * span, 0, span)
    info = jnp.concatenate([place, row_of % per_group, live])

    near_part, far_part = attend(info, near, far, *cached, 2, 128)
    joined = join_cores(near_part, lax.ppermute(far_part, "core", swap))
    joined, queries, new_kv = lax.optimization_barrier((joined, queries, new_kv))
    received = exchange(joined.reshape(chips, ALL_ROWS, HEAD), CHIPS)
    scores, values = new_tokens(queries, new_kv)
    return merge(received, scores, values, queries.shape)


def solution(mesh):
    fine = jax.sharding.Mesh(mesh.devices.reshape(4, 2, 4, 4), ("y", "core", "z", "x"))
    grp, seq = ("y", "core"), ("z", "x")
    placed = (
        P(grp, None, seq),
        P(grp, None, None, None),
        P(grp + seq, None),
        P(grp + seq, None),
        P(grp, seq, None),
        P(grp, seq, None),
        P(grp),
        P(),
    )
    return jax.shard_map(
        per_device, mesh=fine, in_specs=placed, out_specs=P(grp, None, seq), check_vma=False
    )
```

time: 178 us -> 68.3 us (0.38)
  local copies, waits for them, and re-layouts: 40.4 us -> 9.51 us
  blocking collectives: 27.4 us -> 0 us
  waiting for transfers between devices: 49 us -> 24 us
  matrix products: 20.4 us -> 0 us
  Pallas kernels: 0 us -> 17.1 us
  between operations: 13.7 us -> 0.12 us
  other arithmetic: 8.55 us -> 0.29 us
    all_gather x1 -> x0, blocking collectives: 27.4 us -> none  [per_device(): with_heads = lax.all_gather(queries, 'seq', axis=2, tiled=True)]
    dot_general x12 -> x0, matrix products: 20.4 us -> none  [the longest x2 6.26 us: prefix_step(): jnp.einsum('rtkgj,jkd->rtkgd', weights, value_block, preferred_element_ty...]
    reshape x9 -> x0, local copies, waits for them, and re-layouts: 19.5 us -> none  [the longest x3 7.56 us: arrange(): shaped.transpose(order)]
    pallas_call x0 -> x6, Pallas kernels: none -> 17.1 us  [the longest x1 9.07 us: attend(): pl.pallas_call(functools.partial(attend_kernel, heads=heads, chunk=chunk)...]
    all_to_all x3 -> x2, waiting for transfers between devices: 36.1 us -> 20.3 us  [exchange(): return lax.all_to_all(x, axes, split_axis=0, concat_axis=0, tiled=True)]
    all_gather x1 -> x0, waiting for transfers between devices: 12.8 us -> none  [per_device(): gathered = lax.all_gather(with_heads, 'grp', axis=0, tiled=True)]
    reduce_sum x6 -> x1, other arithmetic: 7.23 us -> 0.18 us  [per_device(): row_of = jnp.sum(jnp.where(belongs, row_ids[None, :], 0), axis=1)]
    dynamic_slice x6 -> x0, local copies, waits for them, and re-layouts: 5.6 us -> none  [the longest x4 4.51 us: prefix_step(): lax.dynamic_slice_in_dim(prefix_values, number * prefix_block, prefix_blo...]
  transfers between devices with their start and end apart: 4 -> 4, of which waited for: 4 -> 4; matrix products, arithmetic and copies ran while one was open for 17% -> 0% of each run, Pallas kernels for 0% -> 6%
where the time goes in v1:
time: 68.3 us; the launch traced here: 67.9 us
  waiting for transfers between devices  24 us (35%)
  Pallas kernels  17.1 us (25%)
  starting transfers between devices  16.9 us (25%)
  local copies, waits for them, and re-layouts  9.51 us (14%)
    all_to_all x2, waiting for transfers between devices, exchange(): return lax.all_to_all(x, axes, split_axis=0, concat_axis=0, tiled=True)  20.3 us
    all_to_all x2, starting transfers between devices, exchange(): return lax.all_to_all(x, axes, split_axis=0, concat_axis=0, tiled=True)  16.6 us
    unnamed x22, local copies, waits for them, and re-layouts  9.51 us
    pallas_call x1, Pallas kernels, attend(): pl.pallas_call(functools.partial(attend_kernel, heads=heads, chunk=chunk)...  9.07 us
    pallas_call x1, Pallas kernels, stage(): pl.pallas_call(stage_kernel, in_specs=[pl.BlockSpec(memory_space=pl.ANY)]...  3.91 us
    ppermute x1, waiting for transfers between devices, per_device(): joined = join_cores(near_part, lax.ppermute(far_part, 'core', swap))  1.95 us
    pallas_call x1, Pallas kernels, join_cores(): pl.pallas_call(join_cores_kernel, out_shape=jax.ShapeDtypeStruct(a.shape,...  1.95 us
    ppermute x1, waiting for transfers between devices, per_device(): far = lax.ppermute(near, 'core', swap)  1.79 us
  transfers between devices with their start and end apart: 4, of which 4 were waited for; matrix products, arithmetic and copies ran while one was open for 0% of the time, Pallas kernels for 6%

profile of v1, /device:TPU:0, one launch (start us, length us, event | category | flops | bytes accessed | tf_op | source)
XLA Modules:
  0.0 67.9 jit_solution(13355524927417889534)
XLA Ops:
  0.0 0.0 copy-start.6
  0.0 0.7 %copy-done.6 = bf16[4,2,512]{2,1,0:T(2,128)(2,1)S(1)} copy-done((bf16[4,2,512]{2,1,0:T(2,128)(2,1)S(1)}, bf16[4,2,512]{2,1,0:T(2,128)(2,1)}, u32[]{:S(2)}) %copy-start.6) | copy-done | bytes 8216
  0.7 0.8 %spread.1 = bf16[64,32,128]{2,1,0:T(8,128)(2,1)} custom-call(bf16[4,2,512]{2,1,0:T(2,128)(2,1)S(1)} %copy-done.6), custom_call_target="tpu_custom_call" | custom-call | tf_op jit(solution)/shard_map/spread/pallas_call | solution.py:78
  1.5 11.5 %all-to-all-start = ((bf16[64,32,128]{2,1,0:T(8,128)(2,1)}), bf16[64,32,128]{2,1,0:T(8,128)(2,1)S(1)}, u32[]{:S(2)}, u32[]{:S(2)}) async-start(bf16[64,32,128]{2,1,0:T(8,128)(2,1)} %spread.1), calls=%async_computation | async-start | bytes 1048576 | tf_op jit(solution)/shard_map/all_to_all | solution.py:332
  13.1 0.0 copy-start.9
  13.1 0.0 copy-start.10
  13.1 3.9 %stage.1 = (bf16[8,1024,128]{2,1,0:T(8,128)(2,1)S(1)}, bf16[8,1024,128]{2,1,0:T(8,128)(2,1)S(1)}, bf16[8,4,256,128]{3,2,1,0:T(8,128)(2,1)S(1)}, bf16[8,4,256,128]{3,2,1,0:T(8,128)(2,1)S(1)}) custom-call(bf16[1024,1024]{1,0:T(8,128)(2,1)} %refs_0_, bf16[1024,1024]{1,0:T(8,128)(2,1)} %refs_1_, bf16[4,256,1024]{2,1,0:T(8,128)(2,1)} %refs_2_, ...), custom_call_target="tpu_custom_call" | custom-call | bytes 16777216 | tf_op jit(solution)/shard_map/stage/pallas_call | solution.py:103
  17.0 0.0 copy-start
  17.0 1.3 %copy-done = bf16[8,1024,128]{2,1,0:T(8,128)(2,1)} copy-done((bf16[8,1024,128]{2,1,0:T(8,128)(2,1)}, bf16[8,1024,128]{2,1,0:T(8,128)(2,1)S(1)}, u32[]{:S(2)}) %copy-start) | copy-done | bytes 2097176
  18.3 0.0 copy-start.2
  18.3 1.3 %copy-done.2 = bf16[8,4,256,128]{3,2,1,0:T(8,128)(2,1)} copy-done((bf16[8,4,256,128]{3,2,1,0:T(8,128)(2,1)}, bf16[8,4,256,128]{3,2,1,0:T(8,128)(2,1)S(1)}, u32[]{:S(2)}) %copy-start.2) | copy-done | bytes 2097176
  19.7 0.0 copy-start.4
  19.7 1.4 %copy-done.4 = bf16[8,4,256,128]{3,2,1,0:T(8,128)(2,1)} copy-done((bf16[8,4,256,128]{3,2,1,0:T(8,128)(2,1)}, bf16[8,4,256,128]{3,2,1,0:T(8,128)(2,1)S(1)}, u32[]{:S(2)}) %copy-start.4) | copy-done | bytes 2097176
  21.0 0.0 copy-done.9
  21.0 0.2 select_reduce_fusion
  21.2 5.3 %all-to-all-done = bf16[64,32,128]{2,1,0:T(8,128)(2,1)S(1)} async-done(((bf16[64,32,128]{2,1,0:T(8,128)(2,1)}), bf16[64,32,128]{2,1,0:T(8,128)(2,1)S(1)}, u32[]{:S(2)}, u32[]{:S(2)}) %all-to-all-start) | async-done | bytes 524320 | tf_op jit(solution)/shard_map/all_to_all | solution.py:332
  26.5 0.0 collective-permute-start
  26.5 0.0 copy-done.10
  26.5 0.1 pad_add_fusion.info
  26.6 1.8 %collective-permute-done = bf16[4,16,32,128]{3,2,1,0:T(8,128)(2,1)S(1)} collective-permute-done((bf16[4,16,32,128]{3,2,1,0:T(8,128)(2,1)S(1)}, bf16[4,16,32,128]{3,2,1,0:T(8,128)(2,1)S(1)}, u32[]{:S(2)}, u32[]{:S(2)}) %collective-permute-start) | collective-permute-done | bytes 524320 | tf_op jit(solution)/shard_map/ppermute | solution.py:363
  28.4 0.0 copy-start.1
  28.4 1.6 %copy-done.1 = bf16[8,1024,128]{2,1,0:T(8,128)(2,1)S(1)} copy-done((bf16[8,1024,128]{2,1,0:T(8,128)(2,1)S(1)}, bf16[8,1024,128]{2,1,0:T(8,128)(2,1)}, u32[]{:S(2)}) %copy-start.1) | copy-done | bytes 2097176
  30.0 0.0 copy-start.3
  30.0 1.6 %copy-done.3 = bf16[8,4,256,128]{3,2,1,0:T(8,128)(2,1)S(1)} copy-done((bf16[8,4,256,128]{3,2,1,0:T(8,128)(2,1)S(1)}, bf16[8,4,256,128]{3,2,1,0:T(8,128)(2,1)}, u32[]{:S(2)}) %copy-start.3) | copy-done | bytes 2097176
  31.6 0.0 copy-start.5
  31.6 1.6 %copy-done.5 = bf16[8,4,256,128]{3,2,1,0:T(8,128)(2,1)S(1)} copy-done((bf16[8,4,256,128]{3,2,1,0:T(8,128)(2,1)S(1)}, bf16[8,4,256,128]{3,2,1,0:T(8,128)(2,1)}, u32[]{:S(2)}) %copy-start.5) | copy-done | bytes 2097176
  33.2 9.1 %attend.1 = (bf16[4,16,40,128]{3,2,1,0:T(8,128)(2,1)S(1)}, bf16[4,16,40,128]{3,2,1,0:T(8,128)(2,1)S(1)}) custom-call(s32[12]{0:T(128)S(1)} %pad_add_fusion.info, bf16[4,8,64,128]{3,2,1,0:T(8,128)(2,1)S(1)} %bitcast.5, bf16[4,8,64,128]{3,2,1,0:T(8,128)(2,1)S(1)} %bitcast.6, bf16[8,1024,128]{2,1,0:T(8,128)(2,1)S(1)} %get-tuple-element.36.refs_2_, ...), custom_call_target="tpu_custom_call" | custom-call | tf_op jit(solution)/shard_map/attend/pallas_call | solution.py:200
  42.3 0.0 copy-start.7
  42.3 0.0 copy-start.8
  42.3 0.2 collective-permute-start.1
  42.5 1.9 %collective-permute-done.1.b_ref = bf16[4,16,40,128]{3,2,1,0:T(8,128)(2,1)S(1)} collective-permute-done((bf16[4,16,40,128]{3,2,1,0:T(8,128)(2,1)S(1)}, bf16[4,16,40,128]{3,2,1,0:T(8,128)(2,1)S(1)}, u32[]{:S(2)}, u32[]{:S(2)}) %collective-permute-start.1) | collective-permute-done | bytes 655392 | tf_op jit(solution)/shard_map/ppermute | solution.py:376
  44.5 1.9 %join_cores.1 = bf16[4,16,40,128]{3,2,1,0:T(8,128)(2,1)} custom-call(bf16[4,16,40,128]{3,2,1,0:T(8,128)(2,1)S(1)} %get-tuple-element.40.a_ref, bf16[4,16,40,128]{3,2,1,0:T(8,128)(2,1)S(1)} %collective-permute-done.1.b_ref), custom_call_target="tpu_custom_call" | custom-call | tf_op jit(solution)/shard_map/join_cores/pallas_call | solution.py:250
  46.4 5.1 %all-to-all-start.1 = ((bf16[64,40,128]{2,1,0:T(8,128)(2,1)}), bf16[64,40,128]{2,1,0:T(8,128)(2,1)S(1)}, u32[]{:S(2)}, u32[]{:S(2)}) async-start(bf16[64,40,128]{2,1,0:T(8,128)(2,1)} %bitcast.3), calls=%async_computation.1 | async-start | bytes 1310720 | tf_op jit(solution)/shard_map/all_to_all | solution.py:332
  51.6 0.0 copy-done.7
  51.6 0.0 copy-done.8
  51.6 0.1 new_tokens.1
  51.7 15.0 %all-to-all-done.1.parts_ref = bf16[64,40,128]{2,1,0:T(8,128)(2,1)S(1)} async-done(((bf16[64,40,128]{2,1,0:T(8,128)(2,1)}), bf16[64,40,128]{2,1,0:T(8,128)(2,1)S(1)}, u32[]{:S(2)}, u32[]{:S(2)}) %all-to-all-start.1) | async-done | bytes 655392 | tf_op jit(solution)/shard_map/all_to_all | solution.py:332
  66.7 1.2 %merge.1 = bf16[4,2,512]{2,1,0:T(2,128)(2,1)} custom-call(bf16[64,40,128]{2,1,0:T(8,128)(2,1)S(1)} %all-to-all-done.1.parts_ref, f32[2,4,8,128]{3,2,1,0:T(8,128)S(1)} %get-tuple-element.45.score_ref, f32[2,8,128]{2,1,0:T(8,128)S(1)} %get-tuple-element.46.value_ref), custom_call_target="tpu_custom_call" | custom-call | tf_op jit(solution)/shard_map/merge/pallas_call | solution.py:320
  (3 shorter events, 0.0 us)
Async XLA Ops:
  0.0 0.7 %copy-start.6 = (bf16[4,2,512]{2,1,0:T(2,128)(2,1)S(1)}, bf16[4,2,512]{2,1,0:T(2,128)(2,1)}, u32[]{:S(2)}) copy-start(bf16[4,2,512]{2,1,0:T(2,128)(2,1)} %q_ref.2) | copy-start | bytes 24580
  1.5 25.0 %all-to-all-start = ((bf16[64,32,128]{2,1,0:T(8,128)(2,1)}), bf16[64,32,128]{2,1,0:T(8,128)(2,1)S(1)}, u32[]{:S(2)}, u32[]{:S(2)}) async-start(bf16[64,32,128]{2,1,0:T(8,128)(2,1)} %spread.1), calls=%async_computation | async-start | bytes 1048576 | tf_op jit(solution)/shard_map/all_to_all | solution.py:332
  13.1 8.0 %copy-start.9 = (s32[32]{0:T(128)S(1)}, s32[32]{0:T(128)}, u32[]{:S(2)}) copy-start(s32[32]{0:T(128)} %param.15) | copy-start | bytes 388
  13.1 13.4 %copy-start.10 = (s32[4]{0:T(128)S(1)}, s32[4]{0:T(128)}, u32[]{:S(2)}) copy-start(s32[4]{0:T(128)} %param.14) | copy-start | bytes 52
  17.0 1.3 %copy-start = (bf16[8,1024,128]{2,1,0:T(8,128)(2,1)}, bf16[8,1024,128]{2,1,0:T(8,128)(2,1)S(1)}, u32[]{:S(2)}) copy-start(bf16[8,1024,128]{2,1,0:T(8,128)(2,1)S(1)} %get-tuple-element.37.refs_3_) | copy-start | bytes 6291460
  18.3 1.3 %copy-start.2 = (bf16[8,4,256,128]{3,2,1,0:T(8,128)(2,1)}, bf16[8,4,256,128]{3,2,1,0:T(8,128)(2,1)S(1)}, u32[]{:S(2)}) copy-start(bf16[8,4,256,128]{3,2,1,0:T(8,128)(2,1)S(1)} %get-tuple-element.38.refs_4_) | copy-start | bytes 6291460
  19.7 1.4 %copy-start.4 = (bf16[8,4,256,128]{3,2,1,0:T(8,128)(2,1)}, bf16[8,4,256,128]{3,2,1,0:T(8,128)(2,1)S(1)}, u32[]{:S(2)}) copy-start(bf16[8,4,256,128]{3,2,1,0:T(8,128)(2,1)S(1)} %get-tuple-element.39.refs_5_) | copy-start | bytes 6291460
  26.5 1.9 %collective-permute-start = (bf16[4,16,32,128]{3,2,1,0:T(8,128)(2,1)S(1)}, bf16[4,16,32,128]{3,2,1,0:T(8,128)(2,1)S(1)}, u32[]{:S(2)}, u32[]{:S(2)}) collective-permute-start(bf16[4,16,32,128]{3,2,1,0:T(8,128)(2,1)S(1)} %bitcast.4), channel_id=1, source_target_pairs={{0,16},{16,0},{1,17},{17,1},{2,18},{18,2},{3,19},{19,3},{4,20},{20... | collective-permute-start | bytes 1572872 | tf_op jit(solution)/shard_map/ppermute | solution.py:363
  28.4 1.6 %copy-start.1 = (bf16[8,1024,128]{2,1,0:T(8,128)(2,1)S(1)}, bf16[8,1024,128]{2,1,0:T(8,128)(2,1)}, u32[]{:S(2)}) copy-start(bf16[8,1024,128]{2,1,0:T(8,128)(2,1)} %copy-done) | copy-start | bytes 6291460
  30.0 1.6 %copy-start.3 = (bf16[8,4,256,128]{3,2,1,0:T(8,128)(2,1)S(1)}, bf16[8,4,256,128]{3,2,1,0:T(8,128)(2,1)}, u32[]{:S(2)}) copy-start(bf16[8,4,256,128]{3,2,1,0:T(8,128)(2,1)} %copy-done.2) | copy-start | bytes 6291460
  31.6 1.6 %copy-start.5 = (bf16[8,4,256,128]{3,2,1,0:T(8,128)(2,1)S(1)}, bf16[8,4,256,128]{3,2,1,0:T(8,128)(2,1)}, u32[]{:S(2)}) copy-start(bf16[8,4,256,128]{3,2,1,0:T(8,128)(2,1)} %copy-done.4) | copy-start | bytes 6291460
  42.3 9.3 %copy-start.7 = (bf16[4,2,512]{2,1,0:T(2,128)(2,1)S(1)}, bf16[4,2,512]{2,1,0:T(2,128)(2,1)}, u32[]{:S(2)}) copy-start(bf16[4,2,512]{2,1,0:T(2,128)(2,1)} %q_ref.2) | copy-start | bytes 24580
  42.3 9.3 %copy-start.8 = (bf16[4,2,2,1024]{3,2,1,0:T(2,128)(2,1)S(1)}, bf16[4,2,2,1024]{3,2,1,0:T(2,128)(2,1)}, u32[]{:S(2)}) copy-start(bf16[4,2,2,1024]{3,2,1,0:T(2,128)(2,1)} %new_ref) | copy-start | bytes 98308
  42.3 2.2 %collective-permute-start.1 = (bf16[4,16,40,128]{3,2,1,0:T(8,128)(2,1)S(1)}, bf16[4,16,40,128]{3,2,1,0:T(8,128)(2,1)S(1)}, u32[]{:S(2)}, u32[]{:S(2)}) collective-permute-start(bf16[4,16,40,128]{3,2,1,0:T(8,128)(2,1)S(1)} %get-tuple-element.41), channel_id=1, source_target_pairs={{0,16},{16,0},{1,17},{17,1},{2,18},{18,2},{3,19},{19,3},{4,20},{20... | collective-permute-start | bytes 1966088 | tf_op jit(solution)/shard_map/ppermute | solution.py:376
  46.4 20.3 %all-to-all-start.1 = ((bf16[64,40,128]{2,1,0:T(8,128)(2,1)}), bf16[64,40,128]{2,1,0:T(8,128)(2,1)S(1)}, u32[]{:S(2)}, u32[]{:S(2)}) async-start(bf16[64,40,128]{2,1,0:T(8,128)(2,1)} %bitcast.3), calls=%async_computation.1 | async-start | bytes 1310720 | tf_op jit(solution)/shard_map/all_to_all | solution.py:332

commit v2 on v1

v2 whole, which is shorter than its diff:
```python
import functools
import math

import jax
import jax.numpy as jnp
from jax import lax
from jax.experimental import pallas as pl
from jax.experimental.pallas import tpu as pltpu
from jax.sharding import PartitionSpec as P

H = 64
KVH = 8
HEAD = 128
LOWEST = -(2.0**100)
SCALE = HEAD ** (-0.5) * math.log2(math.e)
TAIL = 8
SHARES = 1
PARAMS = pltpu.CompilerParams(vmem_limit_bytes=32 << 20)

NT = (((1,), (1,)), ((), ()))
NN = (((1,), (0,)), ((), ()))


def dot(a, b, dims):
    return lax.dot_general(a, b, dims, preferred_element_type=jnp.float32)


def iota(shape, axis):
    return lax.broadcasted_iota(jnp.int32, shape, axis)


def as_bf16(x):
    return x.astype(jnp.bfloat16).astype(jnp.float32)


def columns(x):
    return [x[:, a * HEAD : (a + 1) * HEAD] for a in range(x.shape[1] // HEAD)]


def pack(tops, totals):
    lane = iota((TAIL, HEAD), 1)
    piece = lax.rem(lane, 32) // 8
    packed = None
    for a, (top, total) in enumerate(zip(tops, totals)):
        high = as_bf16(total)
        mixed = jnp.where(piece == 1, high, total - high)
        mixed = jnp.where(piece == 0, top, mixed)
        packed = mixed if a == 0 else jnp.where(lane // 32 == a, mixed, packed)
    return packed.astype(jnp.bfloat16)


def unpack(tails, tiles):
    shape = (HEAD, tiles * HEAD)
    start = iota(shape, 0) - 32 * (iota(shape, 1) // HEAD)
    first = (start == 0).astype(jnp.float32).astype(jnp.bfloat16)
    second = ((start == 8) | (start == 16)).astype(jnp.float32).astype(jnp.bfloat16)
    return dot(tails, first, NN), dot(tails, second, NN)


def combine(tops, totals, numerators):
    upper = functools.reduce(jnp.maximum, tops)
    factors = [jnp.exp2(top - upper) for top in tops]
    total = sum(x * f for x, f in zip(totals, factors))
    return upper, total, sum(x * f for x, f in zip(numerators, factors))


def query_rows(q_ref, share):
    count = q_ref.shape[0] // SHARES
    held = [q_ref[share * count + r].astype(jnp.float32) for r in range(count)]
    heads = range(q_ref.shape[2] // HEAD)
    return jnp.concatenate([x[:, h * HEAD : (h + 1) * HEAD] for h in heads for x in held], axis=0)


def spread_kernel(q_ref, *out_refs):
    for share, out_ref in enumerate(out_refs):
        block = query_rows(q_ref, share).astype(jnp.bfloat16)
        for d in range(out_ref.shape[0]):
            out_ref[d] = block


def spread(queries, copies):
    rows = queries.size // HEAD // SHARES
    out = jax.ShapeDtypeStruct((copies, rows, HEAD), jnp.bfloat16)
    return pl.pallas_call(
        spread_kernel,
        out_shape=[out] * SHARES,
        compiler_params=PARAMS,
        name="spread",
    )(queries)


def locate_kernel(slot_ref, length_ref, info, *, span):
    slots = length_ref.shape[0]
    cores, layers = lax.axis_size("core"), lax.axis_size("y")
    core = lax.axis_index("core")
    first = (lax.axis_index("y") * cores + core) * slots
    start = (lax.axis_index("z") * lax.axis_size("x") + lax.axis_index("x")) * span
    for j in range(slots):
        row = jnp.int32(0)
        for r in range(slot_ref.shape[0]):
            row = jnp.where(slot_ref[r] == first + j, jnp.int32(r), row)
        group = lax.div(row, slots)
        far = jnp.where(lax.rem(group, cores) == core, 0, layers)
        info[j] = lax.div(group, cores) + far
        info[slots + j] = lax.rem(row, slots)
        info[2 * slots + j] = jnp.clip(length_ref[j] - start, 0, span)


def locate(row_slot, lengths, span):
    smem = pl.BlockSpec(memory_space=pltpu.SMEM)
    return pl.pallas_call(
        functools.partial(locate_kernel, span=span),
        in_specs=[smem, smem],
        out_specs=smem,
        out_shape=jax.ShapeDtypeStruct((3 * lengths.shape[0],), jnp.int32),
        compiler_params=PARAMS,
        name="locate",
    )(row_slot, lengths)


def attend_kernel(info, *refs, heads, chunk, share, steps):
    near_ref, far_ref, k_ref, v_ref, sk_ref, sv_ref, near_out, far_out = refs[:8]
    q_ref, own_top, own_acc = refs[8:]
    pieces, _, rows, _ = q_ref.shape
    near = near_out.shape[0]
    numerators = near_out.shape[2] - TAIL
    halves = rows // numerators
    per_chunk = chunk // rows
    length = k_ref.shape[0]
    slots, span, _ = sk_ref.shape
    count = slots // SHARES
    stride = count * steps
    ones = jnp.ones((length, HEAD), jnp.bfloat16)

    @pl.when(pl.program_id(0) == 0)
    def _():
        own_top[...] = jnp.full(own_top.shape, LOWEST, jnp.float32)
        own_acc[...] = jnp.zeros(own_acc.shape, jnp.float32)

    q_ref[:near] = near_ref[...]
    q_ref[near:] = far_ref[...]

    def cut(i):
        return slice(i * HEAD, (i + 1) * HEAD)

    def scored(i, c):
        q = q_ref[c * per_chunk : (c + 1) * per_chunk, i].reshape(chunk, HEAD)
        return dot(q, k_ref[:, cut(i)], NT)

    items = [(i, c) for i in range(heads) for c in range(pieces // per_chunk)]
    scores = scored(*items[0])

    row_id = lax.rem(iota((rows, HEAD), 0), stride) // steps + share * count
    row_ids = lax.rem(iota((rows, span), 0), stride) // steps + share * count
    position = iota((rows, span), 1)
    found = []
    for j in range(slots):
        group, row, live = info[j], info[slots + j], info[2 * slots + j]
        kept = (row_ids == row) & (position < live)
        for i in range(heads):
            own = dot(q_ref[group, i], sk_ref[j, :, cut(i)], NT) * SCALE
            own = jnp.where(kept, own, LOWEST)
            peak = jnp.max(own, axis=1, keepdims=True)
            peak = jnp.broadcast_to(as_bf16(peak), (rows, HEAD))
            shift = jnp.concatenate([peak] * (span // HEAD), axis=1)
            weights = jnp.exp2(own - shift).astype(jnp.bfloat16)
            values = jnp.concatenate([sv_ref[j, :, cut(i)], ones[:span]], axis=1)
            found.append((group, i, row_id == row, peak, dot(weights, values, NN)))
    for group, i, here, peak, summed in found:
        own_top[group, i] = jnp.where(here, peak, own_top[group, i])
        both = jnp.concatenate([here, here], axis=1)
        own_acc[group, i] = jnp.where(both, summed, own_acc[group, i])

    for number, (i, c) in enumerate(items):
        later = scored(*items[number + 1]) if number + 1 < len(items) else None
        at = slice(c * per_chunk, (c + 1) * per_chunk)
        before = own_top[at, i].reshape(chunk, HEAD)
        carried = own_acc[at, i].reshape(chunk, 2 * HEAD)
        peak = jnp.max(scores, axis=1, keepdims=True) * SCALE
        top = jnp.maximum(jnp.broadcast_to(as_bf16(peak), (chunk, HEAD)), before)
        shift = jnp.concatenate([top] * (length // HEAD), axis=1)
        weights = jnp.exp2(scores * SCALE - shift).astype(jnp.bfloat16)
        values = jnp.concatenate([v_ref[:, cut(i)], ones], axis=1)
        keep = jnp.exp2(before - top)
        summed = dot(weights, values, NN) + carried * jnp.concatenate([keep, keep], axis=1)
        results = []
        for b in range(chunk // numerators):
            low = b * numerators
            parts = [slice(low + 8 * a, low + 8 * a + 8) for a in range(numerators // 8)]
            tail = pack([top[p] for p in parts], [summed[p, HEAD:] for p in parts])
            results.append((summed[low : low + numerators, :HEAD].astype(jnp.bfloat16), tail))
        for b, (block, tail) in enumerate(results):
            g = c * per_chunk + b // halves
            out_ref = (near_out if g < near else far_out).at[g % near, i * halves + b % halves]
            out_ref[:numerators] = block
            out_ref[numerators:] = tail
        scores = later


def attend(info, near, far, keys, values, suffix_keys, suffix_values, share, heads, chunk):
    layers, members, numerators, _ = near.shape
    rows = members // KVH * numerators
    near, far = (x.reshape(layers, KVH, rows, HEAD) for x in (near, far))
    length = keys.shape[0]
    slots, span, _ = suffix_keys.shape
    steps = numerators * members * SHARES // (H * slots)
    in_hbm = [
        pltpu.with_memory_space_constraint(x, pltpu.HBM)
        for x in (keys, values, suffix_keys, suffix_values)
    ]
    wide = heads * HEAD
    by_head = pl.BlockSpec((layers, heads, rows, HEAD), lambda k: (0, k, 0, 0))
    prompt = pl.BlockSpec((length, wide), lambda k: (0, k))
    own = pl.BlockSpec((slots, span, wide), lambda k: (0, 0, k))
    out_block = (layers, heads * members // KVH, numerators + TAIL, HEAD)
    out_spec = pl.BlockSpec(out_block, lambda k: (0, k, 0, 0))
    out = jax.ShapeDtypeStruct((layers, members, numerators + TAIL, HEAD), jnp.bfloat16)
    return pl.pallas_call(
        functools.partial(attend_kernel, heads=heads, chunk=chunk, share=share, steps=steps),
        grid=(KVH // heads,),
        in_specs=[pl.BlockSpec(memory_space=pltpu.SMEM), by_head, by_head, prompt, prompt, own, own],
        out_specs=[out_spec, out_spec],
        out_shape=[out, out],
        scratch_shapes=[
            pltpu.VMEM((2 * layers, heads, rows, HEAD), jnp.bfloat16),
            pltpu.VMEM((2 * layers, heads, rows, HEAD), jnp.float32),
            pltpu.VMEM((2 * layers, heads, rows, 2 * HEAD), jnp.float32),
        ],
        compiler_params=PARAMS,
        name="attend",
    )(info, near, far, *in_hbm)


def join_parts(parts):
    numerators = parts[0][0].shape[0] - TAIL
    tiles = numerators // 8
    opened = []
    for blocks in parts:
        tails = [x[numerators:].astype(jnp.float32) for x in blocks]
        opened.append(unpack(jnp.concatenate(tails, axis=0).astype(jnp.bfloat16), tiles))
    joined = []
    for b in range(len(parts[0])):
        tops, totals, sums = [], [], []
        for blocks, (top, total) in zip(parts, opened):
            tops.append(columns(top[b * 8 : b * 8 + 8]))
            totals.append(columns(total[b * 8 : b * 8 + 8]))
            found = blocks[b][:numerators].astype(jnp.float32)
            sums.append([found[a * 8 : a * 8 + 8] for a in range(tiles)])
        rows = [
            combine([x[a] for x in tops], [x[a] for x in totals], [x[a] for x in sums])
            for a in range(tiles)
        ]
        block = jnp.concatenate([x[2] for x in rows], axis=0).astype(jnp.bfloat16)
        joined.append((block, pack([x[0] for x in rows], [x[1] for x in rows])))
    return joined


def join_cores_kernel(a_ref, b_ref, out_ref):
    layers, members, rows, _ = a_ref.shape
    for y in range(layers):
        parts = [[ref[y, m] for m in range(members)] for ref in (a_ref, b_ref)]
        for m, (block, tail) in enumerate(join_parts(parts)):
            out_ref[y, m, : rows - TAIL] = block
            out_ref[y, m, rows - TAIL :] = tail


def join_cores(a, b):
    return pl.pallas_call(
        join_cores_kernel,
        out_shape=jax.ShapeDtypeStruct(a.shape, a.dtype),
        compiler_params=PARAMS,
        name="join_cores",
    )(a, b)


def new_kernel(q_ref, new_ref, score_ref, value_ref):
    rows, steps, _ = q_ref.shape
    shares, _, tiles = score_ref.shape[:3]
    count = rows // shares
    heads = q_ref.shape[2] // HEAD
    member = lax.axis_index("z") * lax.axis_size("x") + lax.axis_index("x")
    kv_head = member * heads // (H // KVH)
    at_head = pl.ds(pl.multiple_of(kv_head * HEAD, HEAD), HEAD)
    step = lax.rem(iota((8, HEAD), 0), steps)

    def new_rows(share, u, which):
        found = [
            new_ref[share * count + r, u, which : which + 1, at_head].astype(jnp.float32)
            for r in range(count)
        ]
        found = [jnp.broadcast_to(x, (steps, HEAD)) for x in found]
        return jnp.concatenate(found * (8 // (count * steps)), axis=0)

    for share in range(shares):
        queries = query_rows(q_ref, share)
        for u in range(steps):
            keys = new_rows(share, u, 0)
            value_ref[share, u] = new_rows(share, u, 1)
            for a in range(tiles):
                score = jnp.sum(queries[a * 8 : a * 8 + 8] * keys, axis=1, keepdims=True) * SCALE
                score = jnp.broadcast_to(score, (8, HEAD))
                score_ref[share, u, a] = jnp.where(step >= u, score, LOWEST)


def new_tokens(queries, new_kv):
    steps = queries.shape[1]
    tiles = queries.size // HEAD // SHARES // 8
    return pl.pallas_call(
        new_kernel,
        out_shape=[
            jax.ShapeDtypeStruct((SHARES, steps, tiles, 8, HEAD), jnp.float32),
            jax.ShapeDtypeStruct((SHARES, steps, 8, HEAD), jnp.float32),
        ],
        compiler_params=PARAMS,
        name="new_tokens",
    )(queries, new_kv)


def merge_kernel(*refs):
    parts, (score_ref, value_ref, out_ref) = refs[:-3], refs[-3:]
    rows, steps, _ = out_ref.shape
    count = rows // len(parts)
    one = jnp.ones((8, HEAD), jnp.float32)
    results = []
    for share, ref in enumerate(parts):
        sources, size, _ = ref.shape
        numerators = size - TAIL
        tiles = numerators // 8
        blocks = [ref[s] for s in range(sources)]
        tails = [x[numerators:].astype(jnp.float32) for x in blocks]
        opened = unpack(jnp.concatenate(tails, axis=0).astype(jnp.bfloat16), tiles)
        opened = [columns(x) for x in opened]
        for a in range(tiles):
            pieces = [slice(s * 8, s * 8 + 8) for s in range(sources)]
            tops = [opened[0][a][p] for p in pieces]
            totals = [opened[1][a][p] for p in pieces]
            sums = [x[a * 8 : a * 8 + 8].astype(jnp.float32) for x in blocks]
            for u in range(steps):
                tops.append(score_ref[share, u, a])
                totals.append(one)
                sums.append(value_ref[share, u])
            _, total, summed = combine(tops, totals, sums)
            results.append((share, a * 8, summed / total))
    for share, low, result in results:
        for at in range(0, 8, steps):
            head, row = divmod((low + at) // steps, count)
            out_ref[share * count + row, :, head * HEAD : (head + 1) * HEAD] = result[
                at : at + steps
            ].astype(jnp.bfloat16)


def merge(parts, scores, values, shape):
    return pl.pallas_call(
        merge_kernel,
        out_shape=jax.ShapeDtypeStruct(shape, jnp.bfloat16),
        compiler_params=PARAMS,
        name="merge",
    )(*parts, scores, values)


CHIPS = ("y", "z", "x")


def exchange(x, axes):
    return lax.all_to_all(x, axes, split_axis=0, concat_axis=0, tiled=True)


def per_device(
    queries,
    new_kv,
    prefix_keys,
    prefix_values,
    suffix_keys,
    suffix_values,
    suffix_lengths,
    row_slot,
):
    layers = lax.axis_size("y")
    cores = lax.axis_size("core")
    members = lax.axis_size("z") * lax.axis_size("x")
    chips = layers * members
    swap = [(i, (i + 1) % cores) for i in range(cores)]

    blocks, row_slot, suffix_lengths = lax.optimization_barrier(
        (spread(queries, chips), row_slot, suffix_lengths)
    )
    near = [exchange(x, CHIPS).reshape((layers, members) + x.shape[1:]) for x in blocks]
    info = locate(row_slot, suffix_lengths, suffix_keys.shape[1])
    received = []
    for share, mine in enumerate(near):
        mine, info = lax.optimization_barrier((mine, info))
        other = lax.ppermute(mine, "core", swap)
        near_part, far_part = attend(
            info, mine, other, prefix_keys, prefix_values, suffix_keys, suffix_values, share, 2, 128
        )
        joined = join_cores(near_part, lax.ppermute(far_part, "core", swap))
        if share == SHARES - 1:
            joined, queries, new_kv = lax.optimization_barrier((joined, queries, new_kv))
        received.append(exchange(joined.reshape((chips,) + joined.shape[2:]), CHIPS))
    scores, values = new_tokens(queries, new_kv)
    return merge(received, scores, values, queries.shape)


def solution(mesh):
    fine = jax.sharding.Mesh(mesh.devices.reshape(4, 2, 4, 4), ("y", "core", "z", "x"))
    grp, seq = ("y", "core"), ("z", "x")
    placed = (
        P(grp, None, seq),
        P(grp, None, None, None),
        P(grp + seq, None),
        P(grp + seq, None),
        P(grp, seq, None),
        P(grp, seq, None),
        P(grp),
        P(),
    )
    return jax.shard_map(
        per_device, mesh=fine, in_specs=placed, out_specs=P(grp, None, seq), check_vma=False
    )
```

time: 68.3 us -> 64.4 us (0.943)
  local copies, waits for them, and re-layouts: 9.51 us -> 2.01 us
  waiting for transfers between devices: 24 us -> 30 us
  Pallas kernels: 17.1 us -> 15.6 us
    unnamed x22 -> x10, local copies, waits for them, and re-layouts: 9.51 us -> 2.01 us
    all_to_all x2, waiting for transfers between devices: 20.3 us -> 26.1 us  [exchange(): return lax.all_to_all(x, axes, split_axis=0, concat_axis=0, tiled=True)]
    pallas_call x4, Pallas kernels: 13.9 us -> 12.4 us  [the longest x1 10.2 us: attend(): pl.pallas_call(functools.partial(attend_kernel, heads=heads, chunk=chunk,...]
  transfers between devices with their start and end apart: 4 -> 4, of which waited for: 4 -> 4; matrix products, arithmetic and copies ran while one was open for 0% -> 0% of each run, Pallas kernels for 6% -> 2%
where the time goes in v2:
time: 64.4 us; the launch traced here: 64 us
  waiting for transfers between devices  30 us (47%)
  starting transfers between devices  16.3 us (25%)
  Pallas kernels  15.6 us (24%)
  local copies, waits for them, and re-layouts  2.01 us (3%)
    all_to_all x2, waiting for transfers between devices, exchange(): return lax.all_to_all(x, axes, split_axis=0, concat_axis=0, tiled=True)  26.1 us
    all_to_all x2, starting transfers between devices, exchange(): return lax.all_to_all(x, axes, split_axis=0, concat_axis=0, tiled=True)  16.1 us
    pallas_call x1, Pallas kernels, attend(): pl.pallas_call(functools.partial(attend_kernel, heads=heads, chunk=chunk,...  10.2 us
    unnamed x10, local copies, waits for them, and re-layouts  2.01 us
    ppermute x1, waiting for transfers between devices, per_device(): joined = join_cores(near_part, lax.ppermute(far_part, 'core', swap))  1.98 us
    pallas_call x1, Pallas kernels, join_cores(): pl.pallas_call(join_cores_kernel, out_shape=jax.ShapeDtypeStruct(a.shape,...  1.96 us
    ppermute x1, waiting for transfers between devices, per_device(): other = lax.ppermute(mine, 'core', swap)  1.91 us
  transfers between devices with their start and end apart: 4, of which 4 were waited for; matrix products, arithmetic and copies ran while one was open for 0% of the time, Pallas kernels for 2%

profile of v2, /device:TPU:0, one launch (start us, length us, event | category | flops | bytes accessed | tf_op | source)
XLA Modules:
  0.0 64.0 jit_solution(6312439199457122832)
XLA Ops:
  0.0 0.0 copy-start
  0.0 0.7 %copy-done = bf16[4,2,512]{2,1,0:T(2,128)(2,1)S(1)} copy-done((bf16[4,2,512]{2,1,0:T(2,128)(2,1)S(1)}, bf16[4,2,512]{2,1,0:T(2,128)(2,1)}, u32[]{:S(2)}) %copy-start) | copy-done | bytes 8216
  0.7 0.8 %spread.1 = bf16[64,32,128]{2,1,0:T(8,128)(2,1)} custom-call(bf16[4,2,512]{2,1,0:T(2,128)(2,1)S(1)} %copy-done), custom_call_target="tpu_custom_call" | custom-call | tf_op jit(solution)/shard_map/spread/pallas_call | solution.py:84
  1.5 11.5 %all-to-all-start = ((bf16[64,32,128]{2,1,0:T(8,128)(2,1)}), bf16[64,32,128]{2,1,0:T(8,128)(2,1)S(1)}, u32[]{:S(2)}, u32[]{:S(2)}) async-start(bf16[64,32,128]{2,1,0:T(8,128)(2,1)} %spread.1), calls=%async_computation | async-start | bytes 1048576 | tf_op jit(solution)/shard_map/all_to_all | solution.py:365
  13.1 0.0 copy-start.3
  13.1 0.6 %copy-done.3 = s32[32]{0:T(128)S(1)} copy-done((s32[32]{0:T(128)S(1)}, s32[32]{0:T(128)}, u32[]{:S(2)}) %copy-start.3) | copy-done | bytes 152
  13.7 0.0 copy-start.4
  13.7 0.7 %copy-done.4 = s32[4]{0:T(128)S(1)} copy-done((s32[4]{0:T(128)S(1)}, s32[4]{0:T(128)}, u32[]{:S(2)}) %copy-start.4) | copy-done | bytes 40
  14.4 1.3 %locate.1.info = s32[12]{0:T(128)S(1)} custom-call(s32[32]{0:T(128)S(1)} %copy-done.3, s32[4]{0:T(128)S(1)} %copy-done.4), custom_call_target="tpu_custom_call" | custom-call | tf_op jit(solution)/shard_map/locate/pallas_call | solution.py:111
  15.6 10.9 %all-to-all-done = bf16[64,32,128]{2,1,0:T(8,128)(2,1)S(1)} async-done(((bf16[64,32,128]{2,1,0:T(8,128)(2,1)}), bf16[64,32,128]{2,1,0:T(8,128)(2,1)S(1)}, u32[]{:S(2)}, u32[]{:S(2)}) %all-to-all-start) | async-done | bytes 524320 | tf_op jit(solution)/shard_map/all_to_all | solution.py:365
  26.5 0.0 collective-permute-start
  26.5 1.9 %collective-permute-done = bf16[4,16,32,128]{3,2,1,0:T(8,128)(2,1)S(1)} collective-permute-done((bf16[4,16,32,128]{3,2,1,0:T(8,128)(2,1)S(1)}, bf16[4,16,32,128]{3,2,1,0:T(8,128)(2,1)S(1)}, u32[]{:S(2)}, u32[]{:S(2)}) %collective-permute-start) | collective-permute-done | bytes 524320 | tf_op jit(solution)/shard_map/ppermute | solution.py:392
  28.4 10.2 %attend.1 = (bf16[4,16,40,128]{3,2,1,0:T(8,128)(2,1)S(1)}, bf16[4,16,40,128]{3,2,1,0:T(8,128)(2,1)S(1)}) custom-call(s32[12]{0:T(128)S(1)} %locate.1.info, bf16[4,8,64,128]{3,2,1,0:T(8,128)(2,1)S(1)} %bitcast.5, bf16[4,8,64,128]{3,2,1,0:T(8,128)(2,1)S(1)} %bitcast.6, bf16[1024,1024]{1,0:T(8,128)(2,1)} %refs_2_.1, bf16[1024,1024]{1,0:T(8,128)(2,1)} %refs_3_.1, ...), custom_call_target="tpu_custom_call" | custom-call | tf_op jit(solution)/shard_map/attend/pallas_call | solution.py:218
  38.6 0.0 copy-start.1
  38.6 0.0 copy-start.2
  38.6 0.2 collective-permute-start.1
  38.9 2.0 %collective-permute-done.1.b_ref = bf16[4,16,40,128]{3,2,1,0:T(8,128)(2,1)S(1)} collective-permute-done((bf16[4,16,40,128]{3,2,1,0:T(8,128)(2,1)S(1)}, bf16[4,16,40,128]{3,2,1,0:T(8,128)(2,1)S(1)}, u32[]{:S(2)}, u32[]{:S(2)}) %collective-permute-start.1) | collective-permute-done | bytes 655392 | tf_op jit(solution)/shard_map/ppermute | solution.py:396
  40.8 2.0 %join_cores.1 = bf16[4,16,40,128]{3,2,1,0:T(8,128)(2,1)} custom-call(bf16[4,16,40,128]{3,2,1,0:T(8,128)(2,1)S(1)} %get-tuple-element.22.a_ref, bf16[4,16,40,128]{3,2,1,0:T(8,128)(2,1)S(1)} %collective-permute-done.1.b_ref), custom_call_target="tpu_custom_call" | custom-call | tf_op jit(solution)/shard_map/join_cores/pallas_call | solution.py:268
  42.8 4.6 %all-to-all-start.1 = ((bf16[64,40,128]{2,1,0:T(8,128)(2,1)}), bf16[64,40,128]{2,1,0:T(8,128)(2,1)S(1)}, u32[]{:S(2)}, u32[]{:S(2)}) async-start(bf16[64,40,128]{2,1,0:T(8,128)(2,1)} %bitcast.3), calls=%async_computation.1 | async-start | bytes 1310720 | tf_op jit(solution)/shard_map/all_to_all | solution.py:365
  47.4 0.0 copy-done.1
  47.4 0.0 copy-done.2
  47.5 0.1 new_tokens.1
  47.6 15.3 %all-to-all-done.1.refs_0_ = bf16[64,40,128]{2,1,0:T(8,128)(2,1)S(1)} async-done(((bf16[64,40,128]{2,1,0:T(8,128)(2,1)}), bf16[64,40,128]{2,1,0:T(8,128)(2,1)S(1)}, u32[]{:S(2)}, u32[]{:S(2)}) %all-to-all-start.1) | async-done | bytes 655392 | tf_op jit(solution)/shard_map/all_to_all | solution.py:365
  62.8 1.2 %merge.1 = bf16[4,2,512]{2,1,0:T(2,128)(2,1)} custom-call(bf16[64,40,128]{2,1,0:T(8,128)(2,1)S(1)} %all-to-all-done.1.refs_0_, f32[1,2,4,8,128]{4,3,2,1,0:T(8,128)S(1)} %get-tuple-element.27.refs_1_, f32[1,2,8,128]{3,2,1,0:T(8,128)S(1)} %get-tuple-element.28.refs_2_), custom_call_target="tpu_custom_call" | custom-call | tf_op jit(solution)/shard_map/merge/pallas_call | solution.py:353
Async XLA Ops:
  0.0 0.7 %copy-start = (bf16[4,2,512]{2,1,0:T(2,128)(2,1)S(1)}, bf16[4,2,512]{2,1,0:T(2,128)(2,1)}, u32[]{:S(2)}) copy-start(bf16[4,2,512]{2,1,0:T(2,128)(2,1)} %q_ref.2) | copy-start | bytes 24580
  1.5 25.0 %all-to-all-start = ((bf16[64,32,128]{2,1,0:T(8,128)(2,1)}), bf16[64,32,128]{2,1,0:T(8,128)(2,1)S(1)}, u32[]{:S(2)}, u32[]{:S(2)}) async-start(bf16[64,32,128]{2,1,0:T(8,128)(2,1)} %spread.1), calls=%async_computation | async-start | bytes 1048576 | tf_op jit(solution)/shard_map/all_to_all | solution.py:365
  13.1 0.7 %copy-start.3 = (s32[32]{0:T(128)S(1)}, s32[32]{0:T(128)}, u32[]{:S(2)}) copy-start(s32[32]{0:T(128)} %slot_ref) | copy-start | bytes 388
  13.7 0.7 %copy-start.4 = (s32[4]{0:T(128)S(1)}, s32[4]{0:T(128)}, u32[]{:S(2)}) copy-start(s32[4]{0:T(128)} %length_ref) | copy-start | bytes 52
  26.5 1.9 %collective-permute-start = (bf16[4,16,32,128]{3,2,1,0:T(8,128)(2,1)S(1)}, bf16[4,16,32,128]{3,2,1,0:T(8,128)(2,1)S(1)}, u32[]{:S(2)}, u32[]{:S(2)}) collective-permute-start(bf16[4,16,32,128]{3,2,1,0:T(8,128)(2,1)S(1)} %bitcast.4), channel_id=1, source_target_pairs={{0,16},{16,0},{1,17},{17,1},{2,18},{18,2},{3,19},{19,3},{4,20},{20... | collective-permute-start | bytes 1572872 | tf_op jit(solution)/shard_map/ppermute | solution.py:392
  38.6 8.8 %copy-start.1 = (bf16[4,2,512]{2,1,0:T(2,128)(2,1)S(1)}, bf16[4,2,512]{2,1,0:T(2,128)(2,1)}, u32[]{:S(2)}) copy-start(bf16[4,2,512]{2,1,0:T(2,128)(2,1)} %q_ref.2) | copy-start | bytes 24580
  38.6 8.8 %copy-start.2 = (bf16[4,2,2,1024]{3,2,1,0:T(2,128)(2,1)S(1)}, bf16[4,2,2,1024]{3,2,1,0:T(2,128)(2,1)}, u32[]{:S(2)}) copy-start(bf16[4,2,2,1024]{3,2,1,0:T(2,128)(2,1)} %new_ref) | copy-start | bytes 98308
  38.6 2.2 %collective-permute-start.1 = (bf16[4,16,40,128]{3,2,1,0:T(8,128)(2,1)S(1)}, bf16[4,16,40,128]{3,2,1,0:T(8,128)(2,1)S(1)}, u32[]{:S(2)}, u32[]{:S(2)}) collective-permute-start(bf16[4,16,40,128]{3,2,1,0:T(8,128)(2,1)S(1)} %get-tuple-element.23), channel_id=1, source_target_pairs={{0,16},{16,0},{1,17},{17,1},{2,18},{18,2},{3,19},{19,3},{4,20},{20... | collective-permute-start | bytes 1966088 | tf_op jit(solution)/shard_map/ppermute | solution.py:396
  42.8 20.0 %all-to-all-start.1 = ((bf16[64,40,128]{2,1,0:T(8,128)(2,1)}), bf16[64,40,128]{2,1,0:T(8,128)(2,1)S(1)}, u32[]{:S(2)}, u32[]{:S(2)}) async-start(bf16[64,40,128]{2,1,0:T(8,128)(2,1)} %bitcast.3), calls=%async_computation.1 | async-start | bytes 1310720 | tf_op jit(solution)/shard_map/all_to_all | solution.py:365

commit v3 on v2

v3 whole, which is shorter than its diff:
```python
import functools
import math

import jax
import jax.numpy as jnp
from jax import lax
from jax.experimental import pallas as pl
from jax.experimental.pallas import tpu as pltpu
from jax.sharding import PartitionSpec as P

H = 64
KVH = 8
HEAD = 128
LOWEST = -(2.0**100)
SCALE = HEAD ** (-0.5) * math.log2(math.e)
TAIL = 8
PARAMS = pltpu.CompilerParams(vmem_limit_bytes=32 << 20)

NT = (((1,), (1,)), ((), ()))
NN = (((1,), (0,)), ((), ()))


def dot(a, b, dims):
    return lax.dot_general(a, b, dims, preferred_element_type=jnp.float32)


def iota(shape, axis):
    return lax.broadcasted_iota(jnp.int32, shape, axis)


def as_bf16(x):
    return x.astype(jnp.bfloat16).astype(jnp.float32)


def columns(x):
    return [x[:, a * HEAD : (a + 1) * HEAD] for a in range(x.shape[1] // HEAD)]


def pack(tops, totals):
    lane = iota((TAIL, HEAD), 1)
    piece = lax.rem(lane, 32) // 8
    packed = None
    for a, (top, total) in enumerate(zip(tops, totals)):
        high = as_bf16(total)
        mixed = jnp.where(piece == 1, high, total - high)
        mixed = jnp.where(piece == 0, top, mixed)
        packed = mixed if a == 0 else jnp.where(lane // 32 == a, mixed, packed)
    return packed.astype(jnp.bfloat16)


def unpack(tails, tiles):
    shape = (HEAD, tiles * HEAD)
    start = iota(shape, 0) - 32 * (iota(shape, 1) // HEAD)
    first = (start == 0).astype(jnp.float32).astype(jnp.bfloat16)
    second = ((start == 8) | (start == 16)).astype(jnp.float32).astype(jnp.bfloat16)
    return dot(tails, first, NN), dot(tails, second, NN)


def combine(tops, totals, numerators):
    upper = functools.reduce(jnp.maximum, tops)
    factors = [jnp.exp2(top - upper) for top in tops]
    total = sum(x * f for x, f in zip(totals, factors))
    return upper, total, sum(x * f for x, f in zip(numerators, factors))


def query_rows(q_ref):
    heads = range(q_ref.shape[2] // HEAD)
    held = [q_ref[r].astype(jnp.float32) for r in range(q_ref.shape[0])]
    return jnp.concatenate([x[:, h * HEAD : (h + 1) * HEAD] for x in held for h in heads], axis=0)


def spread_kernel(q_ref, out_ref):
    block = query_rows(q_ref).astype(jnp.bfloat16)
    for d in range(out_ref.shape[0]):
        out_ref[d] = block


def spread(queries, copies):
    return pl.pallas_call(
        spread_kernel,
        out_shape=jax.ShapeDtypeStruct((copies, queries.size // HEAD, HEAD), jnp.bfloat16),
        compiler_params=PARAMS,
        name="spread",
    )(queries)


def locate_kernel(slot_ref, length_ref, info, *, span):
    slots = length_ref.shape[0]
    cores, layers = lax.axis_size("core"), lax.axis_size("y")
    core = lax.axis_index("core")
    first = (lax.axis_index("y") * cores + core) * slots
    start = (lax.axis_index("z") * lax.axis_size("x") + lax.axis_index("x")) * span
    for j in range(slots):
        row = jnp.int32(0)
        for r in range(slot_ref.shape[0]):
            row = jnp.where(slot_ref[r] == first + j, jnp.int32(r), row)
        group = lax.div(row, slots)
        far = jnp.where(lax.rem(group, cores) == core, 0, layers)
        info[j] = lax.div(group, cores) + far
        info[slots + j] = lax.rem(row, slots)
        info[2 * slots + j] = jnp.clip(length_ref[j] - start, 0, span)


def locate(row_slot, lengths, span):
    smem = pl.BlockSpec(memory_space=pltpu.SMEM)
    return pl.pallas_call(
        functools.partial(locate_kernel, span=span),
        in_specs=[smem, smem],
        out_specs=smem,
        out_shape=jax.ShapeDtypeStruct((3 * lengths.shape[0],), jnp.int32),
        compiler_params=PARAMS,
        name="locate",
    )(row_slot, lengths)


def attend_kernel(info, *refs, heads, chunk):
    near_ref, far_ref, k_ref, v_ref, sk_ref, sv_ref, near_out, far_out = refs[:8]
    q_ref, own_top, own_acc = refs[8:]
    near, _, rows, _ = near_ref.shape
    pieces, _, halves, tiles = q_ref.shape[:4]
    numerators = tiles * 8
    per_chunk = chunk // rows
    length = k_ref.shape[0]
    slots, span, _ = sk_ref.shape
    ones = jnp.ones((length, HEAD), jnp.bfloat16)

    @pl.when(pl.program_id(0) == 0)
    def _():
        own_top[...] = jnp.full(own_top.shape, LOWEST, jnp.float32)
        own_acc[...] = jnp.zeros(own_acc.shape, jnp.float32)

    def cut(i):
        return slice(i * HEAD, (i + 1) * HEAD)

    def scored(i, c):
        g = c * per_chunk
        ref = near_ref if g < near else far_ref
        q = ref[g % near : g % near + per_chunk, i].reshape(chunk, HEAD)
        return dot(q, k_ref[:, cut(i)], NT)

    items = [(i, c) for i in range(heads) for c in range(pieces // per_chunk)]
    scores = scored(*items[0])

    held = [near_ref[...].astype(jnp.float32), far_ref[...].astype(jnp.float32)]
    for n, x in enumerate(held):
        q_ref[n * near : (n + 1) * near] = x.reshape((near,) + q_ref.shape[1:])
    position = iota((halves * 8, span), 1)
    found = []
    for j in range(slots):
        group, row, live = info[j], info[slots + j], info[2 * slots + j]
        for i in range(heads):
            q = q_ref[group, i, :, row].reshape(halves * 8, HEAD).astype(jnp.bfloat16)
            own = dot(q, sk_ref[j, :, cut(i)], NT) * SCALE
            own = jnp.where(position < live, own, LOWEST)
            peak = jnp.max(own, axis=1, keepdims=True)
            peak = jnp.broadcast_to(as_bf16(peak), (halves * 8, HEAD))
            shift = jnp.concatenate([peak] * (span // HEAD), axis=1)
            weights = jnp.exp2(own - shift).astype(jnp.bfloat16)
            values = jnp.concatenate([sv_ref[j, :, cut(i)], ones[:span]], axis=1)
            found.append((group, i, row, peak, dot(weights, values, NN)))
    for group, i, row, peak, summed in found:
        own_top[group, i, :, row] = peak.reshape(halves, 8, HEAD)
        own_acc[group, i, :, row] = summed.reshape(halves, 8, 2 * HEAD)

    for number, (i, c) in enumerate(items):
        later = scored(*items[number + 1]) if number + 1 < len(items) else None
        peak = jnp.max(scores, axis=1, keepdims=True) * SCALE
        peak = jnp.broadcast_to(as_bf16(peak), (chunk, HEAD))
        shift = jnp.concatenate([peak] * (length // HEAD), axis=1)
        weights = jnp.exp2(scores * SCALE - shift).astype(jnp.bfloat16)
        values = jnp.concatenate([v_ref[:, cut(i)], ones], axis=1)
        summed = dot(weights, values, NN)
        at = slice(c * per_chunk, (c + 1) * per_chunk)
        own = own_top[at, i].reshape(chunk, HEAD)
        carried = own_acc[at, i].reshape(chunk, 2 * HEAD)
        top = jnp.maximum(peak, own)
        keep, add = jnp.exp2(peak - top), jnp.exp2(own - top)
        total = summed[:, HEAD:] * keep + carried[:, HEAD:] * add
        numerator = (summed[:, :HEAD] * keep + carried[:, :HEAD] * add).astype(jnp.bfloat16)
        results = []
        for b in range(chunk // numerators):
            low = b * numerators
            parts = [slice(low + 8 * a, low + 8 * a + 8) for a in range(tiles)]
            tail = pack([top[p] for p in parts], [total[p] for p in parts])
            results.append((numerator[low : low + numerators], tail))
        for b, (block, tail) in enumerate(results):
            g = c * per_chunk + b // halves
            out_ref = (near_out if g < near else far_out).at[g % near, i * halves + b % halves]
            out_ref[:numerators] = block
            out_ref[numerators:] = tail
        scores = later


def attend(info, near, far, keys, values, suffix_keys, suffix_values, heads, chunk):
    layers, members, numerators, _ = near.shape
    halves = members // KVH
    rows = halves * numerators
    near, far = (x.reshape(layers, KVH, rows, HEAD) for x in (near, far))
    length = keys.shape[0]
    slots, span, _ = suffix_keys.shape
    in_hbm = [
        pltpu.with_memory_space_constraint(x, pltpu.HBM)
        for x in (keys, values, suffix_keys, suffix_values)
    ]
    wide = heads * HEAD
    by_head = pl.BlockSpec((layers, heads, rows, HEAD), lambda k: (0, k, 0, 0))
    prompt = pl.BlockSpec((length, wide), lambda k: (0, k))
    own = pl.BlockSpec((slots, span, wide), lambda k: (0, 0, k))
    out_block = (layers, heads * halves, numerators + TAIL, HEAD)
    out_spec = pl.BlockSpec(out_block, lambda k: (0, k, 0, 0))
    out = jax.ShapeDtypeStruct((layers, members, numerators + TAIL, HEAD), jnp.bfloat16)
    tiled = (2 * layers, heads, halves, numerators // 8, 8)
    return pl.pallas_call(
        functools.partial(attend_kernel, heads=heads, chunk=chunk),
        grid=(KVH // heads,),
        in_specs=[pl.BlockSpec(memory_space=pltpu.SMEM), by_head, by_head, prompt, prompt, own, own],
        out_specs=[out_spec, out_spec],
        out_shape=[out, out],
        scratch_shapes=[
            pltpu.VMEM(tiled + (HEAD,), jnp.float32),
            pltpu.VMEM(tiled + (HEAD,), jnp.float32),
            pltpu.VMEM(tiled + (2 * HEAD,), jnp.float32),
        ],
        compiler_params=PARAMS,
        name="attend",
    )(info, near, far, *in_hbm)


def join_parts(parts):
    numerators = parts[0][0].shape[0] - TAIL
    tiles = numerators // 8
    opened = []
    for blocks in parts:
        tails = [x[numerators:].astype(jnp.float32) for x in blocks]
        opened.append(unpack(jnp.concatenate(tails, axis=0).astype(jnp.bfloat16), tiles))
    joined = []
    for b in range(len(parts[0])):
        tops, totals, sums = [], [], []
        for blocks, (top, total) in zip(parts, opened):
            tops.append(columns(top[b * 8 : b * 8 + 8]))
            totals.append(columns(total[b * 8 : b * 8 + 8]))
            found = blocks[b][:numerators].astype(jnp.float32)
            sums.append([found[a * 8 : a * 8 + 8] for a in range(tiles)])
        rows = [
            combine([x[a] for x in tops], [x[a] for x in totals], [x[a] for x in sums])
            for a in range(tiles)
        ]
        block = jnp.concatenate([x[2] for x in rows], axis=0).astype(jnp.bfloat16)
        joined.append((block, pack([x[0] for x in rows], [x[1] for x in rows])))
    return joined


def join_cores_kernel(a_ref, b_ref, out_ref):
    layers, members, rows, _ = a_ref.shape
    for y in range(layers):
        parts = [[ref[y, m] for m in range(members)] for ref in (a_ref, b_ref)]
        for m, (block, tail) in enumerate(join_parts(parts)):
            out_ref[y, m, : rows - TAIL] = block
            out_ref[y, m, rows - TAIL :] = tail


def join_cores(a, b):
    return pl.pallas_call(
        join_cores_kernel,
        out_shape=jax.ShapeDtypeStruct(a.shape, a.dtype),
        compiler_params=PARAMS,
        name="join_cores",
    )(a, b)


def new_kernel(q_ref, new_ref, score_ref, value_ref):
    rows, steps, width = q_ref.shape
    member = lax.axis_index("z") * lax.axis_size("x") + lax.axis_index("x")
    kv_head = member * (width // HEAD) // (H // KVH)
    at_head = pl.ds(pl.multiple_of(kv_head * HEAD, HEAD), HEAD)
    step = lax.rem(iota((8, HEAD), 0), steps)
    queries = query_rows(q_ref)
    for r in range(rows):
        for u in range(steps):
            key, value = (
                jnp.broadcast_to(new_ref[r, u, n : n + 1, at_head].astype(jnp.float32), (8, HEAD))
                for n in range(2)
            )
            score = jnp.sum(queries[r * 8 : r * 8 + 8] * key, axis=1, keepdims=True) * SCALE
            score_ref[u, r] = jnp.where(step >= u, jnp.broadcast_to(score, (8, HEAD)), LOWEST)
            value_ref[u, r] = value


def new_tokens(queries, new_kv):
    rows, steps, _ = queries.shape
    out = jax.ShapeDtypeStruct((steps, rows, 8, HEAD), jnp.float32)
    return pl.pallas_call(
        new_kernel,
        out_shape=[out, out],
        compiler_params=PARAMS,
        name="new_tokens",
    )(queries, new_kv)


def merge_kernel(parts_ref, score_ref, value_ref, out_ref):
    rows, steps, width = out_ref.shape
    sources, size, _ = parts_ref.shape
    numerators = size - TAIL
    one = jnp.ones((8, HEAD), jnp.float32)
    blocks = [parts_ref[s] for s in range(sources)]
    tails = [x[numerators:].astype(jnp.float32) for x in blocks]
    opened = unpack(jnp.concatenate(tails, axis=0).astype(jnp.bfloat16), rows)
    opened = [columns(x) for x in opened]
    results = []
    for r in range(rows):
        pieces = [slice(s * 8, s * 8 + 8) for s in range(sources)]
        tops = [opened[0][r][p] for p in pieces]
        totals = [opened[1][r][p] for p in pieces]
        sums = [x[r * 8 : r * 8 + 8].astype(jnp.float32) for x in blocks]
        for u in range(steps):
            tops.append(score_ref[u, r])
            totals.append(one)
            sums.append(value_ref[u, r])
        _, total, summed = combine(tops, totals, sums)
        results.append(summed / total)
    for r, result in enumerate(results):
        for h in range(width // HEAD):
            out_ref[r, :, h * HEAD : (h + 1) * HEAD] = result[h * steps : (h + 1) * steps].astype(
                jnp.bfloat16
            )


def merge(parts, scores, values, shape):
    return pl.pallas_call(
        merge_kernel,
        out_shape=jax.ShapeDtypeStruct(shape, jnp.bfloat16),
        compiler_params=PARAMS,
        name="merge",
    )(parts, scores, values)


CHIPS = ("y", "z", "x")


def exchange(x, axes):
    return lax.all_to_all(x, axes, split_axis=0, concat_axis=0, tiled=True)


def per_device(
    queries,
    new_kv,
    prefix_keys,
    prefix_values,
    suffix_keys,
    suffix_values,
    suffix_lengths,
    row_slot,
):
    layers = lax.axis_size("y")
    cores = lax.axis_size("core")
    members = lax.axis_size("z") * lax.axis_size("x")
    chips = layers * members
    swap = [(i, (i + 1) % cores) for i in range(cores)]

    blocks, row_slot, suffix_lengths = lax.optimization_barrier(
        (spread(queries, chips), row_slot, suffix_lengths)
    )
    near = exchange(blocks, CHIPS)
    near, info = lax.optimization_barrier(
        (near, locate(row_slot, suffix_lengths, suffix_keys.shape[1]))
    )
    near = near.reshape((layers, members) + near.shape[1:])
    far = lax.ppermute(near, "core", swap)
    near_part, far_part = attend(
        info, near, far, prefix_keys, prefix_values, suffix_keys, suffix_values, 2, 128
    )
    joined = join_cores(near_part, lax.ppermute(far_part, "core", swap))
    joined, queries, new_kv = lax.optimization_barrier((joined, queries, new_kv))
    received = exchange(joined.reshape((chips,) + joined.shape[2:]), CHIPS)
    scores, values = new_tokens(queries, new_kv)
    return merge(received, scores, values, queries.shape)


def solution(mesh):
    fine = jax.sharding.Mesh(mesh.devices.reshape(4, 2, 4, 4), ("y", "core", "z", "x"))
    grp, seq = ("y", "core"), ("z", "x")
    placed = (
        P(grp, None, seq),
        P(grp, None, None, None),
        P(grp + seq, None),
        P(grp + seq, None),
        P(grp, seq, None),
        P(grp, seq, None),
        P(grp),
        P(),
    )
    return jax.shard_map(
        per_device, mesh=fine, in_specs=placed, out_specs=P(grp, None, seq), check_vma=False
    )
```

time: 64.4 us -> 64.5 us (level)
  no operation moved by 1% of the time
where the time goes in v3:
time: 64.5 us; the launch traced here: 64.1 us
  waiting for transfers between devices  30 us (47%)
  starting transfers between devices  16.3 us (25%)
  Pallas kernels  15.6 us (24%)
  local copies, waits for them, and re-layouts  2.01 us (3%)
    all_to_all x2, waiting for transfers between devices, exchange(): return lax.all_to_all(x, axes, split_axis=0, concat_axis=0, tiled=True)  26.1 us
    all_to_all x2, starting transfers between devices, exchange(): return lax.all_to_all(x, axes, split_axis=0, concat_axis=0, tiled=True)  16.1 us
    pallas_call x1, Pallas kernels, attend(): pl.pallas_call(functools.partial(attend_kernel, heads=heads, chunk=chunk)...  10.2 us
    unnamed x10, local copies, waits for them, and re-layouts  2.01 us
    ppermute x1, waiting for transfers between devices, per_device(): joined = join_cores(near_part, lax.ppermute(far_part, 'core', swap))  1.98 us
    pallas_call x1, Pallas kernels, join_cores(): pl.pallas_call(join_cores_kernel, out_shape=jax.ShapeDtypeStruct(a.shape,...  1.95 us
    ppermute x1, waiting for transfers between devices, per_device(): far = lax.ppermute(near, 'core', swap)  1.91 us
  transfers between devices with their start and end apart: 4, of which 4 were waited for; matrix products, arithmetic and copies ran while one was open for 0% of the time, Pallas kernels for 2%

profile of v3, /device:TPU:0, one launch (start us, length us, event | category | flops | bytes accessed | tf_op | source)
XLA Modules:
  0.0 64.1 jit_solution(15649240114963287103)
XLA Ops:
  0.0 0.0 copy-start
  0.0 0.7 %copy-done = bf16[4,2,512]{2,1,0:T(2,128)(2,1)S(1)} copy-done((bf16[4,2,512]{2,1,0:T(2,128)(2,1)S(1)}, bf16[4,2,512]{2,1,0:T(2,128)(2,1)}, u32[]{:S(2)}) %copy-start) | copy-done | bytes 8216
  0.7 0.8 %spread.1 = bf16[64,32,128]{2,1,0:T(8,128)(2,1)} custom-call(bf16[4,2,512]{2,1,0:T(2,128)(2,1)S(1)} %copy-done), custom_call_target="tpu_custom_call" | custom-call | tf_op jit(solution)/shard_map/spread/pallas_call | solution.py:79
  1.5 11.5 %all-to-all-start = ((bf16[64,32,128]{2,1,0:T(8,128)(2,1)}), bf16[64,32,128]{2,1,0:T(8,128)(2,1)S(1)}, u32[]{:S(2)}, u32[]{:S(2)}) async-start(bf16[64,32,128]{2,1,0:T(8,128)(2,1)} %spread.1), calls=%async_computation | async-start | bytes 1048576 | tf_op jit(solution)/shard_map/all_to_all | solution.py:341
  13.0 0.0 copy-start.3
  13.1 0.6 %copy-done.3 = s32[32]{0:T(128)S(1)} copy-done((s32[32]{0:T(128)S(1)}, s32[32]{0:T(128)}, u32[]{:S(2)}) %copy-start.3) | copy-done | bytes 152
  13.7 0.0 copy-start.4
  13.7 0.7 %copy-done.4 = s32[4]{0:T(128)S(1)} copy-done((s32[4]{0:T(128)S(1)}, s32[4]{0:T(128)}, u32[]{:S(2)}) %copy-start.4) | copy-done | bytes 40
  14.4 1.3 %locate.1.info = s32[12]{0:T(128)S(1)} custom-call(s32[32]{0:T(128)S(1)} %copy-done.3, s32[4]{0:T(128)S(1)} %copy-done.4), custom_call_target="tpu_custom_call" | custom-call | tf_op jit(solution)/shard_map/locate/pallas_call | solution.py:106
  15.6 10.9 %all-to-all-done = bf16[64,32,128]{2,1,0:T(8,128)(2,1)S(1)} async-done(((bf16[64,32,128]{2,1,0:T(8,128)(2,1)}), bf16[64,32,128]{2,1,0:T(8,128)(2,1)S(1)}, u32[]{:S(2)}, u32[]{:S(2)}) %all-to-all-start) | async-done | bytes 524320 | tf_op jit(solution)/shard_map/all_to_all | solution.py:341
  26.5 0.0 collective-permute-start
  26.5 1.9 %collective-permute-done = bf16[4,16,32,128]{3,2,1,0:T(8,128)(2,1)S(1)} collective-permute-done((bf16[4,16,32,128]{3,2,1,0:T(8,128)(2,1)S(1)}, bf16[4,16,32,128]{3,2,1,0:T(8,128)(2,1)S(1)}, u32[]{:S(2)}, u32[]{:S(2)}) %collective-permute-start) | collective-permute-done | bytes 524320 | tf_op jit(solution)/shard_map/ppermute | solution.py:368
  28.4 10.2 %attend.1 = (bf16[4,16,40,128]{3,2,1,0:T(8,128)(2,1)S(1)}, bf16[4,16,40,128]{3,2,1,0:T(8,128)(2,1)S(1)}) custom-call(s32[12]{0:T(128)S(1)} %locate.1.info, bf16[4,8,64,128]{3,2,1,0:T(8,128)(2,1)S(1)} %bitcast.5, bf16[4,8,64,128]{3,2,1,0:T(8,128)(2,1)S(1)} %bitcast.6, bf16[1024,1024]{1,0:T(8,128)(2,1)} %refs_2_.1, bf16[1024,1024]{1,0:T(8,128)(2,1)} %refs_3_.1, ...), custom_call_target="tpu_custom_call" | custom-call | tf_op jit(solution)/shard_map/attend/pallas_call | solution.py:213
  38.7 0.0 copy-start.1
  38.7 0.0 copy-start.2
  38.7 0.2 collective-permute-start.1
  38.9 2.0 %collective-permute-done.1.b_ref = bf16[4,16,40,128]{3,2,1,0:T(8,128)(2,1)S(1)} collective-permute-done((bf16[4,16,40,128]{3,2,1,0:T(8,128)(2,1)S(1)}, bf16[4,16,40,128]{3,2,1,0:T(8,128)(2,1)S(1)}, u32[]{:S(2)}, u32[]{:S(2)}) %collective-permute-start.1) | collective-permute-done | bytes 655392 | tf_op jit(solution)/shard_map/ppermute | solution.py:372
  40.9 2.0 %join_cores.1 = bf16[4,16,40,128]{3,2,1,0:T(8,128)(2,1)} custom-call(bf16[4,16,40,128]{3,2,1,0:T(8,128)(2,1)S(1)} %get-tuple-element.22.a_ref, bf16[4,16,40,128]{3,2,1,0:T(8,128)(2,1)S(1)} %collective-permute-done.1.b_ref), custom_call_target="tpu_custom_call" | custom-call | tf_op jit(solution)/shard_map/join_cores/pallas_call | solution.py:263
  42.8 4.6 %all-to-all-start.1 = ((bf16[64,40,128]{2,1,0:T(8,128)(2,1)}), bf16[64,40,128]{2,1,0:T(8,128)(2,1)S(1)}, u32[]{:S(2)}, u32[]{:S(2)}) async-start(bf16[64,40,128]{2,1,0:T(8,128)(2,1)} %bitcast.3), calls=%async_computation.1 | async-start | bytes 1310720 | tf_op jit(solution)/shard_map/all_to_all | solution.py:341
  47.5 0.0 copy-done.1
  47.5 0.0 copy-done.2
  47.5 0.1 new_tokens.1
  47.6 15.3 %all-to-all-done.1.parts_ref = bf16[64,40,128]{2,1,0:T(8,128)(2,1)S(1)} async-done(((bf16[64,40,128]{2,1,0:T(8,128)(2,1)}), bf16[64,40,128]{2,1,0:T(8,128)(2,1)S(1)}, u32[]{:S(2)}, u32[]{:S(2)}) %all-to-all-start.1) | async-done | bytes 655392 | tf_op jit(solution)/shard_map/all_to_all | solution.py:341
  62.9 1.2 %merge.1 = bf16[4,2,512]{2,1,0:T(2,128)(2,1)} custom-call(bf16[64,40,128]{2,1,0:T(8,128)(2,1)S(1)} %all-to-all-done.1.parts_ref, f32[2,4,8,128]{3,2,1,0:T(8,128)S(1)} %get-tuple-element.27.score_ref, f32[2,4,8,128]{3,2,1,0:T(8,128)S(1)} %get-tuple-element.28.value_ref), custom_call_target="tpu_custom_call" | custom-call | tf_op jit(solution)/shard_map/merge/pallas_call | solution.py:329
Async XLA Ops:
  0.0 0.7 %copy-start = (bf16[4,2,512]{2,1,0:T(2,128)(2,1)S(1)}, bf16[4,2,512]{2,1,0:T(2,128)(2,1)}, u32[]{:S(2)}) copy-start(bf16[4,2,512]{2,1,0:T(2,128)(2,1)} %q_ref.2) | copy-start | bytes 24580
  1.5 25.0 %all-to-all-start = ((bf16[64,32,128]{2,1,0:T(8,128)(2,1)}), bf16[64,32,128]{2,1,0:T(8,128)(2,1)S(1)}, u32[]{:S(2)}, u32[]{:S(2)}) async-start(bf16[64,32,128]{2,1,0:T(8,128)(2,1)} %spread.1), calls=%async_computation | async-start | bytes 1048576 | tf_op jit(solution)/shard_map/all_to_all | solution.py:341
  13.0 0.7 %copy-start.3 = (s32[32]{0:T(128)S(1)}, s32[32]{0:T(128)}, u32[]{:S(2)}) copy-start(s32[32]{0:T(128)} %slot_ref) | copy-start | bytes 388
  13.7 0.7 %copy-start.4 = (s32[4]{0:T(128)S(1)}, s32[4]{0:T(128)}, u32[]{:S(2)}) copy-start(s32[4]{0:T(128)} %length_ref) | copy-start | bytes 52
  26.5 1.9 %collective-permute-start = (bf16[4,16,32,128]{3,2,1,0:T(8,128)(2,1)S(1)}, bf16[4,16,32,128]{3,2,1,0:T(8,128)(2,1)S(1)}, u32[]{:S(2)}, u32[]{:S(2)}) collective-permute-start(bf16[4,16,32,128]{3,2,1,0:T(8,128)(2,1)S(1)} %bitcast.4), channel_id=1, source_target_pairs={{0,16},{16,0},{1,17},{17,1},{2,18},{18,2},{3,19},{19,3},{4,20},{20... | collective-permute-start | bytes 1572872 | tf_op jit(solution)/shard_map/ppermute | solution.py:368
  38.7 8.8 %copy-start.1 = (bf16[4,2,512]{2,1,0:T(2,128)(2,1)S(1)}, bf16[4,2,512]{2,1,0:T(2,128)(2,1)}, u32[]{:S(2)}) copy-start(bf16[4,2,512]{2,1,0:T(2,128)(2,1)} %q_ref.2) | copy-start | bytes 24580
  38.7 8.8 %copy-start.2 = (bf16[4,2,2,1024]{3,2,1,0:T(2,128)(2,1)S(1)}, bf16[4,2,2,1024]{3,2,1,0:T(2,128)(2,1)}, u32[]{:S(2)}) copy-start(bf16[4,2,2,1024]{3,2,1,0:T(2,128)(2,1)} %new_ref) | copy-start | bytes 98308
  38.7 2.2 %collective-permute-start.1 = (bf16[4,16,40,128]{3,2,1,0:T(8,128)(2,1)S(1)}, bf16[4,16,40,128]{3,2,1,0:T(8,128)(2,1)S(1)}, u32[]{:S(2)}, u32[]{:S(2)}) collective-permute-start(bf16[4,16,40,128]{3,2,1,0:T(8,128)(2,1)S(1)} %get-tuple-element.23), channel_id=1, source_target_pairs={{0,16},{16,0},{1,17},{17,1},{2,18},{18,2},{3,19},{19,3},{4,20},{20... | collective-permute-start | bytes 1966088 | tf_op jit(solution)/shard_map/ppermute | solution.py:372
  42.8 20.0 %all-to-all-start.1 = ((bf16[64,40,128]{2,1,0:T(8,128)(2,1)}), bf16[64,40,128]{2,1,0:T(8,128)(2,1)S(1)}, u32[]{:S(2)}, u32[]{:S(2)}) async-start(bf16[64,40,128]{2,1,0:T(8,128)(2,1)} %bitcast.3), calls=%async_computation.1 | async-start | bytes 1310720 | tf_op jit(solution)/shard_map/all_to_all | solution.py:341

commit v4 on v3

--- a/solution.py
+++ b/solution.py
@@ -69,25 +69,45 @@
     return jnp.concatenate([x[:, h * HEAD : (h + 1) * HEAD] for x in held for h in heads], axis=0)
 
 
-def spread_kernel(q_ref, out_ref):
-    block = query_rows(q_ref).astype(jnp.bfloat16)
-    for d in range(out_ref.shape[0]):
-        out_ref[d] = block
-
-
-def spread(queries, copies):
-    return pl.pallas_call(
-        spread_kernel,
-        out_shape=jax.ShapeDtypeStruct((copies, queries.size // HEAD, HEAD), jnp.bfloat16),
-        compiler_params=PARAMS,
-        name="spread",
-    )(queries)
+def gather_rows_kernel(q_ref, out_ref):
+    out_ref[...] = query_rows(q_ref).astype(jnp.bfloat16)
+
+
+def gather_rows(queries):
+    return pl.pallas_call(
+        gather_rows_kernel,
+        out_shape=jax.ShapeDtypeStruct((queries.size // HEAD, HEAD), jnp.bfloat16),
+        compiler_params=PARAMS,
+        name="gather_rows",
+    )(pltpu.with_memory_space_constraint(queries, pltpu.HBM))
+
+
+def layer_at(offset):
+    size = lax.axis_size("y")
+    return lax.rem(lax.axis_index("y") + offset + size, size)
+
+
+def place_kernel(*refs):
+    out_ref = refs[-1]
+    blocks = [ref[...] for ref in refs[:-1]]
+    for offset, block in enumerate(blocks):
+        layer = layer_at(-offset)
+        for d in range(out_ref.shape[0]):
+            out_ref[d, layer] = block
+
+
+def place(blocks, copies):
+    return pl.pallas_call(
+        place_kernel,
+        out_shape=jax.ShapeDtypeStruct((copies, len(blocks)) + blocks[0].shape, jnp.bfloat16),
+        compiler_params=PARAMS,
+        name="place",
+    )(*blocks)
 
 
 def locate_kernel(slot_ref, length_ref, info, *, span):
     slots = length_ref.shape[0]
-    cores, layers = lax.axis_size("core"), lax.axis_size("y")
-    core = lax.axis_index("core")
+    cores, core = lax.axis_size("core"), lax.axis_index("core")
     first = (lax.axis_index("y") * cores + core) * slots
     start = (lax.axis_index("z") * lax.axis_size("x") + lax.axis_index("x")) * span
     for j in range(slots):
@@ -95,10 +115,10 @@
         for r in range(slot_ref.shape[0]):
             row = jnp.where(slot_ref[r] == first + j, jnp.int32(r), row)
         group = lax.div(row, slots)
-        far = jnp.where(lax.rem(group, cores) == core, 0, layers)
-        info[j] = lax.div(group, cores) + far
-        info[slots + j] = lax.rem(row, slots)
-        info[2 * slots + j] = jnp.clip(length_ref[j] - start, 0, span)
+        info[j] = jnp.where(lax.rem(group, cores) == core, 0, 1)
+        info[slots + j] = lax.div(group, cores)
+        info[2 * slots + j] = lax.rem(row, slots)
+        info[3 * slots + j] = jnp.clip(length_ref[j] - start, 0, span)
 
 
 def locate(row_slot, lengths, span):
@@ -107,19 +127,19 @@
         functools.partial(locate_kernel, span=span),
         in_specs=[smem, smem],
         out_specs=smem,
-        out_shape=jax.ShapeDtypeStruct((3 * lengths.shape[0],), jnp.int32),
+        out_shape=jax.ShapeDtypeStruct((4 * lengths.shape[0],), jnp.int32),
         compiler_params=PARAMS,
         name="locate",
     )(row_slot, lengths)
 
 
-def attend_kernel(info, *refs, heads, chunk):
+def attend_kernel(info, *refs, heads):
     near_ref, far_ref, k_ref, v_ref, sk_ref, sv_ref, near_out, far_out = refs[:8]
     q_ref, own_top, own_acc = refs[8:]
-    near, _, rows, _ = near_ref.shape
-    pieces, _, halves, tiles = q_ref.shape[:4]
-    numerators = tiles * 8
-    per_chunk = chunk // rows
+    _, layers, numerators, _ = near_ref.shape
+    halves = near_ref.shape[0] // heads
+    tiles = numerators // 8
+    chunk = layers * numerators
     length = k_ref.shape[0]
     slots, span, _ = sk_ref.shape
     ones = jnp.ones((length, HEAD), jnp.bfloat16)
@@ -132,24 +152,22 @@
     def cut(i):
         return slice(i * HEAD, (i + 1) * HEAD)
 
-    def scored(i, c):
-        g = c * per_chunk
-        ref = near_ref if g < near else far_ref
-        q = ref[g % near : g % near + per_chunk, i].reshape(chunk, HEAD)
+    def scored(i, side, half):
+        q = (near_ref, far_ref)[side][i * halves + half].reshape(chunk, HEAD)
         return dot(q, k_ref[:, cut(i)], NT)
 
-    items = [(i, c) for i in range(heads) for c in range(pieces // per_chunk)]
+    items = [(i, side, half) for i in range(heads) for side in range(2) for half in range(halves)]
     scores = scored(*items[0])
 
-    held = [near_ref[...].astype(jnp.float32), far_ref[...].astype(jnp.float32)]
-    for n, x in enumerate(held):
-        q_ref[n * near : (n + 1) * near] = x.reshape((near,) + q_ref.shape[1:])
+    for side, ref in enumerate((near_ref, far_ref)):
+        q_ref[side] = ref[...].astype(jnp.float32).reshape(q_ref.shape[1:])
     position = iota((halves * 8, span), 1)
     found = []
     for j in range(slots):
-        group, row, live = info[j], info[slots + j], info[2 * slots + j]
+        side, layer, row, live = (info[n * slots + j] for n in range(4))
         for i in range(heads):
-            q = q_ref[group, i, :, row].reshape(halves * 8, HEAD).astype(jnp.bfloat16)
+            at = slice(i * halves, (i + 1) * halves)
+            q = q_ref[side, at, layer, row].reshape(halves * 8, HEAD).astype(jnp.bfloat16)
             own = dot(q, sk_ref[j, :, cut(i)], NT) * SCALE
             own = jnp.where(position < live, own, LOWEST)
             peak = jnp.max(own, axis=1, keepdims=True)
@@ -157,12 +175,12 @@
             shift = jnp.concatenate([peak] * (span // HEAD), axis=1)
             weights = jnp.exp2(own - shift).astype(jnp.bfloat16)
             values = jnp.concatenate([sv_ref[j, :, cut(i)], ones[:span]], axis=1)
-            found.append((group, i, row, peak, dot(weights, values, NN)))
-    for group, i, row, peak, summed in found:
-        own_top[group, i, :, row] = peak.reshape(halves, 8, HEAD)
-        own_acc[group, i, :, row] = summed.reshape(halves, 8, 2 * HEAD)
-
-    for number, (i, c) in enumerate(items):
+            found.append(((side, at, layer, row), peak, dot(weights, values, NN)))
+    for at, peak, summed in found:
+        own_top[at] = peak.reshape(halves, 8, HEAD)
+        own_acc[at] = summed.reshape(halves, 8, 2 * HEAD)
+
+    for number, (i, side, half) in enumerate(items):
         later = scored(*items[number + 1]) if number + 1 < len(items) else None
         peak = jnp.max(scores, axis=1, keepdims=True) * SCALE
         peak = jnp.broadcast_to(as_bf16(peak), (chunk, HEAD))
@@ -170,9 +188,8 @@
         weights = jnp.exp2(scores * SCALE - shift).astype(jnp.bfloat16)
         values = jnp.concatenate([v_ref[:, cut(i)], ones], axis=1)
         summed = dot(weights, values, NN)
-        at = slice(c * per_chunk, (c + 1) * per_chunk)
-        own = own_top[at, i].reshape(chunk, HEAD)
-        carried = own_acc[at, i].reshape(chunk, 2 * HEAD)
+        own = own_top[side, i * halves + half].reshape(chunk, HEAD)
+        carried = own_acc[side, i * halves + half].reshape(chunk, 2 * HEAD)
         top = jnp.maximum(peak, own)
         keep, add = jnp.exp2(peak - top), jnp.exp2(own - top)
         total = summed[:, HEAD:] * keep + carried[:, HEAD:] * add
@@ -183,19 +200,16 @@
             parts = [slice(low + 8 * a, low + 8 * a + 8) for a in range(tiles)]
             tail = pack([top[p] for p in parts], [total[p] for p in parts])
             results.append((numerator[low : low + numerators], tail))
-        for b, (block, tail) in enumerate(results):
-            g = c * per_chunk + b // halves
-            out_ref = (near_out if g < near else far_out).at[g % near, i * halves + b % halves]
-            out_ref[:numerators] = block
-            out_ref[numerators:] = tail
+        out_ref = (near_out, far_out)[side].at[i * halves + half]
+        for layer, (block, tail) in enumerate(results):
+            out_ref[layer, :numerators] = block
+            out_ref[layer, numerators:] = tail
         scores = later
 
 
-def attend(info, near, far, keys, values, suffix_keys, suffix_values, heads, chunk):
-    layers, members, numerators, _ = near.shape
+def attend(info, near, far, keys, values, suffix_keys, suffix_values, heads):
+    members, layers, numerators, _ = near.shape
     halves = members // KVH
-    rows = halves * numerators
-    near, far = (x.reshape(layers, KVH, rows, HEAD) for x in (near, far))
     length = keys.shape[0]
     slots, span, _ = suffix_keys.shape
     in_hbm = [
@@ -203,15 +217,15 @@
         for x in (keys, values, suffix_keys, suffix_values)
     ]
     wide = heads * HEAD
-    by_head = pl.BlockSpec((layers, heads, rows, HEAD), lambda k: (0, k, 0, 0))
+    by_head = pl.BlockSpec((heads * halves, layers, numerators, HEAD), lambda k: (k, 0, 0, 0))
     prompt = pl.BlockSpec((length, wide), lambda k: (0, k))
     own = pl.BlockSpec((slots, span, wide), lambda k: (0, 0, k))
-    out_block = (layers, heads * halves, numerators + TAIL, HEAD)
-    out_spec = pl.BlockSpec(out_block, lambda k: (0, k, 0, 0))
-    out = jax.ShapeDtypeStruct((layers, members, numerators + TAIL, HEAD), jnp.bfloat16)
-    tiled = (2 * layers, heads, halves, numerators // 8, 8)
-    return pl.pallas_call(
-        functools.partial(attend_kernel, heads=heads, chunk=chunk),
+    rows = numerators + TAIL
+    out_spec = pl.BlockSpec((heads * halves, layers, rows, HEAD), lambda k: (k, 0, 0, 0))
+    out = jax.ShapeDtypeStruct((members, layers, rows, HEAD), jnp.bfloat16)
+    tiled = (2, heads * halves, layers, numerators // 8, 8)
+    return pl.pallas_call(
+        functools.partial(attend_kernel, heads=heads),
         grid=(KVH // heads,),
         in_specs=[pl.BlockSpec(memory_space=pltpu.SMEM), by_head, by_head, prompt, prompt, own, own],
         out_specs=[out_spec, out_spec],
@@ -251,12 +265,13 @@
 
 
 def join_cores_kernel(a_ref, b_ref, out_ref):
-    layers, members, rows, _ = a_ref.shape
-    for y in range(layers):
-        parts = [[ref[y, m] for m in range(members)] for ref in (a_ref, b_ref)]
-        for m, (block, tail) in enumerate(join_parts(parts)):
-            out_ref[y, m, : rows - TAIL] = block
-            out_ref[y, m, rows - TAIL :] = tail
+    members, layers, rows, _ = a_ref.shape
+    for first in range(0, members, 4):
+        at = [(m, y) for m in range(first, first + 4) for y in range(layers)]
+        parts = [[ref[m, y] for m, y in at] for ref in (a_ref, b_ref)]
+        for (m, y), (block, tail) in zip(at, join_parts(parts)):
+            out_ref[m, y, : rows - TAIL] = block
+            out_ref[m, y, rows - TAIL :] = tail
 
 
 def join_cores(a, b):
@@ -266,6 +281,25 @@
         compiler_params=PARAMS,
         name="join_cores",
     )(a, b)
+
+
+def join_plane_kernel(parts_ref, *out_refs):
+    members, _, rows, _ = parts_ref.shape
+    order = [layer_at(offset) for offset in range(len(out_refs))]
+    parts = [[parts_ref[m, y] for y in order] for m in range(members)]
+    for (block, tail), out_ref in zip(join_parts(parts), out_refs):
+        out_ref[: rows - TAIL] = block
+        out_ref[rows - TAIL :] = tail
+
+
+def join_plane(parts):
+    out = jax.ShapeDtypeStruct(parts.shape[2:], parts.dtype)
+    return pl.pallas_call(
+        join_plane_kernel,
+        out_shape=[out] * parts.shape[1],
+        compiler_params=PARAMS,
+        name="join_plane",
+    )(parts)
 
 
 def new_kernel(q_ref, new_ref, score_ref, value_ref):
@@ -297,12 +331,13 @@
     )(queries, new_kv)
 
 
-def merge_kernel(parts_ref, score_ref, value_ref, out_ref):
+def merge_kernel(*refs):
+    score_ref, value_ref, out_ref = refs[-3:]
     rows, steps, width = out_ref.shape
-    sources, size, _ = parts_ref.shape
-    numerators = size - TAIL
+    sources = len(refs) - 3
+    numerators = refs[0].shape[0] - TAIL
     one = jnp.ones((8, HEAD), jnp.float32)
-    blocks = [parts_ref[s] for s in range(sources)]
+    blocks = [ref[...] for ref in refs[:sources]]
     tails = [x[numerators:].astype(jnp.float32) for x in blocks]
     opened = unpack(jnp.concatenate(tails, axis=0).astype(jnp.bfloat16), rows)
     opened = [columns(x) for x in opened]
@@ -331,10 +366,10 @@
         out_shape=jax.ShapeDtypeStruct(shape, jnp.bfloat16),
         compiler_params=PARAMS,
         name="merge",
-    )(parts, scores, values)
-
-
-CHIPS = ("y", "z", "x")
+    )(*parts, scores, values)
+
+
+PLANE = ("z", "x")
 
 
 def exchange(x, axes):
@@ -354,25 +389,29 @@
     layers = lax.axis_size("y")
     cores = lax.axis_size("core")
     members = lax.axis_size("z") * lax.axis_size("x")
-    chips = layers * members
     swap = [(i, (i + 1) % cores) for i in range(cores)]
 
-    blocks, row_slot, suffix_lengths = lax.optimization_barrier(
-        (spread(queries, chips), row_slot, suffix_lengths)
-    )
-    near = exchange(blocks, CHIPS)
+    def to_layer(x, by):
+        return lax.ppermute(x, "y", [(i, (i + by) % layers) for i in range(layers)])
+
+    own = gather_rows(queries)
+    blocks = place([own] + [to_layer(own, by) for by in range(1, layers)], members)
+    blocks, row_slot, suffix_lengths = lax.optimization_barrier((blocks, row_slot, suffix_lengths))
+    near = exchange(blocks, PLANE)
     near, info = lax.optimization_barrier(
         (near, locate(row_slot, suffix_lengths, suffix_keys.shape[1]))
     )
-    near = near.reshape((layers, members) + near.shape[1:])
     far = lax.ppermute(near, "core", swap)
     near_part, far_part = attend(
-        info, near, far, prefix_keys, prefix_values, suffix_keys, suffix_values, 2, 128
+        info, near, far, prefix_keys, prefix_values, suffix_keys, suffix_values, 2
     )
     joined = join_cores(near_part, lax.ppermute(far_part, "core", swap))
     joined, queries, new_kv = lax.optimization_barrier((joined, queries, new_kv))
-    received = exchange(joined.reshape((chips,) + joined.shape[2:]), CHIPS)
-    scores, values = new_tokens(queries, new_kv)
+    parts, scores, values = lax.optimization_barrier(
+        (exchange(joined, PLANE), *new_tokens(queries, new_kv))
+    )
+    parts = join_plane(parts)
+    received = [parts[0]] + [to_layer(parts[by], by) for by in range(1, layers)]
     return merge(received, scores, values, queries.shape)
 
 

time: 64.5 us -> 69.9 us (1.084)
  starting transfers between devices: 16.3 us -> 20.8 us
  Pallas kernels: 15.6 us -> 16.9 us
    ppermute x0 -> x6, starting transfers between devices: none -> 9.13 us  [to_layer(): return lax.ppermute(x, 'y', [(i, (i + by) % layers) for i in range(layers)])]
    ppermute x0 -> x6, waiting for transfers between devices: none -> 5.43 us  [to_layer(): return lax.ppermute(x, 'y', [(i, (i + by) % layers) for i in range(layers)])]
    all_to_all x2, waiting for transfers between devices: 26.1 us -> 20.9 us  [exchange(): return lax.all_to_all(x, axes, split_axis=0, concat_axis=0, tiled=True)]
    all_to_all x2, starting transfers between devices: 16.1 us -> 11.5 us  [exchange(): return lax.all_to_all(x, axes, split_axis=0, concat_axis=0, tiled=True)]
    pallas_call x2 -> x4, Pallas kernels: 11.1 us -> 12.8 us  [the longest x1 10.2 us: attend(): pl.pallas_call(functools.partial(attend_kernel, heads=heads), grid=(KVH /...]
    unnamed x10 -> x8, local copies, waits for them, and re-layouts: 2.01 us -> 1.32 us
  transfers between devices with their start and end apart: 4 -> 10, of which waited for: 4 -> 9; matrix products, arithmetic and copies ran while one was open for 0% -> 0% of each run, Pallas kernels for 2% -> 2%
where the time goes in v4:
time: 69.9 us; the launch traced here: 69.3 us
  waiting for transfers between devices  30.2 us (43%)
  starting transfers between devices  20.8 us (30%)
  Pallas kernels  16.9 us (24%)
  local copies, waits for them, and re-layouts  1.32 us (2%)
    all_to_all x2, waiting for transfers between devices, exchange(): return lax.all_to_all(x, axes, split_axis=0, concat_axis=0, tiled=True)  20.9 us
    all_to_all x2, starting transfers between devices, exchange(): return lax.all_to_all(x, axes, split_axis=0, concat_axis=0, tiled=True)  11.5 us
    pallas_call x1, Pallas kernels, attend(): pl.pallas_call(functools.partial(attend_kernel, heads=heads), grid=(KVH /...  10.2 us
    ppermute x6, starting transfers between devices, to_layer(): return lax.ppermute(x, 'y', [(i, (i + by) % layers) for i in range(layers)])  9.13 us
    ppermute x6, waiting for transfers between devices, to_layer(): return lax.ppermute(x, 'y', [(i, (i + by) % layers) for i in range(layers)])  5.43 us
    ppermute x1, waiting for transfers between devices, per_device(): joined = join_cores(near_part, lax.ppermute(far_part, 'core', swap))  1.99 us
    pallas_call x1, Pallas kernels, join_cores(): pl.pallas_call(join_cores_kernel, out_shape=jax.ShapeDtypeStruct(a.shape,...  1.95 us
    ppermute x1, waiting for transfers between devices, per_device(): far = lax.ppermute(near, 'core', swap)  1.91 us
  transfers between devices with their start and end apart: 10, of which 9 were waited for; matrix products, arithmetic and copies ran while one was open for 0% of the time, Pallas kernels for 2%

profile of v4, /device:TPU:0, one launch (start us, length us, event | category | flops | bytes accessed | tf_op | source)
XLA Modules:
  0.0 69.3 jit_solution(6872557945152623550)
XLA Ops:
  0.0 0.7 %gather_rows.1.refs_0_ = bf16[32,128]{1,0:T(8,128)(2,1)S(1)} custom-call(bf16[4,2,512]{2,1,0:T(2,128)(2,1)} %q_ref.2), custom_call_target="tpu_custom_call" | custom-call | tf_op jit(solution)/shard_map/gather_rows/pallas_call | solution.py:77
  0.7 3.2 %collective-permute-start.2 = (bf16[32,128]{1,0:T(8,128)(2,1)S(1)}, bf16[32,128]{1,0:T(8,128)(2,1)S(1)}, u32[]{:S(2)}, u32[]{:S(2)}) collective-permute-start(bf16[32,128]{1,0:T(8,128)(2,1)S(1)} %gather_rows.1.refs_0_), channel_id=1, source_target_pairs={{0,96},{32,0},{64,32},{96,64},{1,97},{33,1},{65,33},{97,65},{2,98}... | collective-permute-start | bytes 24584 | tf_op jit(solution)/shard_map/ppermute | solution.py:395
  3.9 0.6 collective-permute-start.1
  4.5 1.0 %collective-permute-start = (bf16[32,128]{1,0:T(8,128)(2,1)S(1)}, bf16[32,128]{1,0:T(8,128)(2,1)S(1)}, u32[]{:S(2)}, u32[]{:S(2)}) collective-permute-start(bf16[32,128]{1,0:T(8,128)(2,1)S(1)} %gather_rows.1.refs_0_), channel_id=1, source_target_pairs={{0,32},{32,64},{64,96},{96,0},{1,33},{33,65},{65,97},{97,1},{2,34}... | collective-permute-start | bytes 24584 | tf_op jit(solution)/shard_map/ppermute | solution.py:395
  5.5 0.0 collective-permute-done.2.refs_3_
  5.5 3.6 %collective-permute-done.1.refs_2_ = bf16[32,128]{1,0:T(8,128)(2,1)S(1)} collective-permute-done((bf16[32,128]{1,0:T(8,128)(2,1)S(1)}, bf16[32,128]{1,0:T(8,128)(2,1)S(1)}, u32[]{:S(2)}, u32[]{:S(2)}) %collective-permute-start.1) | collective-permute-done | bytes 8224 | tf_op jit(solution)/shard_map/ppermute | solution.py:395
  9.0 0.3 collective-permute-done.refs_1_
  9.4 0.9 %place.1 = bf16[16,4,32,128]{3,2,1,0:T(8,128)(2,1)} custom-call(bf16[32,128]{1,0:T(8,128)(2,1)S(1)} %gather_rows.1.refs_0_, bf16[32,128]{1,0:T(8,128)(2,1)S(1)} %collective-permute-done.refs_1_, bf16[32,128]{1,0:T(8,128)(2,1)S(1)} %collective-permute-done.1.refs_2_, bf16[32,128]{1,0:T(8,128)(2,1)S(1)} %collective-permute-done.2.refs_3_), custom_call_target="tpu_custom_call" | custom-call | tf_op jit(solution)/shard_map/place/pallas_call | solution.py:100
  10.2 7.9 %all-to-all-start = ((bf16[16,4,32,128]{3,2,1,0:T(8,128)(2,1)}), bf16[16,4,32,128]{3,2,1,0:T(8,128)(2,1)S(1)}, u32[]{:S(2)}, u32[]{:S(2)}) async-start(bf16[16,4,32,128]{3,2,1,0:T(8,128)(2,1)} %place.1), calls=%async_computation | async-start | bytes 1048576 | tf_op jit(solution)/shard_map/all_to_all | solution.py:376
  18.1 0.0 copy-start.2
  18.1 0.6 copy-done.2
  18.8 0.0 copy-start.3
  18.8 0.7 copy-done.3
  19.4 1.3 %locate.1.info = s32[16]{0:T(128)S(1)} custom-call(s32[32]{0:T(128)S(1)} %copy-done.2, s32[4]{0:T(128)S(1)} %copy-done.3), custom_call_target="tpu_custom_call" | custom-call | tf_op jit(solution)/shard_map/locate/pallas_call | solution.py:126
  20.7 7.5 %all-to-all-done.refs_0_ = bf16[16,4,32,128]{3,2,1,0:T(8,128)(2,1)S(1)} async-done(((bf16[16,4,32,128]{3,2,1,0:T(8,128)(2,1)}), bf16[16,4,32,128]{3,2,1,0:T(8,128)(2,1)S(1)}, u32[]{:S(2)}, u32[]{:S(2)}) %all-to-all-start) | async-done | bytes 524320 | tf_op jit(solution)/shard_map/all_to_all | solution.py:376
  28.2 0.0 collective-permute-start.3
  28.2 1.9 %collective-permute-done.3.refs_1_ = bf16[16,4,32,128]{3,2,1,0:T(8,128)(2,1)S(1)} collective-permute-done((bf16[16,4,32,128]{3,2,1,0:T(8,128)(2,1)S(1)}, bf16[16,4,32,128]{3,2,1,0:T(8,128)(2,1)S(1)}, u32[]{:S(2)}, u32[]{:S(2)}) %collective-permute-start.3) | collective-permute-done | bytes 524320 | tf_op jit(solution)/shard_map/ppermute | solution.py:404
  30.1 10.2 %attend.1 = (bf16[16,4,40,128]{3,2,1,0:T(8,128)(2,1)S(1)}, bf16[16,4,40,128]{3,2,1,0:T(8,128)(2,1)S(1)}) custom-call(s32[16]{0:T(128)S(1)} %locate.1.info, bf16[16,4,32,128]{3,2,1,0:T(8,128)(2,1)S(1)} %all-to-all-done.refs_0_, bf16[16,4,32,128]{3,2,1,0:T(8,128)(2,1)S(1)} %collective-permute-done.3.refs_1_, bf16[1024,1024]{1,0:T(8,128)(2,1)} %refs_2_.1, ...), custom_call_target="tpu_custom_call" | custom-call | tf_op jit(solution)/shard_map/attend/pallas_call | solution.py:227
  40.3 0.0 copy-start
  40.3 0.0 copy-start.1
  40.3 0.2 collective-permute-start.4
  40.5 2.0 %collective-permute-done.4.b_ref = bf16[16,4,40,128]{3,2,1,0:T(8,128)(2,1)S(1)} collective-permute-done((bf16[16,4,40,128]{3,2,1,0:T(8,128)(2,1)S(1)}, bf16[16,4,40,128]{3,2,1,0:T(8,128)(2,1)S(1)}, u32[]{:S(2)}, u32[]{:S(2)}) %collective-permute-start.4) | collective-permute-done | bytes 655392 | tf_op jit(solution)/shard_map/ppermute | solution.py:408
  42.5 2.0 %join_cores.1 = bf16[16,4,40,128]{3,2,1,0:T(8,128)(2,1)} custom-call(bf16[16,4,40,128]{3,2,1,0:T(8,128)(2,1)S(1)} %get-tuple-element.29.a_ref, bf16[16,4,40,128]{3,2,1,0:T(8,128)(2,1)S(1)} %collective-permute-done.4.b_ref), custom_call_target="tpu_custom_call" | custom-call | tf_op jit(solution)/shard_map/join_cores/pallas_call | solution.py:278
  44.5 3.6 %all-to-all-start.1 = ((bf16[16,4,40,128]{3,2,1,0:T(8,128)(2,1)}), bf16[16,4,40,128]{3,2,1,0:T(8,128)(2,1)S(1)}, u32[]{:S(2)}, u32[]{:S(2)}) async-start(bf16[16,4,40,128]{3,2,1,0:T(8,128)(2,1)} %join_cores.1), calls=%async_computation.1 | async-start | bytes 1310720 | tf_op jit(solution)/shard_map/all_to_all | solution.py:376
  48.1 0.0 copy-done
  48.1 0.0 copy-done.1
  48.1 0.1 new_tokens.1
  48.2 13.4 %all-to-all-done.1.parts_ref = bf16[16,4,40,128]{3,2,1,0:T(8,128)(2,1)S(1)} async-done(((bf16[16,4,40,128]{3,2,1,0:T(8,128)(2,1)}), bf16[16,4,40,128]{3,2,1,0:T(8,128)(2,1)S(1)}, u32[]{:S(2)}, u32[]{:S(2)}) %all-to-all-start.1) | async-done | bytes 655392 | tf_op jit(solution)/shard_map/all_to_all | solution.py:376
  61.5 1.0 %join_plane.1 = (bf16[40,128]{1,0:T(8,128)(2,1)S(1)}, bf16[40,128]{1,0:T(8,128)(2,1)S(1)}, bf16[40,128]{1,0:T(8,128)(2,1)S(1)}, bf16[40,128]{1,0:T(8,128)(2,1)S(1)}) custom-call(bf16[16,4,40,128]{3,2,1,0:T(8,128)(2,1)S(1)} %all-to-all-done.1.parts_ref), custom_call_target="tpu_custom_call" | custom-call | tf_op jit(solution)/shard_map/join_plane/pallas_call | solution.py:297
  62.6 0.1 collective-permute-start.5
  62.7 2.1 %collective-permute-start.6 = (bf16[40,128]{1,0:T(8,128)(2,1)S(1)}, bf16[40,128]{1,0:T(8,128)(2,1)S(1)}, u32[]{:S(2)}, u32[]{:S(2)}) collective-permute-start(bf16[40,128]{1,0:T(8,128)(2,1)S(1)} %get-tuple-element.39), channel_id=1, source_target_pairs={{0,64},{32,96},{64,0},{96,32},{1,65},{33,97},{65,1},{97,33},{2,66}... | collective-permute-start | bytes 30728 | tf_op jit(solution)/shard_map/ppermute | solution.py:395
  64.7 2.2 %collective-permute-start.7 = (bf16[40,128]{1,0:T(8,128)(2,1)S(1)}, bf16[40,128]{1,0:T(8,128)(2,1)S(1)}, u32[]{:S(2)}, u32[]{:S(2)}) collective-permute-start(bf16[40,128]{1,0:T(8,128)(2,1)S(1)} %get-tuple-element.40), channel_id=1, source_target_pairs={{0,96},{32,0},{64,32},{96,64},{1,97},{33,1},{65,33},{97,65},{2,98}... | collective-permute-start | bytes 30728 | tf_op jit(solution)/shard_map/ppermute | solution.py:395
  66.9 0.6 collective-permute-done.5.refs_1_
  67.5 0.4 collective-permute-done.6.refs_2_
  67.9 0.6 collective-permute-done.7.refs_3_
  68.5 0.8 %merge.1 = bf16[4,2,512]{2,1,0:T(2,128)(2,1)} custom-call(bf16[40,128]{1,0:T(8,128)(2,1)S(1)} %get-tuple-element.37.refs_0_, bf16[40,128]{1,0:T(8,128)(2,1)S(1)} %collective-permute-done.5.refs_1_, bf16[40,128]{1,0:T(8,128)(2,1)S(1)} %collective-permute-done.6.refs_2_, bf16[40,128]{1,0:T(8,128)(2,1)S(1)} %collective-permute-done.7.refs_3_, ...), custom_call_target="tpu_custom_call" | custom-call | tf_op jit(solution)/shard_map/merge/pallas_call | solution.py:364
Async XLA Ops:
  0.7 4.8 %collective-permute-start.2 = (bf16[32,128]{1,0:T(8,128)(2,1)S(1)}, bf16[32,128]{1,0:T(8,128)(2,1)S(1)}, u32[]{:S(2)}, u32[]{:S(2)}) collective-permute-start(bf16[32,128]{1,0:T(8,128)(2,1)S(1)} %gather_rows.1.refs_0_), channel_id=1, source_target_pairs={{0,96},{32,0},{64,32},{96,64},{1,97},{33,1},{65,33},{97,65},{2,98}... | collective-permute-start | bytes 24584 | tf_op jit(solution)/shard_map/ppermute | solution.py:395
  3.9 5.2 %collective-permute-start.1 = (bf16[32,128]{1,0:T(8,128)(2,1)S(1)}, bf16[32,128]{1,0:T(8,128)(2,1)S(1)}, u32[]{:S(2)}, u32[]{:S(2)}) collective-permute-start(bf16[32,128]{1,0:T(8,128)(2,1)S(1)} %gather_rows.1.refs_0_), channel_id=1, source_target_pairs={{0,64},{32,96},{64,0},{96,32},{1,65},{33,97},{65,1},{97,33},{2,66}... | collective-permute-start | bytes 24584 | tf_op jit(solution)/shard_map/ppermute | solution.py:395
  4.5 4.9 %collective-permute-start = (bf16[32,128]{1,0:T(8,128)(2,1)S(1)}, bf16[32,128]{1,0:T(8,128)(2,1)S(1)}, u32[]{:S(2)}, u32[]{:S(2)}) collective-permute-start(bf16[32,128]{1,0:T(8,128)(2,1)S(1)} %gather_rows.1.refs_0_), channel_id=1, source_target_pairs={{0,32},{32,64},{64,96},{96,0},{1,33},{33,65},{65,97},{97,1},{2,34}... | collective-permute-start | bytes 24584 | tf_op jit(solution)/shard_map/ppermute | solution.py:395
  10.2 18.0 %all-to-all-start = ((bf16[16,4,32,128]{3,2,1,0:T(8,128)(2,1)}), bf16[16,4,32,128]{3,2,1,0:T(8,128)(2,1)S(1)}, u32[]{:S(2)}, u32[]{:S(2)}) async-start(bf16[16,4,32,128]{3,2,1,0:T(8,128)(2,1)} %place.1), calls=%async_computation | async-start | bytes 1048576 | tf_op jit(solution)/shard_map/all_to_all | solution.py:376
  18.1 0.7 copy-start.2
  18.8 0.7 copy-start.3
  28.2 1.9 %collective-permute-start.3 = (bf16[16,4,32,128]{3,2,1,0:T(8,128)(2,1)S(1)}, bf16[16,4,32,128]{3,2,1,0:T(8,128)(2,1)S(1)}, u32[]{:S(2)}, u32[]{:S(2)}) collective-permute-start(bf16[16,4,32,128]{3,2,1,0:T(8,128)(2,1)S(1)} %all-to-all-done.refs_0_), channel_id=1, source_target_pairs={{0,16},{16,0},{1,17},{17,1},{2,18},{18,2},{3,19},{19,3},{4,20},{20... | collective-permute-start | bytes 1572872 | tf_op jit(solution)/shard_map/ppermute | solution.py:404
  40.3 7.8 %copy-start = (bf16[4,2,2,1024]{3,2,1,0:T(2,128)(2,1)S(1)}, bf16[4,2,2,1024]{3,2,1,0:T(2,128)(2,1)}, u32[]{:S(2)}) copy-start(bf16[4,2,2,1024]{3,2,1,0:T(2,128)(2,1)} %new_ref) | copy-start | bytes 98308
  40.3 7.8 %copy-start.1 = (bf16[4,2,512]{2,1,0:T(2,128)(2,1)S(1)}, bf16[4,2,512]{2,1,0:T(2,128)(2,1)}, u32[]{:S(2)}) copy-start(bf16[4,2,512]{2,1,0:T(2,128)(2,1)} %q_ref.2) | copy-start | bytes 24580
  40.3 2.2 %collective-permute-start.4 = (bf16[16,4,40,128]{3,2,1,0:T(8,128)(2,1)S(1)}, bf16[16,4,40,128]{3,2,1,0:T(8,128)(2,1)S(1)}, u32[]{:S(2)}, u32[]{:S(2)}) collective-permute-start(bf16[16,4,40,128]{3,2,1,0:T(8,128)(2,1)S(1)} %get-tuple-element.30), channel_id=1, source_target_pairs={{0,16},{16,0},{1,17},{17,1},{2,18},{18,2},{3,19},{19,3},{4,20},{20... | collective-permute-start | bytes 1966088 | tf_op jit(solution)/shard_map/ppermute | solution.py:408
  44.5 17.1 %all-to-all-start.1 = ((bf16[16,4,40,128]{3,2,1,0:T(8,128)(2,1)}), bf16[16,4,40,128]{3,2,1,0:T(8,128)(2,1)S(1)}, u32[]{:S(2)}, u32[]{:S(2)}) async-start(bf16[16,4,40,128]{3,2,1,0:T(8,128)(2,1)} %join_cores.1), calls=%async_computation.1 | async-start | bytes 1310720 | tf_op jit(solution)/shard_map/all_to_all | solution.py:376
  62.6 5.0 %collective-permute-start.5 = (bf16[40,128]{1,0:T(8,128)(2,1)S(1)}, bf16[40,128]{1,0:T(8,128)(2,1)S(1)}, u32[]{:S(2)}, u32[]{:S(2)}) collective-permute-start(bf16[40,128]{1,0:T(8,128)(2,1)S(1)} %get-tuple-element.38), channel_id=1, source_target_pairs={{0,32},{32,64},{64,96},{96,0},{1,33},{33,65},{65,97},{97,1},{2,34}... | collective-permute-start | bytes 30728 | tf_op jit(solution)/shard_map/ppermute | solution.py:395
  62.7 5.3 %collective-permute-start.6 = (bf16[40,128]{1,0:T(8,128)(2,1)S(1)}, bf16[40,128]{1,0:T(8,128)(2,1)S(1)}, u32[]{:S(2)}, u32[]{:S(2)}) collective-permute-start(bf16[40,128]{1,0:T(8,128)(2,1)S(1)} %get-tuple-element.39), channel_id=1, source_target_pairs={{0,64},{32,96},{64,0},{96,32},{1,65},{33,97},{65,1},{97,33},{2,66}... | collective-permute-start | bytes 30728 | tf_op jit(solution)/shard_map/ppermute | solution.py:395
  64.7 3.7 %collective-permute-start.7 = (bf16[40,128]{1,0:T(8,128)(2,1)S(1)}, bf16[40,128]{1,0:T(8,128)(2,1)S(1)}, u32[]{:S(2)}, u32[]{:S(2)}) collective-permute-start(bf16[40,128]{1,0:T(8,128)(2,1)S(1)} %get-tuple-element.40), channel_id=1, source_target_pairs={{0,96},{32,0},{64,32},{96,64},{1,97},{33,1},{65,33},{97,65},{2,98}... | collective-permute-start | bytes 30728 | tf_op jit(solution)/shard_map/ppermute | solution.py:395

commit v5 on v3

--- a/solution.py
+++ b/solution.py
@@ -81,7 +81,7 @@
         out_shape=jax.ShapeDtypeStruct((copies, queries.size // HEAD, HEAD), jnp.bfloat16),
         compiler_params=PARAMS,
         name="spread",
-    )(queries)
+    )(pltpu.with_memory_space_constraint(queries, pltpu.HBM))
 
 
 def locate_kernel(slot_ref, length_ref, info, *, span):
@@ -113,117 +113,122 @@
     )(row_slot, lengths)
 
 
-def attend_kernel(info, *refs, heads, chunk):
-    near_ref, far_ref, k_ref, v_ref, sk_ref, sv_ref, near_out, far_out = refs[:8]
-    q_ref, own_top, own_acc = refs[8:]
+def attend_kernel(info, near_ref, far_ref, *refs, heads):
+    sources, (near_out, far_out), held = refs[:4], refs[4:6], refs[6:10]
+    q_ref, own_top, own_acc, sems = refs[10:]
+    k_ref, v_ref, sk_ref, sv_ref = held
     near, _, rows, _ = near_ref.shape
-    pieces, _, halves, tiles = q_ref.shape[:4]
+    _, _, halves, tiles = q_ref.shape[:4]
     numerators = tiles * 8
-    per_chunk = chunk // rows
-    length = k_ref.shape[0]
-    slots, span, _ = sk_ref.shape
+    chunk = near * rows
+    length = k_ref.shape[1]
+    _, slots, span, _ = sk_ref.shape
     ones = jnp.ones((length, HEAD), jnp.bfloat16)
 
-    @pl.when(pl.program_id(0) == 0)
-    def _():
-        own_top[...] = jnp.full(own_top.shape, LOWEST, jnp.float32)
-        own_acc[...] = jnp.zeros(own_acc.shape, jnp.float32)
-
-    def cut(i):
-        return slice(i * HEAD, (i + 1) * HEAD)
-
-    def scored(i, c):
-        g = c * per_chunk
-        ref = near_ref if g < near else far_ref
-        q = ref[g % near : g % near + per_chunk, i].reshape(chunk, HEAD)
-        return dot(q, k_ref[:, cut(i)], NT)
-
-    items = [(i, c) for i in range(heads) for c in range(pieces // per_chunk)]
-    scores = scored(*items[0])
-
-    held = [near_ref[...].astype(jnp.float32), far_ref[...].astype(jnp.float32)]
-    for n, x in enumerate(held):
-        q_ref[n * near : (n + 1) * near] = x.reshape((near,) + q_ref.shape[1:])
+    def copy(n, k):
+        start = k * HEAD if isinstance(k, int) else pl.multiple_of(k * HEAD, HEAD)
+        at = pl.ds(start, HEAD)
+        part = sources[n].at[:, at] if n < 2 else sources[n].at[:, :, at]
+        return pltpu.make_async_copy(part, held[n].at[k], sems.at[n, k])
+
+    for k in range(KVH):
+        for n in range(4):
+            copy(n, k).start()
+
+    own_top[...] = jnp.full(own_top.shape, LOWEST, jnp.float32)
+    own_acc[...] = jnp.zeros(own_acc.shape, jnp.float32)
     position = iota((halves * 8, span), 1)
-    found = []
-    for j in range(slots):
-        group, row, live = info[j], info[slots + j], info[2 * slots + j]
+
+    def work(first):
         for i in range(heads):
-            q = q_ref[group, i, :, row].reshape(halves * 8, HEAD).astype(jnp.bfloat16)
-            own = dot(q, sk_ref[j, :, cut(i)], NT) * SCALE
-            own = jnp.where(position < live, own, LOWEST)
-            peak = jnp.max(own, axis=1, keepdims=True)
-            peak = jnp.broadcast_to(as_bf16(peak), (halves * 8, HEAD))
-            shift = jnp.concatenate([peak] * (span // HEAD), axis=1)
-            weights = jnp.exp2(own - shift).astype(jnp.bfloat16)
-            values = jnp.concatenate([sv_ref[j, :, cut(i)], ones[:span]], axis=1)
-            found.append((group, i, row, peak, dot(weights, values, NN)))
-    for group, i, row, peak, summed in found:
-        own_top[group, i, :, row] = peak.reshape(halves, 8, HEAD)
-        own_acc[group, i, :, row] = summed.reshape(halves, 8, 2 * HEAD)
-
-    for number, (i, c) in enumerate(items):
-        later = scored(*items[number + 1]) if number + 1 < len(items) else None
-        peak = jnp.max(scores, axis=1, keepdims=True) * SCALE
-        peak = jnp.broadcast_to(as_bf16(peak), (chunk, HEAD))
-        shift = jnp.concatenate([peak] * (length // HEAD), axis=1)
-        weights = jnp.exp2(scores * SCALE - shift).astype(jnp.bfloat16)
-        values = jnp.concatenate([v_ref[:, cut(i)], ones], axis=1)
-        summed = dot(weights, values, NN)
-        at = slice(c * per_chunk, (c + 1) * per_chunk)
-        own = own_top[at, i].reshape(chunk, HEAD)
-        carried = own_acc[at, i].reshape(chunk, 2 * HEAD)
-        top = jnp.maximum(peak, own)
-        keep, add = jnp.exp2(peak - top), jnp.exp2(own - top)
-        total = summed[:, HEAD:] * keep + carried[:, HEAD:] * add
-        numerator = (summed[:, :HEAD] * keep + carried[:, :HEAD] * add).astype(jnp.bfloat16)
-        results = []
-        for b in range(chunk // numerators):
-            low = b * numerators
-            parts = [slice(low + 8 * a, low + 8 * a + 8) for a in range(tiles)]
-            tail = pack([top[p] for p in parts], [total[p] for p in parts])
-            results.append((numerator[low : low + numerators], tail))
-        for b, (block, tail) in enumerate(results):
-            g = c * per_chunk + b // halves
-            out_ref = (near_out if g < near else far_out).at[g % near, i * halves + b % halves]
-            out_ref[:numerators] = block
-            out_ref[numerators:] = tail
-        scores = later
-
-
-def attend(info, near, far, keys, values, suffix_keys, suffix_values, heads, chunk):
+            for n in range(4):
+                copy(n, first + i).wait()
+
+        def scored(i, side):
+            q = (near_ref, far_ref)[side][:, first + i].reshape(chunk, HEAD)
+            return dot(q, k_ref[first + i], NT)
+
+        items = [(i, side) for i in range(heads) for side in range(2)]
+        scores = scored(*items[0])
+
+        for i in range(heads):
+            for side, ref in enumerate((near_ref, far_ref)):
+                x = ref[:, first + i].astype(jnp.float32)
+                q_ref[side * near : (side + 1) * near, i] = x.reshape((near,) + q_ref.shape[2:])
+        found = []
+        for j in range(slots):
+            group, row, live = info[j], info[slots + j], info[2 * slots + j]
+            for i in range(heads):
+                q = q_ref[group, i, :, row].reshape(halves * 8, HEAD).astype(jnp.bfloat16)
+                own = dot(q, sk_ref[first + i, j], NT) * SCALE
+                own = jnp.where(position < live, own, LOWEST)
+                peak = jnp.max(own, axis=1, keepdims=True)
+                peak = jnp.broadcast_to(as_bf16(peak), (halves * 8, HEAD))
+                shift = jnp.concatenate([peak] * (span // HEAD), axis=1)
+                weights = jnp.exp2(own - shift).astype(jnp.bfloat16)
+                values = jnp.concatenate([sv_ref[first + i, j], ones[:span]], axis=1)
+                found.append((group, i, row, peak, dot(weights, values, NN)))
+        for group, i, row, peak, summed in found:
+            own_top[group, i, :, row] = peak.reshape(halves, 8, HEAD)
+            own_acc[group, i, :, row] = summed.reshape(halves, 8, 2 * HEAD)
+
+        for number, (i, side) in enumerate(items):
+            later = scored(*items[number + 1]) if number + 1 < len(items) else None
+            peak = jnp.max(scores, axis=1, keepdims=True) * SCALE
+            peak = jnp.broadcast_to(as_bf16(peak), (chunk, HEAD))
+            shift = jnp.concatenate([peak] * (length // HEAD), axis=1)
+            weights = jnp.exp2(scores * SCALE - shift).astype(jnp.bfloat16)
+            values = jnp.concatenate([v_ref[first + i], ones], axis=1)
+            summed = dot(weights, values, NN)
+            at = slice(side * near, (side + 1) * near)
+            own = own_top[at, i].reshape(chunk, HEAD)
+            carried = own_acc[at, i].reshape(chunk, 2 * HEAD)
+            top = jnp.maximum(peak, own)
+            keep, add = jnp.exp2(peak - top), jnp.exp2(own - top)
+            total = summed[:, HEAD:] * keep + carried[:, HEAD:] * add
+            numerator = (summed[:, :HEAD] * keep + carried[:, :HEAD] * add).astype(jnp.bfloat16)
+            results = []
+            for b in range(chunk // numerators):
+                low = b * numerators
+                parts = [slice(low + 8 * a, low + 8 * a + 8) for a in range(tiles)]
+                tail = pack([top[p] for p in parts], [total[p] for p in parts])
+                results.append((numerator[low : low + numerators], tail))
+            for b, (block, tail) in enumerate(results):
+                member = (first + i) * halves + b % halves
+                out_ref = (near_out, far_out)[side].at[b // halves, member]
+                out_ref[:numerators] = block
+                out_ref[numerators:] = tail
+            scores = later
+
+    @pl.loop(0, KVH // heads)
+    def _(pair):
+        work(pair * heads)
+
+
+def attend(info, near, far, keys, values, suffix_keys, suffix_values, heads):
     layers, members, numerators, _ = near.shape
     halves = members // KVH
-    rows = halves * numerators
-    near, far = (x.reshape(layers, KVH, rows, HEAD) for x in (near, far))
-    length = keys.shape[0]
-    slots, span, _ = suffix_keys.shape
-    in_hbm = [
-        pltpu.with_memory_space_constraint(x, pltpu.HBM)
-        for x in (keys, values, suffix_keys, suffix_values)
-    ]
-    wide = heads * HEAD
-    by_head = pl.BlockSpec((layers, heads, rows, HEAD), lambda k: (0, k, 0, 0))
-    prompt = pl.BlockSpec((length, wide), lambda k: (0, k))
-    own = pl.BlockSpec((slots, span, wide), lambda k: (0, 0, k))
-    out_block = (layers, heads * halves, numerators + TAIL, HEAD)
-    out_spec = pl.BlockSpec(out_block, lambda k: (0, k, 0, 0))
+    near, far = (x.reshape(layers, KVH, halves * numerators, HEAD) for x in (near, far))
+    arrays = (keys, values, suffix_keys, suffix_values)
+    vmem = pl.BlockSpec(memory_space=pltpu.VMEM)
     out = jax.ShapeDtypeStruct((layers, members, numerators + TAIL, HEAD), jnp.bfloat16)
     tiled = (2 * layers, heads, halves, numerators // 8, 8)
     return pl.pallas_call(
-        functools.partial(attend_kernel, heads=heads, chunk=chunk),
-        grid=(KVH // heads,),
-        in_specs=[pl.BlockSpec(memory_space=pltpu.SMEM), by_head, by_head, prompt, prompt, own, own],
-        out_specs=[out_spec, out_spec],
+        functools.partial(attend_kernel, heads=heads),
+        in_specs=[pl.BlockSpec(memory_space=pltpu.SMEM), vmem, vmem]
+        + [pl.BlockSpec(memory_space=pl.ANY)] * len(arrays),
+        out_specs=[vmem, vmem],
         out_shape=[out, out],
-        scratch_shapes=[
+        scratch_shapes=[pltpu.VMEM((KVH,) + x.shape[:-1] + (HEAD,), x.dtype) for x in arrays]
+        + [
             pltpu.VMEM(tiled + (HEAD,), jnp.float32),
             pltpu.VMEM(tiled + (HEAD,), jnp.float32),
             pltpu.VMEM(tiled + (2 * HEAD,), jnp.float32),
+            pltpu.SemaphoreType.DMA((len(arrays), KVH)),
         ],
         compiler_params=PARAMS,
         name="attend",
-    )(info, near, far, *in_hbm)
+    )(info, near, far, *[pltpu.with_memory_space_constraint(x, pltpu.HBM) for x in arrays])
 
 
 def join_parts(parts):
@@ -250,19 +255,32 @@
     return joined
 
 
-def join_cores_kernel(a_ref, b_ref, out_ref):
+def join_cores_kernel(a_ref, b_ref, out_ref, held, sems):
     layers, members, rows, _ = a_ref.shape
+    copies = [
+        pltpu.make_async_copy(held.at[y], out_ref.at[y], sems.at[y]) for y in range(layers)
+    ]
     for y in range(layers):
         parts = [[ref[y, m] for m in range(members)] for ref in (a_ref, b_ref)]
         for m, (block, tail) in enumerate(join_parts(parts)):
-            out_ref[y, m, : rows - TAIL] = block
-            out_ref[y, m, rows - TAIL :] = tail
+            held[y, m, : rows - TAIL] = block
+            held[y, m, rows - TAIL :] = tail
+        copies[y].start()
+    for copy in copies:
+        copy.wait()
 
 
 def join_cores(a, b):
+    vmem = pl.BlockSpec(memory_space=pltpu.VMEM)
     return pl.pallas_call(
         join_cores_kernel,
+        in_specs=[vmem, vmem],
+        out_specs=pl.BlockSpec(memory_space=pl.ANY),
         out_shape=jax.ShapeDtypeStruct(a.shape, a.dtype),
+        scratch_shapes=[
+            pltpu.VMEM(a.shape, a.dtype),
+            pltpu.SemaphoreType.DMA((a.shape[0],)),
+        ],
         compiler_params=PARAMS,
         name="join_cores",
     )(a, b)
@@ -367,7 +385,7 @@
     near = near.reshape((layers, members) + near.shape[1:])
     far = lax.ppermute(near, "core", swap)
     near_part, far_part = attend(
-        info, near, far, prefix_keys, prefix_values, suffix_keys, suffix_values, 2, 128
+        info, near, far, prefix_keys, prefix_values, suffix_keys, suffix_values, 2
     )
     joined = join_cores(near_part, lax.ppermute(far_part, "core", swap))
     joined, queries, new_kv = lax.optimization_barrier((joined, queries, new_kv))

time: 64.5 us -> 64.5 us (level)
  Pallas kernels: 15.6 us -> 16.3 us
  local copies, waits for them, and re-layouts: 2.01 us -> 1.32 us
    unnamed x10 -> x8, local copies, waits for them, and re-layouts: 2.01 us -> 1.32 us
    pallas_call x1, Pallas kernels: 0.85 us -> 1.53 us  [spread(): pl.pallas_call(spread_kernel, out_shape=jax.ShapeDtypeStruct((copies, que...]
where the time goes in v5:
time: 64.5 us; the launch traced here: 64.1 us
  waiting for transfers between devices  30 us (47%)
  starting transfers between devices  16.4 us (25%)
  Pallas kernels  16.3 us (25%)
  local copies, waits for them, and re-layouts  1.32 us (2%)
    all_to_all x2, waiting for transfers between devices, exchange(): return lax.all_to_all(x, axes, split_axis=0, concat_axis=0, tiled=True)  26.1 us
    all_to_all x2, starting transfers between devices, exchange(): return lax.all_to_all(x, axes, split_axis=0, concat_axis=0, tiled=True)  16.2 us
    pallas_call x1, Pallas kernels, attend(): pl.pallas_call(functools.partial(attend_kernel, heads=heads), in_specs=[p...  10.4 us
    ppermute x1, waiting for transfers between devices, per_device(): joined = join_cores(near_part, lax.ppermute(far_part, 'core', swap))  1.96 us
    ppermute x1, waiting for transfers between devices, per_device(): far = lax.ppermute(near, 'core', swap)  1.91 us
    pallas_call x1, Pallas kernels, join_cores(): pl.pallas_call(join_cores_kernel, in_specs=[vmem, vmem], out_specs=pl.Blo...  1.81 us
    pallas_call x1, Pallas kernels, spread(): pl.pallas_call(spread_kernel, out_shape=jax.ShapeDtypeStruct((copies, que...  1.53 us
    unnamed x8, local copies, waits for them, and re-layouts  1.32 us
  transfers between devices with their start and end apart: 4, of which 4 were waited for; matrix products, arithmetic and copies ran while one was open for 0% of the time, Pallas kernels for 2%

profile of v5, /device:TPU:0, one launch (start us, length us, event | category | flops | bytes accessed | tf_op | source)
XLA Modules:
  0.0 64.1 jit_solution(15227609644154102791)
XLA Ops:
  0.0 1.5 %spread.1 = bf16[64,32,128]{2,1,0:T(8,128)(2,1)} custom-call(bf16[4,2,512]{2,1,0:T(2,128)(2,1)} %q_ref.2), custom_call_target="tpu_custom_call" | custom-call | tf_op jit(solution)/shard_map/spread/pallas_call | solution.py:79
  1.5 11.5 %all-to-all-start = ((bf16[64,32,128]{2,1,0:T(8,128)(2,1)}), bf16[64,32,128]{2,1,0:T(8,128)(2,1)S(1)}, u32[]{:S(2)}, u32[]{:S(2)}) async-start(bf16[64,32,128]{2,1,0:T(8,128)(2,1)} %spread.1), calls=%async_computation | async-start | bytes 1048576 | tf_op jit(solution)/shard_map/all_to_all | solution.py:359
  13.0 0.0 copy-start.2
  13.0 0.6 %copy-done.2 = s32[32]{0:T(128)S(1)} copy-done((s32[32]{0:T(128)S(1)}, s32[32]{0:T(128)}, u32[]{:S(2)}) %copy-start.2) | copy-done | bytes 152
  13.7 0.0 copy-start.3
  13.7 0.7 %copy-done.3 = s32[4]{0:T(128)S(1)} copy-done((s32[4]{0:T(128)S(1)}, s32[4]{0:T(128)}, u32[]{:S(2)}) %copy-start.3) | copy-done | bytes 40
  14.3 1.3 %locate.1.info = s32[12]{0:T(128)S(1)} custom-call(s32[32]{0:T(128)S(1)} %copy-done.2, s32[4]{0:T(128)S(1)} %copy-done.3), custom_call_target="tpu_custom_call" | custom-call | tf_op jit(solution)/shard_map/locate/pallas_call | solution.py:106
  15.6 10.9 %all-to-all-done = bf16[64,32,128]{2,1,0:T(8,128)(2,1)S(1)} async-done(((bf16[64,32,128]{2,1,0:T(8,128)(2,1)}), bf16[64,32,128]{2,1,0:T(8,128)(2,1)S(1)}, u32[]{:S(2)}, u32[]{:S(2)}) %all-to-all-start) | async-done | bytes 524320 | tf_op jit(solution)/shard_map/all_to_all | solution.py:359
  26.5 0.0 collective-permute-start
  26.5 1.9 %collective-permute-done = bf16[4,16,32,128]{3,2,1,0:T(8,128)(2,1)S(1)} collective-permute-done((bf16[4,16,32,128]{3,2,1,0:T(8,128)(2,1)S(1)}, bf16[4,16,32,128]{3,2,1,0:T(8,128)(2,1)S(1)}, u32[]{:S(2)}, u32[]{:S(2)}) %collective-permute-start) | collective-permute-done | bytes 524320 | tf_op jit(solution)/shard_map/ppermute | solution.py:386
  28.4 10.4 %attend.1 = (bf16[4,16,40,128]{3,2,1,0:T(8,128)(2,1)S(1)}, bf16[4,16,40,128]{3,2,1,0:T(8,128)(2,1)S(1)}) custom-call(s32[12]{0:T(128)S(1)} %locate.1.info, bf16[4,8,64,128]{3,2,1,0:T(8,128)(2,1)S(1)} %bitcast.5, bf16[4,8,64,128]{3,2,1,0:T(8,128)(2,1)S(1)} %bitcast.6, bf16[1024,1024]{1,0:T(8,128)(2,1)} %refs_0_.1, bf16[1024,1024]{1,0:T(8,128)(2,1)} %refs_1_.1, ...), custom_call_target="tpu_custom_call" | custom-call | tf_op jit(solution)/shard_map/attend/pallas_call | solution.py:216
  38.8 0.0 copy-start
  38.8 0.0 copy-start.1
  38.8 0.2 collective-permute-start.1
  39.1 2.0 %collective-permute-done.1.b_ref = bf16[4,16,40,128]{3,2,1,0:T(8,128)(2,1)S(1)} collective-permute-done((bf16[4,16,40,128]{3,2,1,0:T(8,128)(2,1)S(1)}, bf16[4,16,40,128]{3,2,1,0:T(8,128)(2,1)S(1)}, u32[]{:S(2)}, u32[]{:S(2)}) %collective-permute-start.1) | collective-permute-done | bytes 655392 | tf_op jit(solution)/shard_map/ppermute | solution.py:390
  41.0 1.8 %join_cores.1 = bf16[4,16,40,128]{3,2,1,0:T(8,128)(2,1)} custom-call(bf16[4,16,40,128]{3,2,1,0:T(8,128)(2,1)S(1)} %get-tuple-element.22.a_ref, bf16[4,16,40,128]{3,2,1,0:T(8,128)(2,1)S(1)} %collective-permute-done.1.b_ref), custom_call_target="tpu_custom_call" | custom-call | tf_op jit(solution)/shard_map/join_cores/pallas_call | solution.py:275
  42.8 4.7 %all-to-all-start.1 = ((bf16[64,40,128]{2,1,0:T(8,128)(2,1)}), bf16[64,40,128]{2,1,0:T(8,128)(2,1)S(1)}, u32[]{:S(2)}, u32[]{:S(2)}) async-start(bf16[64,40,128]{2,1,0:T(8,128)(2,1)} %bitcast.3), calls=%async_computation.1 | async-start | bytes 1310720 | tf_op jit(solution)/shard_map/all_to_all | solution.py:359
  47.5 0.0 copy-done
  47.5 0.0 copy-done.1
  47.5 0.1 new_tokens.1
  47.6 15.3 %all-to-all-done.1.parts_ref = bf16[64,40,128]{2,1,0:T(8,128)(2,1)S(1)} async-done(((bf16[64,40,128]{2,1,0:T(8,128)(2,1)}), bf16[64,40,128]{2,1,0:T(8,128)(2,1)S(1)}, u32[]{:S(2)}, u32[]{:S(2)}) %all-to-all-start.1) | async-done | bytes 655392 | tf_op jit(solution)/shard_map/all_to_all | solution.py:359
  62.9 1.2 %merge.1 = bf16[4,2,512]{2,1,0:T(2,128)(2,1)} custom-call(bf16[64,40,128]{2,1,0:T(8,128)(2,1)S(1)} %all-to-all-done.1.parts_ref, f32[2,4,8,128]{3,2,1,0:T(8,128)S(1)} %get-tuple-element.27.score_ref, f32[2,4,8,128]{3,2,1,0:T(8,128)S(1)} %get-tuple-element.28.value_ref), custom_call_target="tpu_custom_call" | custom-call | tf_op jit(solution)/shard_map/merge/pallas_call | solution.py:347
Async XLA Ops:
  1.5 25.0 %all-to-all-start = ((bf16[64,32,128]{2,1,0:T(8,128)(2,1)}), bf16[64,32,128]{2,1,0:T(8,128)(2,1)S(1)}, u32[]{:S(2)}, u32[]{:S(2)}) async-start(bf16[64,32,128]{2,1,0:T(8,128)(2,1)} %spread.1), calls=%async_computation | async-start | bytes 1048576 | tf_op jit(solution)/shard_map/all_to_all | solution.py:359
  13.0 0.7 %copy-start.2 = (s32[32]{0:T(128)S(1)}, s32[32]{0:T(128)}, u32[]{:S(2)}) copy-start(s32[32]{0:T(128)} %slot_ref) | copy-start | bytes 388
  13.7 0.7 %copy-start.3 = (s32[4]{0:T(128)S(1)}, s32[4]{0:T(128)}, u32[]{:S(2)}) copy-start(s32[4]{0:T(128)} %length_ref) | copy-start | bytes 52
  26.5 1.9 %collective-permute-start = (bf16[4,16,32,128]{3,2,1,0:T(8,128)(2,1)S(1)}, bf16[4,16,32,128]{3,2,1,0:T(8,128)(2,1)S(1)}, u32[]{:S(2)}, u32[]{:S(2)}) collective-permute-start(bf16[4,16,32,128]{3,2,1,0:T(8,128)(2,1)S(1)} %bitcast.4), channel_id=1, source_target_pairs={{0,16},{16,0},{1,17},{17,1},{2,18},{18,2},{3,19},{19,3},{4,20},{20... | collective-permute-start | bytes 1572872 | tf_op jit(solution)/shard_map/ppermute | solution.py:386
  38.8 8.7 %copy-start = (bf16[4,2,512]{2,1,0:T(2,128)(2,1)S(1)}, bf16[4,2,512]{2,1,0:T(2,128)(2,1)}, u32[]{:S(2)}) copy-start(bf16[4,2,512]{2,1,0:T(2,128)(2,1)} %q_ref.2) | copy-start | bytes 24580
  38.8 8.7 %copy-start.1 = (bf16[4,2,2,1024]{3,2,1,0:T(2,128)(2,1)S(1)}, bf16[4,2,2,1024]{3,2,1,0:T(2,128)(2,1)}, u32[]{:S(2)}) copy-start(bf16[4,2,2,1024]{3,2,1,0:T(2,128)(2,1)} %new_ref) | copy-start | bytes 98308
  38.8 2.2 %collective-permute-start.1 = (bf16[4,16,40,128]{3,2,1,0:T(8,128)(2,1)S(1)}, bf16[4,16,40,128]{3,2,1,0:T(8,128)(2,1)S(1)}, u32[]{:S(2)}, u32[]{:S(2)}) collective-permute-start(bf16[4,16,40,128]{3,2,1,0:T(8,128)(2,1)S(1)} %get-tuple-element.23), channel_id=1, source_target_pairs={{0,16},{16,0},{1,17},{17,1},{2,18},{18,2},{3,19},{19,3},{4,20},{20... | collective-permute-start | bytes 1966088 | tf_op jit(solution)/shard_map/ppermute | solution.py:390
  42.8 20.1 %all-to-all-start.1 = ((bf16[64,40,128]{2,1,0:T(8,128)(2,1)}), bf16[64,40,128]{2,1,0:T(8,128)(2,1)S(1)}, u32[]{:S(2)}, u32[]{:S(2)}) async-start(bf16[64,40,128]{2,1,0:T(8,128)(2,1)} %bitcast.3), calls=%async_computation.1 | async-start | bytes 1310720 | tf_op jit(solution)/shard_map/all_to_all | solution.py:359

commit v6 on v5

v6 whole, which is shorter than its diff:
```python
import functools
import math

import jax
import jax.numpy as jnp
from jax import lax
from jax.experimental import pallas as pl
from jax.experimental.pallas import tpu as pltpu
from jax.sharding import PartitionSpec as P

H = 64
KVH = 8
HEAD = 128
LOWEST = -(2.0**100)
SCALE = HEAD ** (-0.5) * math.log2(math.e)
TAIL = 8
PARAMS = pltpu.CompilerParams(vmem_limit_bytes=32 << 20)

NT = (((1,), (1,)), ((), ()))
NN = (((1,), (0,)), ((), ()))


def dot(a, b, dims):
    return lax.dot_general(a, b, dims, preferred_element_type=jnp.float32)


def iota(shape, axis):
    return lax.broadcasted_iota(jnp.int32, shape, axis)


def as_bf16(x):
    return x.astype(jnp.bfloat16).astype(jnp.float32)


def columns(x):
    return [x[:, a * HEAD : (a + 1) * HEAD] for a in range(x.shape[1] // HEAD)]


def pack(tops, totals):
    lane = iota((TAIL, HEAD), 1)
    piece = lax.rem(lane, 32) // 8
    packed = None
    for a, (top, total) in enumerate(zip(tops, totals)):
        high = as_bf16(total)
        mixed = jnp.where(piece == 1, high, total - high)
        mixed = jnp.where(piece == 0, top, mixed)
        packed = mixed if a == 0 else jnp.where(lane // 32 == a, mixed, packed)
    return packed.astype(jnp.bfloat16)


def unpack(tails, tiles):
    shape = (HEAD, tiles * HEAD)
    start = iota(shape, 0) - 32 * (iota(shape, 1) // HEAD)
    first = (start == 0).astype(jnp.float32).astype(jnp.bfloat16)
    second = ((start == 8) | (start == 16)).astype(jnp.float32).astype(jnp.bfloat16)
    return dot(tails, first, NN), dot(tails, second, NN)


def combine(tops, totals, numerators):
    upper = functools.reduce(jnp.maximum, tops)
    factors = [jnp.exp2(top - upper) for top in tops]
    total = sum(x * f for x, f in zip(totals, factors))
    return upper, total, sum(x * f for x, f in zip(numerators, factors))


def query_rows(q_ref):
    heads = range(q_ref.shape[2] // HEAD)
    held = [q_ref[r].astype(jnp.float32) for r in range(q_ref.shape[0])]
    return jnp.concatenate([x[:, h * HEAD : (h + 1) * HEAD] for x in held for h in heads], axis=0)


def spread_kernel(q_ref, out_ref):
    block = query_rows(q_ref).astype(jnp.bfloat16)
    for d in range(out_ref.shape[0]):
        out_ref[d] = block


def spread(queries, copies):
    return pl.pallas_call(
        spread_kernel,
        out_shape=jax.ShapeDtypeStruct((copies, queries.size // HEAD, HEAD), jnp.bfloat16),
        compiler_params=PARAMS,
        name="spread",
    )(pltpu.with_memory_space_constraint(queries, pltpu.HBM))


def locate_kernel(slot_ref, *refs, span):
    lengths, info = refs[:-1], refs[-1]
    slots = lengths[0].shape[0]
    cores, layers = lax.axis_size("core"), lax.axis_size("y")
    core = lax.axis_index("core")
    start = (lax.axis_index("z") * lax.axis_size("x") + lax.axis_index("x")) * span
    total = slots * len(lengths)
    for side, length_ref in enumerate(lengths):
        owner = lax.rem(core + side, cores)
        first = (lax.axis_index("y") * cores + owner) * slots
        for j in range(slots):
            row = jnp.int32(0)
            for r in range(slot_ref.shape[0]):
                row = jnp.where(slot_ref[r] == first + j, jnp.int32(r), row)
            group = lax.div(row, slots)
            served = lax.rem(group, cores) == core
            at = side * slots + j
            info[at] = jnp.where(served, lax.div(group, cores), layers)
            info[total + at] = lax.rem(row, slots)
            info[2 * total + at] = jnp.clip(length_ref[j] - start, 0, span)


def locate(row_slot, lengths, span):
    smem = pl.BlockSpec(memory_space=pltpu.SMEM)
    total = sum(x.shape[0] for x in lengths)
    return pl.pallas_call(
        functools.partial(locate_kernel, span=span),
        in_specs=[smem] * (1 + len(lengths)),
        out_specs=smem,
        out_shape=jax.ShapeDtypeStruct((3 * total,), jnp.int32),
        compiler_params=PARAMS,
        name="locate",
    )(row_slot, *lengths)


def attend_kernel(info, near_ref, *refs, sides, heads, chunk):
    count = 4 * sides
    sources, out_ref, held = refs[:count], refs[count], refs[count + 1 : 2 * count + 1]
    block, q_ref, own_top, own_acc, sems, out_sems = refs[2 * count + 1 :]
    layers, _, rows, _ = near_ref.shape
    _, _, halves, tiles = q_ref.shape[:4]
    numerators = tiles * 8
    per_chunk = chunk // rows
    wide = heads * HEAD
    length = sources[0].shape[0]
    slots, span, _ = sources[2].shape
    ones = jnp.ones((length, HEAD), jnp.bfloat16)
    pairs = KVH // heads

    def copy(n, pair):
        start = pair * wide if isinstance(pair, int) else pl.multiple_of(pair * wide, wide)
        at = pl.ds(start, wide)
        part = sources[n].at[:, at] if n % 4 < 2 else sources[n].at[:, :, at]
        return pltpu.make_async_copy(part, held[n].at[pair], sems.at[n, pair])

    def send(pair):
        at = pl.ds(pair * heads * halves, heads * halves)
        return pltpu.make_async_copy(block.at[:, at], out_ref.at[:, at], out_sems.at[pair])

    for pair in range(pairs):
        for n in range(count):
            copy(n, pair).start()

    own_top[...] = jnp.full(own_top.shape, LOWEST, jnp.float32)
    own_acc[...] = jnp.zeros(own_acc.shape, jnp.float32)
    position = iota((halves * 8, span), 1)

    def cut(i):
        return slice(i * HEAD, (i + 1) * HEAD)

    @pl.loop(0, pairs)
    def _(pair):
        for n in range(count):
            copy(n, pair).wait()
        first = pair * heads

        def scored(i, c):
            at = slice(c * per_chunk, (c + 1) * per_chunk)
            q = near_ref[at, first + i].reshape(chunk, HEAD)
            return [dot(q, held[4 * side][pair, :, cut(i)], NT) for side in range(sides)]

        items = [(i, c) for i in range(heads) for c in range(layers // per_chunk)]
        scores = scored(*items[0])

        for i in range(heads):
            x = near_ref[:, first + i].astype(jnp.float32)
            q_ref[:, i] = x.reshape((layers,) + q_ref.shape[2:])
        found = []
        total = sides * slots
        for j in range(total):
            layer, row, live = info[j], info[total + j], info[2 * total + j]
            sk_ref, sv_ref = held[4 * (j // slots) + 2 : 4 * (j // slots) + 4]
            for i in range(heads):
                q = q_ref[jnp.minimum(layer, layers - 1), i, :, row]
                q = q.reshape(halves * 8, HEAD).astype(jnp.bfloat16)
                own = dot(q, sk_ref[pair, j % slots, :, cut(i)], NT) * SCALE
                own = jnp.where(position < live, own, LOWEST)
                peak = jnp.max(own, axis=1, keepdims=True)
                peak = jnp.broadcast_to(as_bf16(peak), (halves * 8, HEAD))
                shift = jnp.concatenate([peak] * (span // HEAD), axis=1)
                weights = jnp.exp2(own - shift).astype(jnp.bfloat16)
                values = sv_ref[pair, j % slots, :, cut(i)]
                values = jnp.concatenate([values, ones[:span]], axis=1)
                found.append((layer, i, row, peak, dot(weights, values, NN)))
        for layer, i, row, peak, summed in found:
            own_top[layer, i, :, row] = peak.reshape(halves, 8, HEAD)
            own_acc[layer, i, :, row] = summed.reshape(halves, 8, 2 * HEAD)

        for number, (i, c) in enumerate(items):
            later = scored(*items[number + 1]) if number + 1 < len(items) else None
            peak = functools.reduce(jnp.maximum, [jnp.max(x, axis=1, keepdims=True) for x in scores])
            peak = jnp.broadcast_to(as_bf16(peak * SCALE), (chunk, HEAD))
            shift = jnp.concatenate([peak] * (length // HEAD), axis=1)
            summed = None
            for side, x in enumerate(scores):
                weights = jnp.exp2(x * SCALE - shift).astype(jnp.bfloat16)
                values = held[4 * side + 1][pair, :, cut(i)]
                part = dot(weights, jnp.concatenate([values, ones], axis=1), NN)
                summed = part if summed is None else summed + part
            at = slice(c * per_chunk, (c + 1) * per_chunk)
            own = own_top[at, i].reshape(chunk, HEAD)
            carried = own_acc[at, i].reshape(chunk, 2 * HEAD)
            top = jnp.maximum(peak, own)
            keep, add = jnp.exp2(peak - top), jnp.exp2(own - top)
            sums = summed[:, HEAD:] * keep + carried[:, HEAD:] * add
            numerator = (summed[:, :HEAD] * keep + carried[:, :HEAD] * add).astype(jnp.bfloat16)
            results = []
            for b in range(chunk // numerators):
                low = b * numerators
                parts = [slice(low + 8 * a, low + 8 * a + 8) for a in range(tiles)]
                tail = pack([top[p] for p in parts], [sums[p] for p in parts])
                results.append((numerator[low : low + numerators], tail))
            for b, (found_block, tail) in enumerate(results):
                to = block.at[c * per_chunk + b // halves, (first + i) * halves + b % halves]
                to[:numerators] = found_block
                to[numerators:] = tail
            scores = later
        send(pair).start()

    for pair in range(pairs):
        send(pair).wait()


def attend(info, near, caches, heads, chunk):
    layers, members, numerators, _ = near.shape
    halves = members // KVH
    near = near.reshape(layers, KVH, halves * numerators, HEAD)
    arrays = [x for cache in caches for x in cache]
    out = jax.ShapeDtypeStruct((layers, members, numerators + TAIL, HEAD), jnp.bfloat16)
    tiled = (heads, halves, numerators // 8, 8)
    anywhere = pl.BlockSpec(memory_space=pl.ANY)
    pairs = KVH // heads
    return pl.pallas_call(
        functools.partial(attend_kernel, sides=len(caches), heads=heads, chunk=chunk),
        in_specs=[
            pl.BlockSpec(memory_space=pltpu.SMEM),
            pl.BlockSpec(memory_space=pltpu.VMEM),
        ]
        + [anywhere] * len(arrays),
        out_specs=anywhere,
        out_shape=out,
        scratch_shapes=[
            pltpu.VMEM((pairs,) + x.shape[:-1] + (heads * HEAD,), x.dtype) for x in arrays
        ]
        + [
            pltpu.VMEM(out.shape, out.dtype),
            pltpu.VMEM((layers,) + tiled + (HEAD,), jnp.float32),
            pltpu.VMEM((layers + 1,) + tiled + (HEAD,), jnp.float32),
            pltpu.VMEM((layers + 1,) + tiled + (2 * HEAD,), jnp.float32),
            pltpu.SemaphoreType.DMA((len(arrays), pairs)),
            pltpu.SemaphoreType.DMA((pairs,)),
        ],
        compiler_params=pltpu.CompilerParams(vmem_limit_bytes=48 << 20),
        name="attend",
    )(info, near, *arrays)


def new_kernel(q_ref, new_ref, score_ref, value_ref):
    rows, steps, width = q_ref.shape
    member = lax.axis_index("z") * lax.axis_size("x") + lax.axis_index("x")
    kv_head = member * (width // HEAD) // (H // KVH)
    at_head = pl.ds(pl.multiple_of(kv_head * HEAD, HEAD), HEAD)
    step = lax.rem(iota((8, HEAD), 0), steps)
    queries = query_rows(q_ref)
    for r in range(rows):
        for u in range(steps):
            key, value = (
                jnp.broadcast_to(new_ref[r, u, n : n + 1, at_head].astype(jnp.float32), (8, HEAD))
                for n in range(2)
            )
            score = jnp.sum(queries[r * 8 : r * 8 + 8] * key, axis=1, keepdims=True) * SCALE
            score_ref[u, r] = jnp.where(step >= u, jnp.broadcast_to(score, (8, HEAD)), LOWEST)
            value_ref[u, r] = value


def new_tokens(queries, new_kv):
    rows, steps, _ = queries.shape
    out = jax.ShapeDtypeStruct((steps, rows, 8, HEAD), jnp.float32)
    return pl.pallas_call(
        new_kernel,
        out_shape=[out, out],
        compiler_params=PARAMS,
        name="new_tokens",
    )(queries, new_kv)


def merge_kernel(parts_ref, score_ref, value_ref, out_ref):
    rows, steps, width = out_ref.shape
    sources, size, _ = parts_ref.shape
    numerators = size - TAIL
    one = jnp.ones((8, HEAD), jnp.float32)
    blocks = [parts_ref[s] for s in range(sources)]
    tails = [x[numerators:].astype(jnp.float32) for x in blocks]
    opened = unpack(jnp.concatenate(tails, axis=0).astype(jnp.bfloat16), rows)
    opened = [columns(x) for x in opened]
    results = []
    for r in range(rows):
        pieces = [slice(s * 8, s * 8 + 8) for s in range(sources)]
        tops = [opened[0][r][p] for p in pieces]
        totals = [opened[1][r][p] for p in pieces]
        sums = [x[r * 8 : r * 8 + 8].astype(jnp.float32) for x in blocks]
        for u in range(steps):
            tops.append(score_ref[u, r])
            totals.append(one)
            sums.append(value_ref[u, r])
        _, total, summed = combine(tops, totals, sums)
        results.append(summed / total)
    for r, result in enumerate(results):
        for h in range(width // HEAD):
            out_ref[r, :, h * HEAD : (h + 1) * HEAD] = result[h * steps : (h + 1) * steps].astype(
                jnp.bfloat16
            )


def merge(parts, scores, values, shape):
    return pl.pallas_call(
        merge_kernel,
        out_shape=jax.ShapeDtypeStruct(shape, jnp.bfloat16),
        compiler_params=PARAMS,
        name="merge",
    )(parts, scores, values)


CHIPS = ("y", "z", "x")


def exchange(x, axes):
    return lax.all_to_all(x, axes, split_axis=0, concat_axis=0, tiled=True)


def per_device(
    queries,
    new_kv,
    prefix_keys,
    prefix_values,
    suffix_keys,
    suffix_values,
    suffix_lengths,
    row_slot,
):
    layers = lax.axis_size("y")
    cores = lax.axis_size("core")
    members = lax.axis_size("z") * lax.axis_size("x")
    chips = layers * members
    swap = [(i, (i + 1) % cores) for i in range(cores)]

    own = (prefix_keys, prefix_values, suffix_keys, suffix_values)
    far = tuple(lax.ppermute(x, "core", swap) for x in own)
    own = tuple(pltpu.with_memory_space_constraint(x, pltpu.HBM) for x in own)
    far_lengths = lax.ppermute(suffix_lengths, "core", swap)

    blocks, row_slot = lax.optimization_barrier((spread(queries, chips), row_slot))
    near = exchange(blocks, CHIPS)
    info = locate(row_slot, (suffix_lengths, far_lengths), suffix_keys.shape[1])
    near, info = lax.optimization_barrier((near, info))
    near = near.reshape((layers, members) + near.shape[1:])
    parts = attend(info, near, (own, far), 2, 128)
    parts, queries, new_kv = lax.optimization_barrier((parts, queries, new_kv))
    received = exchange(parts.reshape((chips,) + parts.shape[2:]), CHIPS)
    scores, values = new_tokens(queries, new_kv)
    return merge(received, scores, values, queries.shape)


def solution(mesh):
    fine = jax.sharding.Mesh(mesh.devices.reshape(4, 2, 4, 4), ("y", "core", "z", "x"))
    grp, seq = ("y", "core"), ("z", "x")
    placed = (
        P(grp, None, seq),
        P(grp, None, None, None),
        P(grp + seq, None),
        P(grp + seq, None),
        P(grp, seq, None),
        P(grp, seq, None),
        P(grp),
        P(),
    )
    return jax.shard_map(
        per_device, mesh=fine, in_specs=placed, out_specs=P(grp, None, seq), check_vma=False
    )
```

time: 64.5 us -> 60.4 us (0.936)
  waiting for transfers between devices: 30 us -> 24.4 us
  starting transfers between devices: 16.4 us -> 17.3 us
  Pallas kernels: 16.3 us -> 17 us
    all_to_all x2, waiting for transfers between devices: 26.1 us -> 23.2 us  [exchange(): return lax.all_to_all(x, axes, split_axis=0, concat_axis=0, tiled=True)]
    ppermute x2 -> x5, waiting for transfers between devices: 3.86 us -> 1.25 us  [the longest x1 1.24 us: per_device(): far_lengths = lax.ppermute(suffix_lengths, 'core', swap)]
    ppermute x2 -> x5, starting transfers between devices: 0.22 us -> 1.11 us  [the longest x4 1.02 us: per_device(): far = tuple((lax.ppermute(x, 'core', swap) for x in own))]
    pallas_call x2 -> x1, Pallas kernels: 12.2 us -> 12.7 us  [attend(): pl.pallas_call(functools.partial(attend_kernel, sides=len(caches), heads=...]
  transfers between devices with their start and end apart: 4 -> 7, of which waited for: 4 -> 3; matrix products, arithmetic and copies ran while one was open for 0% -> 0% of each run, Pallas kernels for 2% -> 5%
where the time goes in v6:
time: 60.4 us; the launch traced here: 60 us
  waiting for transfers between devices  24.4 us (40%)
  starting transfers between devices  17.3 us (29%)
  Pallas kernels  17 us (28%)
  local copies, waits for them, and re-layouts  1.32 us (2%)
    all_to_all x2, waiting for transfers between devices, exchange(): return lax.all_to_all(x, axes, split_axis=0, concat_axis=0, tiled=True)  23.2 us
    all_to_all x2, starting transfers between devices, exchange(): return lax.all_to_all(x, axes, split_axis=0, concat_axis=0, tiled=True)  16.1 us
    pallas_call x1, Pallas kernels, attend(): pl.pallas_call(functools.partial(attend_kernel, sides=len(caches), heads=...  12.7 us
    pallas_call x1, Pallas kernels, spread(): pl.pallas_call(spread_kernel, out_shape=jax.ShapeDtypeStruct((copies, que...  1.54 us
    pallas_call x1, Pallas kernels, locate(): pl.pallas_call(functools.partial(locate_kernel, span=span), in_specs=[sme...  1.4 us
    unnamed x8, local copies, waits for them, and re-layouts  1.32 us
    ppermute x1, waiting for transfers between devices, per_device(): far_lengths = lax.ppermute(suffix_lengths, 'core', swap)  1.24 us
    pallas_call x1, Pallas kernels, merge(): pl.pallas_call(merge_kernel, out_shape=jax.ShapeDtypeStruct(shape, jnp.bf...  1.22 us
  transfers between devices with their start and end apart: 7, of which 3 were waited for; matrix products, arithmetic and copies ran while one was open for 0% of the time, Pallas kernels for 5%

profile of v6, /device:TPU:0, one launch (start us, length us, event | category | flops | bytes accessed | tf_op | source)
XLA Modules:
  0.0 60.0 jit_solution(4241675441226684815)
XLA Ops:
  0.0 0.0 collective-permute-start.1
  0.0 0.5 collective-permute-start.2
  0.5 0.0 collective-permute-start.3
  0.5 0.5 collective-permute-start.4
  1.0 1.5 %spread.1 = bf16[64,32,128]{2,1,0:T(8,128)(2,1)} custom-call(bf16[4,2,512]{2,1,0:T(2,128)(2,1)} %q_ref.2), custom_call_target="tpu_custom_call" | custom-call | tf_op jit(solution)/shard_map/spread/pallas_call | solution.py:79
  2.6 11.5 %all-to-all-start = ((bf16[64,32,128]{2,1,0:T(8,128)(2,1)}), bf16[64,32,128]{2,1,0:T(8,128)(2,1)S(1)}, u32[]{:S(2)}, u32[]{:S(2)}) async-start(bf16[64,32,128]{2,1,0:T(8,128)(2,1)} %spread.1), calls=%async_computation | async-start | bytes 1048576 | tf_op jit(solution)/shard_map/all_to_all | solution.py:334
  14.1 0.1 collective-permute-start
  14.2 1.2 %collective-permute-done.refs_1_ = s32[4]{0:T(128)S(1)} collective-permute-done((s32[4]{0:T(128)}, s32[4]{0:T(128)S(1)}, u32[]{:S(2)}, u32[]{:S(2)}) %collective-permute-start) | collective-permute-done | bytes 48 | tf_op jit(solution)/shard_map/ppermute | solution.py:356
  15.4 0.0 copy-start.2
  15.4 0.7 %copy-done.2 = s32[32]{0:T(128)S(1)} copy-done((s32[32]{0:T(128)S(1)}, s32[32]{0:T(128)}, u32[]{:S(2)}) %copy-start.2) | copy-done | bytes 152
  16.1 0.0 copy-start.3
  16.1 0.7 %copy-done.3 = s32[4]{0:T(128)S(1)} copy-done((s32[4]{0:T(128)S(1)}, s32[4]{0:T(128)}, u32[]{:S(2)}) %copy-start.3) | copy-done | bytes 40
  16.7 1.4 %locate.1.info = s32[24]{0:T(128)S(1)} custom-call(s32[32]{0:T(128)S(1)} %copy-done.2, s32[4]{0:T(128)S(1)} %copy-done.3, s32[4]{0:T(128)S(1)} %collective-permute-done.refs_1_), custom_call_target="tpu_custom_call" | custom-call | tf_op jit(solution)/shard_map/locate/pallas_call | solution.py:112
  18.1 9.6 %all-to-all-done = bf16[64,32,128]{2,1,0:T(8,128)(2,1)S(1)} async-done(((bf16[64,32,128]{2,1,0:T(8,128)(2,1)}), bf16[64,32,128]{2,1,0:T(8,128)(2,1)S(1)}, u32[]{:S(2)}, u32[]{:S(2)}) %all-to-all-start) | async-done | bytes 524320 | tf_op jit(solution)/shard_map/all_to_all | solution.py:334
  27.7 0.0 collective-permute-done.1.refs_4_
  27.7 0.0 collective-permute-done.2.refs_5_
  27.7 0.0 collective-permute-done.3.refs_6_
  27.7 0.0 collective-permute-done.4.refs_7_
  27.7 0.0 copy-start
  27.7 0.0 copy-start.1
  27.7 12.7 %attend.1 = bf16[4,16,40,128]{3,2,1,0:T(8,128)(2,1)} custom-call(s32[24]{0:T(128)S(1)} %locate.1.info, bf16[4,8,64,128]{3,2,1,0:T(8,128)(2,1)S(1)} %bitcast.2, bf16[1024,1024]{1,0:T(8,128)(2,1)} %refs_0_.3, bf16[1024,1024]{1,0:T(8,128)(2,1)} %refs_1_.1, bf16[4,256,1024]{2,1,0:T(8,128)(2,1)} %refs_2_.1, bf16[4,256,1024]{2,1,0:T(8,128)(2,1)} %refs_3_.1, ...), custom_call_target="tpu_custom_call" | custom-call | tf_op jit(solution)/shard_map/attend/pallas_call | solution.py:239
  40.4 4.7 %all-to-all-start.1 = ((bf16[64,40,128]{2,1,0:T(8,128)(2,1)}), bf16[64,40,128]{2,1,0:T(8,128)(2,1)S(1)}, u32[]{:S(2)}, u32[]{:S(2)}) async-start(bf16[64,40,128]{2,1,0:T(8,128)(2,1)} %bitcast.1), calls=%async_computation.1 | async-start | bytes 1310720 | tf_op jit(solution)/shard_map/all_to_all | solution.py:334
  45.1 0.0 copy-done
  45.1 0.0 copy-done.1
  45.1 0.1 new_tokens.1
  45.2 13.6 %all-to-all-done.1.parts_ref = bf16[64,40,128]{2,1,0:T(8,128)(2,1)S(1)} async-done(((bf16[64,40,128]{2,1,0:T(8,128)(2,1)}), bf16[64,40,128]{2,1,0:T(8,128)(2,1)S(1)}, u32[]{:S(2)}, u32[]{:S(2)}) %all-to-all-start.1) | async-done | bytes 655392 | tf_op jit(solution)/shard_map/all_to_all | solution.py:334
  58.8 1.2 %merge.1 = bf16[4,2,512]{2,1,0:T(2,128)(2,1)} custom-call(bf16[64,40,128]{2,1,0:T(8,128)(2,1)S(1)} %all-to-all-done.1.parts_ref, f32[2,4,8,128]{3,2,1,0:T(8,128)S(1)} %get-tuple-element.21.score_ref, f32[2,4,8,128]{3,2,1,0:T(8,128)S(1)} %get-tuple-element.22.value_ref), custom_call_target="tpu_custom_call" | custom-call | tf_op jit(solution)/shard_map/merge/pallas_call | solution.py:322
Async XLA Ops:
  0.0 27.7 %collective-permute-start.1 = (bf16[1024,1024]{1,0:T(8,128)(2,1)}, bf16[1024,1024]{1,0:T(8,128)(2,1)S(1)}, u32[]{:S(2)}, u32[]{:S(2)}) collective-permute-start(bf16[1024,1024]{1,0:T(8,128)(2,1)} %refs_0_.3), channel_id=1, source_target_pairs={{0,16},{16,0},{1,17},{17,1},{2,18},{18,2},{3,19},{19,3},{4,20},{20... | collective-permute-start | bytes 6291464 | tf_op jit(solution)/shard_map/ppermute | solution.py:354
  0.0 27.7 %collective-permute-start.2 = (bf16[1024,1024]{1,0:T(8,128)(2,1)}, bf16[1024,1024]{1,0:T(8,128)(2,1)}, u32[]{:S(2)}, u32[]{:S(2)}) collective-permute-start(bf16[1024,1024]{1,0:T(8,128)(2,1)} %refs_1_.1), channel_id=1, source_target_pairs={{0,16},{16,0},{1,17},{17,1},{2,18},{18,2},{3,19},{19,3},{4,20},{20... | collective-permute-start | bytes 6291464 | tf_op jit(solution)/shard_map/ppermute | solution.py:354
  0.5 27.2 %collective-permute-start.3 = (bf16[4,256,1024]{2,1,0:T(8,128)(2,1)}, bf16[4,256,1024]{2,1,0:T(8,128)(2,1)}, u32[]{:S(2)}, u32[]{:S(2)}) collective-permute-start(bf16[4,256,1024]{2,1,0:T(8,128)(2,1)} %refs_2_.1), channel_id=1, source_target_pairs={{0,16},{16,0},{1,17},{17,1},{2,18},{18,2},{3,19},{19,3},{4,20},{20... | collective-permute-start | bytes 6291464 | tf_op jit(solution)/shard_map/ppermute | solution.py:354
  0.5 27.2 %collective-permute-start.4 = (bf16[4,256,1024]{2,1,0:T(8,128)(2,1)}, bf16[4,256,1024]{2,1,0:T(8,128)(2,1)}, u32[]{:S(2)}, u32[]{:S(2)}) collective-permute-start(bf16[4,256,1024]{2,1,0:T(8,128)(2,1)} %refs_3_.1), channel_id=1, source_target_pairs={{0,16},{16,0},{1,17},{17,1},{2,18},{18,2},{3,19},{19,3},{4,20},{20... | collective-permute-start | bytes 6291464 | tf_op jit(solution)/shard_map/ppermute | solution.py:354
  2.6 25.1 %all-to-all-start = ((bf16[64,32,128]{2,1,0:T(8,128)(2,1)}), bf16[64,32,128]{2,1,0:T(8,128)(2,1)S(1)}, u32[]{:S(2)}, u32[]{:S(2)}) async-start(bf16[64,32,128]{2,1,0:T(8,128)(2,1)} %spread.1), calls=%async_computation | async-start | bytes 1048576 | tf_op jit(solution)/shard_map/all_to_all | solution.py:334
  14.1 1.3 %collective-permute-start = (s32[4]{0:T(128)}, s32[4]{0:T(128)S(1)}, u32[]{:S(2)}, u32[]{:S(2)}) collective-permute-start(s32[4]{0:T(128)} %refs_0_.2), channel_id=1, source_target_pairs={{0,16},{16,0},{1,17},{17,1},{2,18},{18,2},{3,19},{19,3},{4,20},{20... | collective-permute-start | bytes 56 | tf_op jit(solution)/shard_map/ppermute | solution.py:356
  15.4 0.7 %copy-start.2 = (s32[32]{0:T(128)S(1)}, s32[32]{0:T(128)}, u32[]{:S(2)}) copy-start(s32[32]{0:T(128)} %slot_ref) | copy-start | bytes 388
  16.1 0.7 %copy-start.3 = (s32[4]{0:T(128)S(1)}, s32[4]{0:T(128)}, u32[]{:S(2)}) copy-start(s32[4]{0:T(128)} %refs_0_.2) | copy-start | bytes 52
  27.7 17.4 %copy-start = (bf16[4,2,512]{2,1,0:T(2,128)(2,1)S(1)}, bf16[4,2,512]{2,1,0:T(2,128)(2,1)}, u32[]{:S(2)}) copy-start(bf16[4,2,512]{2,1,0:T(2,128)(2,1)} %q_ref.2) | copy-start | bytes 24580
  27.7 17.4 %copy-start.1 = (bf16[4,2,2,1024]{3,2,1,0:T(2,128)(2,1)S(1)}, bf16[4,2,2,1024]{3,2,1,0:T(2,128)(2,1)}, u32[]{:S(2)}) copy-start(bf16[4,2,2,1024]{3,2,1,0:T(2,128)(2,1)} %new_ref) | copy-start | bytes 98308
  40.4 18.4 %all-to-all-start.1 = ((bf16[64,40,128]{2,1,0:T(8,128)(2,1)}), bf16[64,40,128]{2,1,0:T(8,128)(2,1)S(1)}, u32[]{:S(2)}, u32[]{:S(2)}) async-start(bf16[64,40,128]{2,1,0:T(8,128)(2,1)} %bitcast.1), calls=%async_computation.1 | async-start | bytes 1310720 | tf_op jit(solution)/shard_map/all_to_all | solution.py:334

commit v7 on v6

--- a/solution.py
+++ b/solution.py
@@ -119,14 +119,14 @@
     )(row_slot, *lengths)
 
 
-def attend_kernel(info, near_ref, *refs, sides, heads, chunk):
+def attend_kernel(info, near_ref, *refs, sides, heads):
     count = 4 * sides
     sources, out_ref, held = refs[:count], refs[count], refs[count + 1 : 2 * count + 1]
     block, q_ref, own_top, own_acc, sems, out_sems = refs[2 * count + 1 :]
     layers, _, rows, _ = near_ref.shape
     _, _, halves, tiles = q_ref.shape[:4]
     numerators = tiles * 8
-    per_chunk = chunk // rows
+    chunk = layers * rows
     wide = heads * HEAD
     length = sources[0].shape[0]
     slots, span, _ = sources[2].shape
@@ -149,51 +149,24 @@
 
     own_top[...] = jnp.full(own_top.shape, LOWEST, jnp.float32)
     own_acc[...] = jnp.zeros(own_acc.shape, jnp.float32)
-    position = iota((halves * 8, span), 1)
+    position = iota((heads * halves * 8, span), 1)
 
     def cut(i):
         return slice(i * HEAD, (i + 1) * HEAD)
 
     @pl.loop(0, pairs)
     def _(pair):
-        for n in range(count):
-            copy(n, pair).wait()
         first = pair * heads
 
-        def scored(i, c):
-            at = slice(c * per_chunk, (c + 1) * per_chunk)
-            q = near_ref[at, first + i].reshape(chunk, HEAD)
+        def wait(kind):
+            for side in range(sides):
+                copy(4 * side + kind, pair).wait()
+
+        def scored(i):
+            q = near_ref[:, first + i].reshape(chunk, HEAD)
             return [dot(q, held[4 * side][pair, :, cut(i)], NT) for side in range(sides)]
 
-        items = [(i, c) for i in range(heads) for c in range(layers // per_chunk)]
-        scores = scored(*items[0])
-
-        for i in range(heads):
-            x = near_ref[:, first + i].astype(jnp.float32)
-            q_ref[:, i] = x.reshape((layers,) + q_ref.shape[2:])
-        found = []
-        total = sides * slots
-        for j in range(total):
-            layer, row, live = info[j], info[total + j], info[2 * total + j]
-            sk_ref, sv_ref = held[4 * (j // slots) + 2 : 4 * (j // slots) + 4]
-            for i in range(heads):
-                q = q_ref[jnp.minimum(layer, layers - 1), i, :, row]
-                q = q.reshape(halves * 8, HEAD).astype(jnp.bfloat16)
-                own = dot(q, sk_ref[pair, j % slots, :, cut(i)], NT) * SCALE
-                own = jnp.where(position < live, own, LOWEST)
-                peak = jnp.max(own, axis=1, keepdims=True)
-                peak = jnp.broadcast_to(as_bf16(peak), (halves * 8, HEAD))
-                shift = jnp.concatenate([peak] * (span // HEAD), axis=1)
-                weights = jnp.exp2(own - shift).astype(jnp.bfloat16)
-                values = sv_ref[pair, j % slots, :, cut(i)]
-                values = jnp.concatenate([values, ones[:span]], axis=1)
-                found.append((layer, i, row, peak, dot(weights, values, NN)))
-        for layer, i, row, peak, summed in found:
-            own_top[layer, i, :, row] = peak.reshape(halves, 8, HEAD)
-            own_acc[layer, i, :, row] = summed.reshape(halves, 8, 2 * HEAD)
-
-        for number, (i, c) in enumerate(items):
-            later = scored(*items[number + 1]) if number + 1 < len(items) else None
+        def weigh(i, scores):
             peak = functools.reduce(jnp.maximum, [jnp.max(x, axis=1, keepdims=True) for x in scores])
             peak = jnp.broadcast_to(as_bf16(peak * SCALE), (chunk, HEAD))
             shift = jnp.concatenate([peak] * (length // HEAD), axis=1)
@@ -203,9 +176,11 @@
                 values = held[4 * side + 1][pair, :, cut(i)]
                 part = dot(weights, jnp.concatenate([values, ones], axis=1), NN)
                 summed = part if summed is None else summed + part
-            at = slice(c * per_chunk, (c + 1) * per_chunk)
-            own = own_top[at, i].reshape(chunk, HEAD)
-            carried = own_acc[at, i].reshape(chunk, 2 * HEAD)
+            return peak, summed
+
+        def finish(i, peak, summed):
+            own = own_top[:layers, i].reshape(chunk, HEAD)
+            carried = own_acc[:layers, i].reshape(chunk, 2 * HEAD)
             top = jnp.maximum(peak, own)
             keep, add = jnp.exp2(peak - top), jnp.exp2(own - top)
             sums = summed[:, HEAD:] * keep + carried[:, HEAD:] * add
@@ -217,9 +192,56 @@
                 tail = pack([top[p] for p in parts], [sums[p] for p in parts])
                 results.append((numerator[low : low + numerators], tail))
             for b, (found_block, tail) in enumerate(results):
-                to = block.at[c * per_chunk + b // halves, (first + i) * halves + b % halves]
+                to = block.at[b // halves, (first + i) * halves + b % halves]
                 to[:numerators] = found_block
                 to[numerators:] = tail
+
+        def continuations():
+            for i in range(heads):
+                x = near_ref[:, first + i].astype(jnp.float32)
+                q_ref[:, i] = x.reshape((layers,) + q_ref.shape[2:])
+            total = sides * slots
+            size = halves * 8
+            none = jnp.zeros((size, HEAD), jnp.float32)
+            found = []
+            for j in range(total):
+                layer, row, live = info[j], info[total + j], info[2 * total + j]
+                sk_ref, sv_ref = held[4 * (j // slots) + 2 : 4 * (j // slots) + 4]
+                wide_rows = []
+                for i in range(heads):
+                    q = q_ref[jnp.minimum(layer, layers - 1), i, :, row].reshape(size, HEAD)
+                    wide_rows.append(
+                        jnp.concatenate([q if n == i else none for n in range(heads)], axis=1)
+                    )
+                q = jnp.concatenate(wide_rows, axis=0).astype(jnp.bfloat16)
+                own = dot(q, sk_ref[pair, j % slots], NT) * SCALE
+                own = jnp.where(position < live, own, LOWEST)
+                peak = jnp.max(own, axis=1, keepdims=True)
+                peak = jnp.broadcast_to(as_bf16(peak), (heads * size, HEAD))
+                shift = jnp.concatenate([peak] * (span // HEAD), axis=1)
+                weights = jnp.exp2(own - shift)
+                sums = jnp.sum(weights, axis=1, keepdims=True)
+                sums = jnp.broadcast_to(sums, (heads * size, HEAD))
+                summed = dot(weights.astype(jnp.bfloat16), sv_ref[pair, j % slots], NN)
+                found.append((layer, row, peak, sums, summed))
+            for layer, row, peak, sums, summed in found:
+                for i in range(heads):
+                    at = slice(i * size, (i + 1) * size)
+                    state = jnp.concatenate([summed[at, cut(i)], sums[at]], axis=1)
+                    own_top[layer, i, :, row] = peak[at].reshape(halves, 8, HEAD)
+                    own_acc[layer, i, :, row] = state.reshape(halves, 8, 2 * HEAD)
+
+        wait(0)
+        scores = scored(0)
+        wait(1)
+        wait(2)
+        wait(3)
+        for i in range(heads):
+            later = scored(i + 1) if i + 1 < heads else None
+            peak, summed = weigh(i, scores)
+            if i == 0:
+                continuations()
+            finish(i, peak, summed)
             scores = later
         send(pair).start()
 
@@ -227,7 +249,7 @@
         send(pair).wait()
 
 
-def attend(info, near, caches, heads, chunk):
+def attend(info, near, caches, heads):
     layers, members, numerators, _ = near.shape
     halves = members // KVH
     near = near.reshape(layers, KVH, halves * numerators, HEAD)
@@ -237,7 +259,7 @@
     anywhere = pl.BlockSpec(memory_space=pl.ANY)
     pairs = KVH // heads
     return pl.pallas_call(
-        functools.partial(attend_kernel, sides=len(caches), heads=heads, chunk=chunk),
+        functools.partial(attend_kernel, sides=len(caches), heads=heads),
         in_specs=[
             pl.BlockSpec(memory_space=pltpu.SMEM),
             pl.BlockSpec(memory_space=pltpu.VMEM),
@@ -360,7 +382,7 @@
     info = locate(row_slot, (suffix_lengths, far_lengths), suffix_keys.shape[1])
     near, info = lax.optimization_barrier((near, info))
     near = near.reshape((layers, members) + near.shape[1:])
-    parts = attend(info, near, (own, far), 2, 128)
+    parts = attend(info, near, (own, far), 2)
     parts, queries, new_kv = lax.optimization_barrier((parts, queries, new_kv))
     received = exchange(parts.reshape((chips,) + parts.shape[2:]), CHIPS)
     scores, values = new_tokens(queries, new_kv)

time: 60.4 us -> 66.2 us (1.096)
  Pallas kernels: 17 us -> 22.7 us
    pallas_call x1, Pallas kernels: 12.7 us -> 18.5 us  [attend(): pl.pallas_call(functools.partial(attend_kernel, sides=len(caches), heads=...]
where the time goes in v7:
time: 66.2 us; the launch traced here: 65.8 us
  waiting for transfers between devices  24.4 us (37%)
  Pallas kernels  22.7 us (34%)
  starting transfers between devices  17.3 us (26%)
  local copies, waits for them, and re-layouts  1.32 us (2%)
    all_to_all x2, waiting for transfers between devices, exchange(): return lax.all_to_all(x, axes, split_axis=0, concat_axis=0, tiled=True)  23.2 us
    pallas_call x1, Pallas kernels, attend(): pl.pallas_call(functools.partial(attend_kernel, sides=len(caches), heads=...  18.5 us
    all_to_all x2, starting transfers between devices, exchange(): return lax.all_to_all(x, axes, split_axis=0, concat_axis=0, tiled=True)  16.2 us
    pallas_call x1, Pallas kernels, spread(): pl.pallas_call(spread_kernel, out_shape=jax.ShapeDtypeStruct((copies, que...  1.54 us
    pallas_call x1, Pallas kernels, locate(): pl.pallas_call(functools.partial(locate_kernel, span=span), in_specs=[sme...  1.4 us
  transfers between devices with their start and end apart: 7, of which 3 were waited for; matrix products, arithmetic and copies ran while one was open for 0% of the time, Pallas kernels for 5%

profile of v7, /device:TPU:0, one launch (start us, length us, event | category | flops | bytes accessed | tf_op | source)
XLA Modules:
  0.0 65.8 jit_solution(11971064838103541294)
XLA Ops:
  0.0 0.0 collective-permute-start.1
  0.0 0.5 collective-permute-start.2
  0.5 0.0 collective-permute-start.3
  0.5 0.5 collective-permute-start.4
  1.0 1.5 %spread.1 = bf16[64,32,128]{2,1,0:T(8,128)(2,1)} custom-call(bf16[4,2,512]{2,1,0:T(2,128)(2,1)} %q_ref.2), custom_call_target="tpu_custom_call" | custom-call | tf_op jit(solution)/shard_map/spread/pallas_call | solution.py:79
  2.6 11.5 %all-to-all-start = ((bf16[64,32,128]{2,1,0:T(8,128)(2,1)}), bf16[64,32,128]{2,1,0:T(8,128)(2,1)S(1)}, u32[]{:S(2)}, u32[]{:S(2)}) async-start(bf16[64,32,128]{2,1,0:T(8,128)(2,1)} %spread.1), calls=%async_computation | async-start | bytes 1048576 | tf_op jit(solution)/shard_map/all_to_all | solution.py:356
  14.1 0.1 collective-permute-start
  14.2 1.2 %collective-permute-done.refs_1_ = s32[4]{0:T(128)S(1)} collective-permute-done((s32[4]{0:T(128)}, s32[4]{0:T(128)S(1)}, u32[]{:S(2)}, u32[]{:S(2)}) %collective-permute-start) | collective-permute-done | bytes 48 | tf_op jit(solution)/shard_map/ppermute | solution.py:378
  15.4 0.0 copy-start.2
  15.4 0.7 copy-done.2
  16.1 0.0 copy-start.3
  16.1 0.7 copy-done.3
  16.7 1.4 %locate.1.info = s32[24]{0:T(128)S(1)} custom-call(s32[32]{0:T(128)S(1)} %copy-done.2, s32[4]{0:T(128)S(1)} %copy-done.3, s32[4]{0:T(128)S(1)} %collective-permute-done.refs_1_), custom_call_target="tpu_custom_call" | custom-call | tf_op jit(solution)/shard_map/locate/pallas_call | solution.py:112
  18.1 9.6 %all-to-all-done = bf16[64,32,128]{2,1,0:T(8,128)(2,1)S(1)} async-done(((bf16[64,32,128]{2,1,0:T(8,128)(2,1)}), bf16[64,32,128]{2,1,0:T(8,128)(2,1)S(1)}, u32[]{:S(2)}, u32[]{:S(2)}) %all-to-all-start) | async-done | bytes 524320 | tf_op jit(solution)/shard_map/all_to_all | solution.py:356
  27.7 0.0 collective-permute-done.1.refs_4_
  27.7 0.0 collective-permute-done.2.refs_5_
  27.7 0.0 collective-permute-done.3.refs_6_
  27.7 0.0 collective-permute-done.4.refs_7_
  27.7 0.0 copy-start
  27.7 0.0 copy-start.1
  27.7 18.5 %attend.1 = bf16[4,16,40,128]{3,2,1,0:T(8,128)(2,1)} custom-call(s32[24]{0:T(128)S(1)} %locate.1.info, bf16[4,8,64,128]{3,2,1,0:T(8,128)(2,1)S(1)} %bitcast.2, bf16[1024,1024]{1,0:T(8,128)(2,1)} %refs_0_.3, bf16[1024,1024]{1,0:T(8,128)(2,1)} %refs_1_.1, bf16[4,256,1024]{2,1,0:T(8,128)(2,1)} %refs_2_.1, bf16[4,256,1024]{2,1,0:T(8,128)(2,1)} %refs_3_.1, ...), custom_call_target="tpu_custom_call" | custom-call | tf_op jit(solution)/shard_map/attend/pallas_call | solution.py:261
  46.2 4.7 %all-to-all-start.1 = ((bf16[64,40,128]{2,1,0:T(8,128)(2,1)}), bf16[64,40,128]{2,1,0:T(8,128)(2,1)S(1)}, u32[]{:S(2)}, u32[]{:S(2)}) async-start(bf16[64,40,128]{2,1,0:T(8,128)(2,1)} %bitcast.1), calls=%async_computation.1 | async-start | bytes 1310720 | tf_op jit(solution)/shard_map/all_to_all | solution.py:356
  50.9 0.0 copy-done
  50.9 0.0 copy-done.1
  50.9 0.1 new_tokens.1
  51.0 13.6 %all-to-all-done.1.parts_ref = bf16[64,40,128]{2,1,0:T(8,128)(2,1)S(1)} async-done(((bf16[64,40,128]{2,1,0:T(8,128)(2,1)}), bf16[64,40,128]{2,1,0:T(8,128)(2,1)S(1)}, u32[]{:S(2)}, u32[]{:S(2)}) %all-to-all-start.1) | async-done | bytes 655392 | tf_op jit(solution)/shard_map/all_to_all | solution.py:356
  64.6 1.2 %merge.1 = bf16[4,2,512]{2,1,0:T(2,128)(2,1)} custom-call(bf16[64,40,128]{2,1,0:T(8,128)(2,1)S(1)} %all-to-all-done.1.parts_ref, f32[2,4,8,128]{3,2,1,0:T(8,128)S(1)} %get-tuple-element.21.score_ref, f32[2,4,8,128]{3,2,1,0:T(8,128)S(1)} %get-tuple-element.22.value_ref), custom_call_target="tpu_custom_call" | custom-call | tf_op jit(solution)/shard_map/merge/pallas_call | solution.py:344
Async XLA Ops:
  0.0 27.7 %collective-permute-start.1 = (bf16[1024,1024]{1,0:T(8,128)(2,1)}, bf16[1024,1024]{1,0:T(8,128)(2,1)S(1)}, u32[]{:S(2)}, u32[]{:S(2)}) collective-permute-start(bf16[1024,1024]{1,0:T(8,128)(2,1)} %refs_0_.3), channel_id=1, source_target_pairs={{0,16},{16,0},{1,17},{17,1},{2,18},{18,2},{3,19},{19,3},{4,20},{20... | collective-permute-start | bytes 6291464 | tf_op jit(solution)/shard_map/ppermute | solution.py:376
  0.0 27.7 %collective-permute-start.2 = (bf16[1024,1024]{1,0:T(8,128)(2,1)}, bf16[1024,1024]{1,0:T(8,128)(2,1)}, u32[]{:S(2)}, u32[]{:S(2)}) collective-permute-start(bf16[1024,1024]{1,0:T(8,128)(2,1)} %refs_1_.1), channel_id=1, source_target_pairs={{0,16},{16,0},{1,17},{17,1},{2,18},{18,2},{3,19},{19,3},{4,20},{20... | collective-permute-start | bytes 6291464 | tf_op jit(solution)/shard_map/ppermute | solution.py:376
  0.5 27.2 %collective-permute-start.3 = (bf16[4,256,1024]{2,1,0:T(8,128)(2,1)}, bf16[4,256,1024]{2,1,0:T(8,128)(2,1)}, u32[]{:S(2)}, u32[]{:S(2)}) collective-permute-start(bf16[4,256,1024]{2,1,0:T(8,128)(2,1)} %refs_2_.1), channel_id=1, source_target_pairs={{0,16},{16,0},{1,17},{17,1},{2,18},{18,2},{3,19},{19,3},{4,20},{20... | collective-permute-start | bytes 6291464 | tf_op jit(solution)/shard_map/ppermute | solution.py:376
  0.5 27.2 %collective-permute-start.4 = (bf16[4,256,1024]{2,1,0:T(8,128)(2,1)}, bf16[4,256,1024]{2,1,0:T(8,128)(2,1)}, u32[]{:S(2)}, u32[]{:S(2)}) collective-permute-start(bf16[4,256,1024]{2,1,0:T(8,128)(2,1)} %refs_3_.1), channel_id=1, source_target_pairs={{0,16},{16,0},{1,17},{17,1},{2,18},{18,2},{3,19},{19,3},{4,20},{20... | collective-permute-start | bytes 6291464 | tf_op jit(solution)/shard_map/ppermute | solution.py:376
  2.6 25.1 %all-to-all-start = ((bf16[64,32,128]{2,1,0:T(8,128)(2,1)}), bf16[64,32,128]{2,1,0:T(8,128)(2,1)S(1)}, u32[]{:S(2)}, u32[]{:S(2)}) async-start(bf16[64,32,128]{2,1,0:T(8,128)(2,1)} %spread.1), calls=%async_computation | async-start | bytes 1048576 | tf_op jit(solution)/shard_map/all_to_all | solution.py:356
  14.1 1.3 %collective-permute-start = (s32[4]{0:T(128)}, s32[4]{0:T(128)S(1)}, u32[]{:S(2)}, u32[]{:S(2)}) collective-permute-start(s32[4]{0:T(128)} %refs_0_.2), channel_id=1, source_target_pairs={{0,16},{16,0},{1,17},{17,1},{2,18},{18,2},{3,19},{19,3},{4,20},{20... | collective-permute-start | bytes 56 | tf_op jit(solution)/shard_map/ppermute | solution.py:378
  15.4 0.7 copy-start.2
  16.1 0.7 copy-start.3
  27.7 23.2 %copy-start = (bf16[4,2,512]{2,1,0:T(2,128)(2,1)S(1)}, bf16[4,2,512]{2,1,0:T(2,128)(2,1)}, u32[]{:S(2)}) copy-start(bf16[4,2,512]{2,1,0:T(2,128)(2,1)} %q_ref.2) | copy-start | bytes 24580
  27.7 23.2 %copy-start.1 = (bf16[4,2,2,1024]{3,2,1,0:T(2,128)(2,1)S(1)}, bf16[4,2,2,1024]{3,2,1,0:T(2,128)(2,1)}, u32[]{:S(2)}) copy-start(bf16[4,2,2,1024]{3,2,1,0:T(2,128)(2,1)} %new_ref) | copy-start | bytes 98308
  46.2 18.4 %all-to-all-start.1 = ((bf16[64,40,128]{2,1,0:T(8,128)(2,1)}), bf16[64,40,128]{2,1,0:T(8,128)(2,1)S(1)}, u32[]{:S(2)}, u32[]{:S(2)}) async-start(bf16[64,40,128]{2,1,0:T(8,128)(2,1)} %bitcast.1), calls=%async_computation.1 | async-start | bytes 1310720 | tf_op jit(solution)/shard_map/all_to_all | solution.py:356

commit v8 on v6

--- a/solution.py
+++ b/solution.py
@@ -119,146 +119,212 @@
     )(row_slot, *lengths)
 
 
-def attend_kernel(info, near_ref, *refs, sides, heads, chunk):
-    count = 4 * sides
-    sources, out_ref, held = refs[:count], refs[count], refs[count + 1 : 2 * count + 1]
-    block, q_ref, own_top, own_acc, sems, out_sems = refs[2 * count + 1 :]
+def attend_kernel(info, near_ref, *refs, sides, heads, tile):
+    sources, out_ref = refs[: 4 * sides], refs[4 * sides]
+    k_ref, v_ref, sk_ref, sv_ref, block, q_ref, own_top, own_acc = refs[4 * sides + 1 :][:8]
+    even_scores, odd_scores, even_peak, odd_peak, sems, own_sems, out_sems = refs[4 * sides + 9 :]
     layers, _, rows, _ = near_ref.shape
     _, _, halves, tiles = q_ref.shape[:4]
     numerators = tiles * 8
-    per_chunk = chunk // rows
+    chunk = layers * rows
     wide = heads * HEAD
     length = sources[0].shape[0]
     slots, span, _ = sources[2].shape
-    ones = jnp.ones((length, HEAD), jnp.bfloat16)
     pairs = KVH // heads
-
-    def copy(n, pair):
-        start = pair * wide if isinstance(pair, int) else pl.multiple_of(pair * wide, wide)
-        at = pl.ds(start, wide)
-        part = sources[n].at[:, at] if n % 4 < 2 else sources[n].at[:, :, at]
-        return pltpu.make_async_copy(part, held[n].at[pair], sems.at[n, pair])
+    ones = jnp.ones((tile, HEAD), jnp.bfloat16)
+
+    def columns_at(index, width):
+        start = index * width if isinstance(index, int) else pl.multiple_of(index * width, width)
+        return pl.ds(start, width)
+
+    def copy(side, kind, index):
+        source = sources[4 * side + kind]
+        if kind < 2:
+            to = (k_ref, v_ref)[kind].at[index, pl.ds(side * length, length)]
+            part = source.at[:, columns_at(index, HEAD)]
+            return pltpu.make_async_copy(part, to, sems.at[2 * side + kind, index])
+        to = (sk_ref, sv_ref)[kind - 2].at[index, pl.ds(side * slots, slots)]
+        part = source.at[:, :, columns_at(index, wide)]
+        return pltpu.make_async_copy(part, to, own_sems.at[2 * side + kind - 2, index])
+
+    def wait(kind, index):
+        for side in range(sides):
+            copy(side, kind, index).wait()
 
     def send(pair):
         at = pl.ds(pair * heads * halves, heads * halves)
         return pltpu.make_async_copy(block.at[:, at], out_ref.at[:, at], out_sems.at[pair])
 
     for pair in range(pairs):
-        for n in range(count):
-            copy(n, pair).start()
+        for kind in (0, 1):
+            for i in range(heads):
+                for side in range(sides):
+                    copy(side, kind, pair * heads + i).start()
+        for kind in (2, 3):
+            for side in range(sides):
+                copy(side, kind, pair).start()
 
     own_top[...] = jnp.full(own_top.shape, LOWEST, jnp.float32)
     own_acc[...] = jnp.zeros(own_acc.shape, jnp.float32)
-    position = iota((halves * 8, span), 1)
-
-    def cut(i):
-        return slice(i * HEAD, (i + 1) * HEAD)
+    position = iota((heads * halves * 8, span), 1)
+    steps = sides * length // tile
+
+    def score(head, n, scores, peak):
+        q = near_ref[:, head].reshape(chunk, HEAD)
+        found = dot(q, k_ref[head, n * tile : (n + 1) * tile], NT)
+        scores[n] = found
+        return functools.reduce(jnp.maximum, columns(found) + ([] if peak is None else [peak]))
+
+    def keep_peak(peak, peak_ref):
+        peak = jnp.max(peak, axis=1, keepdims=True) * SCALE
+        peak_ref[...] = jnp.broadcast_to(as_bf16(peak), (chunk, HEAD))
+
+    def weigh(head, n, scores, shift, summed):
+        weights = jnp.exp2(scores[n] * SCALE - shift).astype(jnp.bfloat16)
+        values = v_ref[head, n * tile : (n + 1) * tile]
+        part = dot(weights, jnp.concatenate([values, ones], axis=1), NN)
+        return part if summed is None else summed + part
+
+    def both(head, scores, peak_ref, next_head, next_scores):
+        shift = jnp.concatenate([peak_ref[...]] * (tile // HEAD), axis=1)
+        summed = peak = None
+        for n in range(steps):
+            summed = weigh(head, n, scores, shift, summed)
+            peak = score(next_head, n, next_scores, peak)
+        return summed, peak
+
+    def finish(head, i, peak, summed):
+        own = own_top[:layers, i].reshape(chunk, HEAD)
+        carried = own_acc[:layers, i].reshape(chunk, 2 * HEAD)
+        top = jnp.maximum(peak, own)
+        keep, add = jnp.exp2(peak - top), jnp.exp2(own - top)
+        sums = summed[:, HEAD:] * keep + carried[:, HEAD:] * add
+        numerator = (summed[:, :HEAD] * keep + carried[:, :HEAD] * add).astype(jnp.bfloat16)
+        results = []
+        for b in range(chunk // numerators):
+            low = b * numerators
+            parts = [slice(low + 8 * a, low + 8 * a + 8) for a in range(tiles)]
+            tail = pack([top[p] for p in parts], [sums[p] for p in parts])
+            results.append((numerator[low : low + numerators], tail))
+        for b, (found, tail) in enumerate(results):
+            to = block.at[b // halves, head * halves + b % halves]
+            to[:numerators] = found
+            to[numerators:] = tail
+
+    def continuations(pair):
+        for i in range(heads):
+            x = near_ref[:, pair * heads + i].astype(jnp.float32)
+            q_ref[:, i] = x.reshape((layers,) + q_ref.shape[2:])
+        total = sides * slots
+        size = halves * 8
+        none = jnp.zeros((size, HEAD), jnp.float32)
+        found = []
+        for j in range(total):
+            layer, row, live = info[j], info[total + j], info[2 * total + j]
+            wide_rows = []
+            for i in range(heads):
+                q = q_ref[jnp.minimum(layer, layers - 1), i, :, row].reshape(size, HEAD)
+                q = [q if n == i else none for n in range(heads)]
+                wide_rows.append(jnp.concatenate(q, axis=1))
+            q = jnp.concatenate(wide_rows, axis=0).astype(jnp.bfloat16)
+            own = dot(q, sk_ref[pair, j], NT) * SCALE
+            own = jnp.where(position < live, own, LOWEST)
+            peak = jnp.max(own, axis=1, keepdims=True)
+            peak = jnp.broadcast_to(as_bf16(peak), (heads * size, HEAD))
+            shift = jnp.concatenate([peak] * (span // HEAD), axis=1)
+            weights = jnp.exp2(own - shift)
+            sums = jnp.sum(weights, axis=1, keepdims=True)
+            sums = jnp.broadcast_to(sums, (heads * size, HEAD))
+            summed = dot(weights.astype(jnp.bfloat16), sv_ref[pair, j], NN)
+            found.append((layer, row, peak, sums, summed))
+        for layer, row, peak, sums, summed in found:
+            for i in range(heads):
+                at = slice(i * size, (i + 1) * size)
+                state = [summed[at, i * HEAD : (i + 1) * HEAD], sums[at]]
+                state = jnp.concatenate(state, axis=1)
+                own_top[layer, i, :, row] = peak[at].reshape(halves, 8, HEAD)
+                own_acc[layer, i, :, row] = state.reshape(halves, 8, 2 * HEAD)
+
+    wait(0, 0)
+    peak = None
+    for n in range(steps):
+        peak = score(0, n, even_scores, peak)
+    keep_peak(peak, even_peak)
 
     @pl.loop(0, pairs)
     def _(pair):
-        for n in range(count):
-            copy(n, pair).wait()
-        first = pair * heads
-
-        def scored(i, c):
-            at = slice(c * per_chunk, (c + 1) * per_chunk)
-            q = near_ref[at, first + i].reshape(chunk, HEAD)
-            return [dot(q, held[4 * side][pair, :, cut(i)], NT) for side in range(sides)]
-
-        items = [(i, c) for i in range(heads) for c in range(layers // per_chunk)]
-        scores = scored(*items[0])
-
-        for i in range(heads):
-            x = near_ref[:, first + i].astype(jnp.float32)
-            q_ref[:, i] = x.reshape((layers,) + q_ref.shape[2:])
-        found = []
-        total = sides * slots
-        for j in range(total):
-            layer, row, live = info[j], info[total + j], info[2 * total + j]
-            sk_ref, sv_ref = held[4 * (j // slots) + 2 : 4 * (j // slots) + 4]
-            for i in range(heads):
-                q = q_ref[jnp.minimum(layer, layers - 1), i, :, row]
-                q = q.reshape(halves * 8, HEAD).astype(jnp.bfloat16)
-                own = dot(q, sk_ref[pair, j % slots, :, cut(i)], NT) * SCALE
-                own = jnp.where(position < live, own, LOWEST)
-                peak = jnp.max(own, axis=1, keepdims=True)
-                peak = jnp.broadcast_to(as_bf16(peak), (halves * 8, HEAD))
-                shift = jnp.concatenate([peak] * (span // HEAD), axis=1)
-                weights = jnp.exp2(own - shift).astype(jnp.bfloat16)
-                values = sv_ref[pair, j % slots, :, cut(i)]
-                values = jnp.concatenate([values, ones[:span]], axis=1)
-                found.append((layer, i, row, peak, dot(weights, values, NN)))
-        for layer, i, row, peak, summed in found:
-            own_top[layer, i, :, row] = peak.reshape(halves, 8, HEAD)
-            own_acc[layer, i, :, row] = summed.reshape(halves, 8, 2 * HEAD)
-
-        for number, (i, c) in enumerate(items):
-            later = scored(*items[number + 1]) if number + 1 < len(items) else None
-            peak = functools.reduce(jnp.maximum, [jnp.max(x, axis=1, keepdims=True) for x in scores])
-            peak = jnp.broadcast_to(as_bf16(peak * SCALE), (chunk, HEAD))
-            shift = jnp.concatenate([peak] * (length // HEAD), axis=1)
-            summed = None
-            for side, x in enumerate(scores):
-                weights = jnp.exp2(x * SCALE - shift).astype(jnp.bfloat16)
-                values = held[4 * side + 1][pair, :, cut(i)]
-                part = dot(weights, jnp.concatenate([values, ones], axis=1), NN)
-                summed = part if summed is None else summed + part
-            at = slice(c * per_chunk, (c + 1) * per_chunk)
-            own = own_top[at, i].reshape(chunk, HEAD)
-            carried = own_acc[at, i].reshape(chunk, 2 * HEAD)
-            top = jnp.maximum(peak, own)
-            keep, add = jnp.exp2(peak - top), jnp.exp2(own - top)
-            sums = summed[:, HEAD:] * keep + carried[:, HEAD:] * add
-            numerator = (summed[:, :HEAD] * keep + carried[:, :HEAD] * add).astype(jnp.bfloat16)
-            results = []
-            for b in range(chunk // numerators):
-                low = b * numerators
-                parts = [slice(low + 8 * a, low + 8 * a + 8) for a in range(tiles)]
-                tail = pack([top[p] for p in parts], [sums[p] for p in parts])
-                results.append((numerator[low : low + numerators], tail))
-            for b, (found_block, tail) in enumerate(results):
-                to = block.at[c * per_chunk + b // halves, (first + i) * halves + b % halves]
-                to[:numerators] = found_block
-                to[numerators:] = tail
-            scores = later
+        even = pair * heads
+        odd, after = even + 1, jnp.minimum(even + 2, KVH - 1)
+        wait(0, odd)
+        wait(1, even)
+        wait(2, pair)
+        wait(3, pair)
+        summed, peak = both(even, even_scores, even_peak, odd, odd_scores)
+        continuations(pair)
+        finish(even, 0, even_peak[...], summed)
+        keep_peak(peak, odd_peak)
+        wait(1, odd)
+
+        @pl.when(pair < pairs - 1)
+        def _():
+            wait(0, after)
+
+        summed, peak = both(odd, odd_scores, odd_peak, after, even_scores)
+        finish(odd, 1, odd_peak[...], summed)
+        keep_peak(peak, even_peak)
         send(pair).start()
 
     for pair in range(pairs):
         send(pair).wait()
 
 
-def attend(info, near, caches, heads, chunk):
+def attend(info, near, caches, tile):
+    heads = 2
     layers, members, numerators, _ = near.shape
     halves = members // KVH
     near = near.reshape(layers, KVH, halves * numerators, HEAD)
-    arrays = [x for cache in caches for x in cache]
+    keys, values, suffix_keys, suffix_values = caches[0]
+    sides = len(caches)
+    length = sides * keys.shape[0]
+    slots, span, _ = suffix_keys.shape
     out = jax.ShapeDtypeStruct((layers, members, numerators + TAIL, HEAD), jnp.bfloat16)
     tiled = (heads, halves, numerators // 8, 8)
+    rows = layers * halves * numerators
     anywhere = pl.BlockSpec(memory_space=pl.ANY)
     pairs = KVH // heads
+    prompt = pltpu.VMEM((KVH, length, HEAD), keys.dtype)
+    own = pltpu.VMEM((pairs, sides * slots, span, heads * HEAD), keys.dtype)
+    scores = pltpu.VMEM((length // tile, rows, tile), jnp.float32)
+    peak = pltpu.VMEM((rows, HEAD), jnp.float32)
     return pl.pallas_call(
-        functools.partial(attend_kernel, sides=len(caches), heads=heads, chunk=chunk),
+        functools.partial(attend_kernel, sides=sides, heads=heads, tile=tile),
         in_specs=[
             pl.BlockSpec(memory_space=pltpu.SMEM),
             pl.BlockSpec(memory_space=pltpu.VMEM),
         ]
-        + [anywhere] * len(arrays),
+        + [anywhere] * (4 * sides),
         out_specs=anywhere,
         out_shape=out,
         scratch_shapes=[
-            pltpu.VMEM((pairs,) + x.shape[:-1] + (heads * HEAD,), x.dtype) for x in arrays
-        ]
-        + [
+            prompt,
+            prompt,
+            own,
+            own,
             pltpu.VMEM(out.shape, out.dtype),
             pltpu.VMEM((layers,) + tiled + (HEAD,), jnp.float32),
             pltpu.VMEM((layers + 1,) + tiled + (HEAD,), jnp.float32),
             pltpu.VMEM((layers + 1,) + tiled + (2 * HEAD,), jnp.float32),
-            pltpu.SemaphoreType.DMA((len(arrays), pairs)),
+            scores,
+            scores,
+            peak,
+            peak,
+            pltpu.SemaphoreType.DMA((2 * sides, KVH)),
+            pltpu.SemaphoreType.DMA((2 * sides, pairs)),
             pltpu.SemaphoreType.DMA((pairs,)),
         ],
         compiler_params=pltpu.CompilerParams(vmem_limit_bytes=48 << 20),
         name="attend",
-    )(info, near, *arrays)
+    )(info, near, *[x for cache in caches for x in cache])
 
 
 def new_kernel(q_ref, new_ref, score_ref, value_ref):
@@ -360,7 +426,7 @@
     info = locate(row_slot, (suffix_lengths, far_lengths), suffix_keys.shape[1])
     near, info = lax.optimization_barrier((near, info))
     near = near.reshape((layers, members) + near.shape[1:])
-    parts = attend(info, near, (own, far), 2, 128)
+    parts = attend(info, near, (own, far), 512)
     parts, queries, new_kv = lax.optimization_barrier((parts, queries, new_kv))
     received = exchange(parts.reshape((chips,) + parts.shape[2:]), CHIPS)
     scores, values = new_tokens(queries, new_kv)

time: 60.4 us -> 65 us (1.076)
  Pallas kernels: 17 us -> 21.6 us
    pallas_call x1, Pallas kernels: 12.7 us -> 17.3 us  [attend(): pl.pallas_call(functools.partial(attend_kernel, sides=sides, heads=heads,...]
where the time goes in v8:
time: 65 us; the launch traced here: 64.7 us
  waiting for transfers between devices  24.4 us (38%)
  Pallas kernels  21.6 us (33%)
  starting transfers between devices  17.3 us (27%)
  local copies, waits for them, and re-layouts  1.32 us (2%)
    all_to_all x2, waiting for transfers between devices, exchange(): return lax.all_to_all(x, axes, split_axis=0, concat_axis=0, tiled=True)  23.1 us
    pallas_call x1, Pallas kernels, attend(): pl.pallas_call(functools.partial(attend_kernel, sides=sides, heads=heads,...  17.3 us
    all_to_all x2, starting transfers between devices, exchange(): return lax.all_to_all(x, axes, split_axis=0, concat_axis=0, tiled=True)  16.1 us
    pallas_call x1, Pallas kernels, spread(): pl.pallas_call(spread_kernel, out_shape=jax.ShapeDtypeStruct((copies, que...  1.54 us
    pallas_call x1, Pallas kernels, locate(): pl.pallas_call(functools.partial(locate_kernel, span=span), in_specs=[sme...  1.4 us
    unnamed x8, local copies, waits for them, and re-layouts  1.32 us
  transfers between devices with their start and end apart: 7, of which 3 were waited for; matrix products, arithmetic and copies ran while one was open for 0% of the time, Pallas kernels for 5%

profile of v8, /device:TPU:0, one launch (start us, length us, event | category | flops | bytes accessed | tf_op | source)
XLA Modules:
  0.0 64.7 jit_solution(17945406083058157880)
XLA Ops:
  0.0 0.0 collective-permute-start.1
  0.0 0.5 collective-permute-start.2
  0.5 0.0 collective-permute-start.3
  0.5 0.5 collective-permute-start.4
  1.0 1.5 %spread.1 = bf16[64,32,128]{2,1,0:T(8,128)(2,1)} custom-call(bf16[4,2,512]{2,1,0:T(2,128)(2,1)} %q_ref.2), custom_call_target="tpu_custom_call" | custom-call | tf_op jit(solution)/shard_map/spread/pallas_call | solution.py:79
  2.6 11.5 %all-to-all-start = ((bf16[64,32,128]{2,1,0:T(8,128)(2,1)}), bf16[64,32,128]{2,1,0:T(8,128)(2,1)S(1)}, u32[]{:S(2)}, u32[]{:S(2)}) async-start(bf16[64,32,128]{2,1,0:T(8,128)(2,1)} %spread.1), calls=%async_computation | async-start | bytes 1048576 | tf_op jit(solution)/shard_map/all_to_all | solution.py:400
  14.1 0.1 collective-permute-start
  14.2 1.2 %collective-permute-done.refs_1_ = s32[4]{0:T(128)S(1)} collective-permute-done((s32[4]{0:T(128)}, s32[4]{0:T(128)S(1)}, u32[]{:S(2)}, u32[]{:S(2)}) %collective-permute-start) | collective-permute-done | bytes 48 | tf_op jit(solution)/shard_map/ppermute | solution.py:422
  15.4 0.0 copy-start.2
  15.4 0.7 %copy-done.2 = s32[32]{0:T(128)S(1)} copy-done((s32[32]{0:T(128)S(1)}, s32[32]{0:T(128)}, u32[]{:S(2)}) %copy-start.2) | copy-done | bytes 152
  16.1 0.0 copy-start.3
  16.1 0.7 %copy-done.3 = s32[4]{0:T(128)S(1)} copy-done((s32[4]{0:T(128)S(1)}, s32[4]{0:T(128)}, u32[]{:S(2)}) %copy-start.3) | copy-done | bytes 40
  16.7 1.4 %locate.1.info = s32[24]{0:T(128)S(1)} custom-call(s32[32]{0:T(128)S(1)} %copy-done.2, s32[4]{0:T(128)S(1)} %copy-done.3, s32[4]{0:T(128)S(1)} %collective-permute-done.refs_1_), custom_call_target="tpu_custom_call" | custom-call | tf_op jit(solution)/shard_map/locate/pallas_call | solution.py:112
  18.1 9.6 %all-to-all-done = bf16[64,32,128]{2,1,0:T(8,128)(2,1)S(1)} async-done(((bf16[64,32,128]{2,1,0:T(8,128)(2,1)}), bf16[64,32,128]{2,1,0:T(8,128)(2,1)S(1)}, u32[]{:S(2)}, u32[]{:S(2)}) %all-to-all-start) | async-done | bytes 524320 | tf_op jit(solution)/shard_map/all_to_all | solution.py:400
  27.7 0.0 collective-permute-done.1.refs_4_
  27.7 0.0 collective-permute-done.2.refs_5_
  27.7 0.0 collective-permute-done.3.refs_6_
  27.7 0.0 collective-permute-done.4.refs_7_
  27.7 0.0 copy-start
  27.7 0.0 copy-start.1
  27.7 17.3 %attend.1 = bf16[4,16,40,128]{3,2,1,0:T(8,128)(2,1)} custom-call(s32[24]{0:T(128)S(1)} %locate.1.info, bf16[4,8,64,128]{3,2,1,0:T(8,128)(2,1)S(1)} %bitcast.2, bf16[1024,1024]{1,0:T(8,128)(2,1)} %refs_0_.3, bf16[1024,1024]{1,0:T(8,128)(2,1)} %refs_1_.1, bf16[4,256,1024]{2,1,0:T(8,128)(2,1)} %refs_2_.1, bf16[4,256,1024]{2,1,0:T(8,128)(2,1)} %refs_3_.1, ...), custom_call_target="tpu_custom_call" | custom-call | tf_op jit(solution)/shard_map/attend/pallas_call | solution.py:299
  45.1 4.7 %all-to-all-start.1 = ((bf16[64,40,128]{2,1,0:T(8,128)(2,1)}), bf16[64,40,128]{2,1,0:T(8,128)(2,1)S(1)}, u32[]{:S(2)}, u32[]{:S(2)}) async-start(bf16[64,40,128]{2,1,0:T(8,128)(2,1)} %bitcast.1), calls=%async_computation.1 | async-start | bytes 1310720 | tf_op jit(solution)/shard_map/all_to_all | solution.py:400
  49.7 0.0 copy-done
  49.7 0.0 copy-done.1
  49.8 0.1 new_tokens.1
  49.9 13.6 %all-to-all-done.1.parts_ref = bf16[64,40,128]{2,1,0:T(8,128)(2,1)S(1)} async-done(((bf16[64,40,128]{2,1,0:T(8,128)(2,1)}), bf16[64,40,128]{2,1,0:T(8,128)(2,1)S(1)}, u32[]{:S(2)}, u32[]{:S(2)}) %all-to-all-start.1) | async-done | bytes 655392 | tf_op jit(solution)/shard_map/all_to_all | solution.py:400
  63.4 1.2 %merge.1 = bf16[4,2,512]{2,1,0:T(2,128)(2,1)} custom-call(bf16[64,40,128]{2,1,0:T(8,128)(2,1)S(1)} %all-to-all-done.1.parts_ref, f32[2,4,8,128]{3,2,1,0:T(8,128)S(1)} %get-tuple-element.21.score_ref, f32[2,4,8,128]{3,2,1,0:T(8,128)S(1)} %get-tuple-element.22.value_ref), custom_call_target="tpu_custom_call" | custom-call | tf_op jit(solution)/shard_map/merge/pallas_call | solution.py:388
Async XLA Ops:
  0.0 27.7 %collective-permute-start.1 = (bf16[1024,1024]{1,0:T(8,128)(2,1)}, bf16[1024,1024]{1,0:T(8,128)(2,1)S(1)}, u32[]{:S(2)}, u32[]{:S(2)}) collective-permute-start(bf16[1024,1024]{1,0:T(8,128)(2,1)} %refs_0_.3), channel_id=1, source_target_pairs={{0,16},{16,0},{1,17},{17,1},{2,18},{18,2},{3,19},{19,3},{4,20},{20... | collective-permute-start | bytes 6291464 | tf_op jit(solution)/shard_map/ppermute | solution.py:420
  0.0 27.7 %collective-permute-start.2 = (bf16[1024,1024]{1,0:T(8,128)(2,1)}, bf16[1024,1024]{1,0:T(8,128)(2,1)}, u32[]{:S(2)}, u32[]{:S(2)}) collective-permute-start(bf16[1024,1024]{1,0:T(8,128)(2,1)} %refs_1_.1), channel_id=1, source_target_pairs={{0,16},{16,0},{1,17},{17,1},{2,18},{18,2},{3,19},{19,3},{4,20},{20... | collective-permute-start | bytes 6291464 | tf_op jit(solution)/shard_map/ppermute | solution.py:420
  0.5 27.2 %collective-permute-start.3 = (bf16[4,256,1024]{2,1,0:T(8,128)(2,1)}, bf16[4,256,1024]{2,1,0:T(8,128)(2,1)}, u32[]{:S(2)}, u32[]{:S(2)}) collective-permute-start(bf16[4,256,1024]{2,1,0:T(8,128)(2,1)} %refs_2_.1), channel_id=1, source_target_pairs={{0,16},{16,0},{1,17},{17,1},{2,18},{18,2},{3,19},{19,3},{4,20},{20... | collective-permute-start | bytes 6291464 | tf_op jit(solution)/shard_map/ppermute | solution.py:420
  0.5 27.2 %collective-permute-start.4 = (bf16[4,256,1024]{2,1,0:T(8,128)(2,1)}, bf16[4,256,1024]{2,1,0:T(8,128)(2,1)}, u32[]{:S(2)}, u32[]{:S(2)}) collective-permute-start(bf16[4,256,1024]{2,1,0:T(8,128)(2,1)} %refs_3_.1), channel_id=1, source_target_pairs={{0,16},{16,0},{1,17},{17,1},{2,18},{18,2},{3,19},{19,3},{4,20},{20... | collective-permute-start | bytes 6291464 | tf_op jit(solution)/shard_map/ppermute | solution.py:420
  2.6 25.1 %all-to-all-start = ((bf16[64,32,128]{2,1,0:T(8,128)(2,1)}), bf16[64,32,128]{2,1,0:T(8,128)(2,1)S(1)}, u32[]{:S(2)}, u32[]{:S(2)}) async-start(bf16[64,32,128]{2,1,0:T(8,128)(2,1)} %spread.1), calls=%async_computation | async-start | bytes 1048576 | tf_op jit(solution)/shard_map/all_to_all | solution.py:400
  14.1 1.3 %collective-permute-start = (s32[4]{0:T(128)}, s32[4]{0:T(128)S(1)}, u32[]{:S(2)}, u32[]{:S(2)}) collective-permute-start(s32[4]{0:T(128)} %refs_0_.2), channel_id=1, source_target_pairs={{0,16},{16,0},{1,17},{17,1},{2,18},{18,2},{3,19},{19,3},{4,20},{20... | collective-permute-start | bytes 56 | tf_op jit(solution)/shard_map/ppermute | solution.py:422
  15.4 0.7 %copy-start.2 = (s32[32]{0:T(128)S(1)}, s32[32]{0:T(128)}, u32[]{:S(2)}) copy-start(s32[32]{0:T(128)} %slot_ref) | copy-start | bytes 388
  16.1 0.7 %copy-start.3 = (s32[4]{0:T(128)S(1)}, s32[4]{0:T(128)}, u32[]{:S(2)}) copy-start(s32[4]{0:T(128)} %refs_0_.2) | copy-start | bytes 52
  27.7 22.0 %copy-start = (bf16[4,2,512]{2,1,0:T(2,128)(2,1)S(1)}, bf16[4,2,512]{2,1,0:T(2,128)(2,1)}, u32[]{:S(2)}) copy-start(bf16[4,2,512]{2,1,0:T(2,128)(2,1)} %q_ref.2) | copy-start | bytes 24580
  27.7 22.0 %copy-start.1 = (bf16[4,2,2,1024]{3,2,1,0:T(2,128)(2,1)S(1)}, bf16[4,2,2,1024]{3,2,1,0:T(2,128)(2,1)}, u32[]{:S(2)}) copy-start(bf16[4,2,2,1024]{3,2,1,0:T(2,128)(2,1)} %new_ref) | copy-start | bytes 98308
  45.1 18.4 %all-to-all-start.1 = ((bf16[64,40,128]{2,1,0:T(8,128)(2,1)}), bf16[64,40,128]{2,1,0:T(8,128)(2,1)S(1)}, u32[]{:S(2)}, u32[]{:S(2)}) async-start(bf16[64,40,128]{2,1,0:T(8,128)(2,1)} %bitcast.1), calls=%async_computation.1 | async-start | bytes 1310720 | tf_op jit(solution)/shard_map/all_to_all | solution.py:400

commit v9 on v6

--- a/solution.py
+++ b/solution.py
@@ -143,8 +143,9 @@
         at = pl.ds(pair * heads * halves, heads * halves)
         return pltpu.make_async_copy(block.at[:, at], out_ref.at[:, at], out_sems.at[pair])
 
+    order = [4 * side + kind for kind in (0, 2, 3, 1) for side in range(sides)]
     for pair in range(pairs):
-        for n in range(count):
+        for n in order:
             copy(n, pair).start()
 
     own_top[...] = jnp.full(own_top.shape, LOWEST, jnp.float32)
@@ -156,9 +157,11 @@
 
     @pl.loop(0, pairs)
     def _(pair):
-        for n in range(count):
-            copy(n, pair).wait()
         first = pair * heads
+
+        def wait(kind):
+            for side in range(sides):
+                copy(4 * side + kind, pair).wait()
 
         def scored(i, c):
             at = slice(c * per_chunk, (c + 1) * per_chunk)
@@ -166,7 +169,10 @@
             return [dot(q, held[4 * side][pair, :, cut(i)], NT) for side in range(sides)]
 
         items = [(i, c) for i in range(heads) for c in range(layers // per_chunk)]
+        wait(0)
         scores = scored(*items[0])
+        wait(2)
+        wait(3)
 
         for i in range(heads):
             x = near_ref[:, first + i].astype(jnp.float32)
@@ -184,14 +190,17 @@
                 peak = jnp.max(own, axis=1, keepdims=True)
                 peak = jnp.broadcast_to(as_bf16(peak), (halves * 8, HEAD))
                 shift = jnp.concatenate([peak] * (span // HEAD), axis=1)
-                weights = jnp.exp2(own - shift).astype(jnp.bfloat16)
+                weights = jnp.exp2(own - shift)
+                sums = jnp.sum(weights, axis=1, keepdims=True)
+                sums = jnp.broadcast_to(sums, (halves * 8, HEAD))
                 values = sv_ref[pair, j % slots, :, cut(i)]
-                values = jnp.concatenate([values, ones[:span]], axis=1)
-                found.append((layer, i, row, peak, dot(weights, values, NN)))
+                summed = dot(weights.astype(jnp.bfloat16), values, NN)
+                found.append((layer, i, row, peak, jnp.concatenate([summed, sums], axis=1)))
         for layer, i, row, peak, summed in found:
             own_top[layer, i, :, row] = peak.reshape(halves, 8, HEAD)
             own_acc[layer, i, :, row] = summed.reshape(halves, 8, 2 * HEAD)
 
+        wait(1)
         for number, (i, c) in enumerate(items):
             later = scored(*items[number + 1]) if number + 1 < len(items) else None
             peak = functools.reduce(jnp.maximum, [jnp.max(x, axis=1, keepdims=True) for x in scores])
@@ -351,11 +360,13 @@
     swap = [(i, (i + 1) % cores) for i in range(cores)]
 
     own = (prefix_keys, prefix_values, suffix_keys, suffix_values)
+    blocks, row_slot, suffix_lengths, *own = lax.optimization_barrier(
+        (spread(queries, chips), row_slot, suffix_lengths, *own)
+    )
     far = tuple(lax.ppermute(x, "core", swap) for x in own)
+    far_lengths = lax.ppermute(suffix_lengths, "core", swap)
     own = tuple(pltpu.with_memory_space_constraint(x, pltpu.HBM) for x in own)
-    far_lengths = lax.ppermute(suffix_lengths, "core", swap)
-
-    blocks, row_slot = lax.optimization_barrier((spread(queries, chips), row_slot))
+
     near = exchange(blocks, CHIPS)
     info = locate(row_slot, (suffix_lengths, far_lengths), suffix_keys.shape[1])
     near, info = lax.optimization_barrier((near, info))

time: 60.4 us -> 72.4 us (1.20)
  Pallas kernels: 17 us -> 28.9 us
    pallas_call x1, Pallas kernels: 12.7 us -> 24.7 us  [attend(): pl.pallas_call(functools.partial(attend_kernel, sides=len(caches), heads=...]
  transfers between devices with their start and end apart: 7 -> 7, of which waited for: 3 -> 3; matrix products, arithmetic and copies ran while one was open for 0% -> 0% of each run, Pallas kernels for 5% -> 2%
where the time goes in v9:
time: 72.4 us; the launch traced here: 72 us
  Pallas kernels  28.9 us (40%)
  waiting for transfers between devices  24.4 us (34%)
  starting transfers between devices  17.3 us (24%)
  local copies, waits for them, and re-layouts  1.32 us (2%)
    pallas_call x1, Pallas kernels, attend(): pl.pallas_call(functools.partial(attend_kernel, sides=len(caches), heads=...  24.7 us
    all_to_all x2, waiting for transfers between devices, exchange(): return lax.all_to_all(x, axes, split_axis=0, concat_axis=0, tiled=True)  23.2 us
    all_to_all x2, starting transfers between devices, exchange(): return lax.all_to_all(x, axes, split_axis=0, concat_axis=0, tiled=True)  16.2 us
    pallas_call x1, Pallas kernels, spread(): pl.pallas_call(spread_kernel, out_shape=jax.ShapeDtypeStruct((copies, que...  1.54 us
  transfers between devices with their start and end apart: 7, of which 3 were waited for; matrix products, arithmetic and copies ran while one was open for 0% of the time, Pallas kernels for 2%

profile of v9, /device:TPU:0, one launch (start us, length us, event | category | flops | bytes accessed | tf_op | source)
XLA Modules:
  0.0 72.0 jit_solution(9801966351776301166)
XLA Ops:
  0.0 1.5 %spread.1 = bf16[64,32,128]{2,1,0:T(8,128)(2,1)} custom-call(bf16[4,2,512]{2,1,0:T(2,128)(2,1)} %q_ref.2), custom_call_target="tpu_custom_call" | custom-call | tf_op jit(solution)/shard_map/spread/pallas_call | solution.py:79
  1.5 0.0 collective-permute-start.1
  1.5 0.5 collective-permute-start.2
  2.0 0.0 collective-permute-start.3
  2.1 0.5 collective-permute-start.4
  2.6 11.5 %all-to-all-start = ((bf16[64,32,128]{2,1,0:T(8,128)(2,1)}), bf16[64,32,128]{2,1,0:T(8,128)(2,1)S(1)}, u32[]{:S(2)}, u32[]{:S(2)}) async-start(bf16[64,32,128]{2,1,0:T(8,128)(2,1)} %spread.1), calls=%async_computation | async-start | bytes 1048576 | tf_op jit(solution)/shard_map/all_to_all | solution.py:343
  14.1 0.1 collective-permute-start
  14.2 1.2 %collective-permute-done.refs_1_ = s32[4]{0:T(128)S(1)} collective-permute-done((s32[4]{0:T(128)}, s32[4]{0:T(128)S(1)}, u32[]{:S(2)}, u32[]{:S(2)}) %collective-permute-start) | collective-permute-done | bytes 48 | tf_op jit(solution)/shard_map/ppermute | solution.py:367
  15.4 0.0 copy-start.2
  15.4 0.7 copy-done.2
  16.1 0.0 copy-start.3
  16.1 0.7 copy-done.3
  16.7 1.4 %locate.1.info = s32[24]{0:T(128)S(1)} custom-call(s32[32]{0:T(128)S(1)} %copy-done.2, s32[4]{0:T(128)S(1)} %copy-done.3, s32[4]{0:T(128)S(1)} %collective-permute-done.refs_1_), custom_call_target="tpu_custom_call" | custom-call | tf_op jit(solution)/shard_map/locate/pallas_call | solution.py:112
  18.1 9.6 %all-to-all-done = bf16[64,32,128]{2,1,0:T(8,128)(2,1)S(1)} async-done(((bf16[64,32,128]{2,1,0:T(8,128)(2,1)}), bf16[64,32,128]{2,1,0:T(8,128)(2,1)S(1)}, u32[]{:S(2)}, u32[]{:S(2)}) %all-to-all-start) | async-done | bytes 524320 | tf_op jit(solution)/shard_map/all_to_all | solution.py:343
  27.7 0.0 collective-permute-done.1.refs_4_
  27.7 0.0 collective-permute-done.2.refs_5_
  27.7 0.0 collective-permute-done.3.refs_6_
  27.7 0.0 collective-permute-done.4.refs_7_
  27.7 0.0 copy-start
  27.7 0.0 copy-start.1
  27.7 24.7 %attend.1 = bf16[4,16,40,128]{3,2,1,0:T(8,128)(2,1)} custom-call(s32[24]{0:T(128)S(1)} %locate.1.info, bf16[4,8,64,128]{3,2,1,0:T(8,128)(2,1)S(1)} %bitcast.2, bf16[1024,1024]{1,0:T(8,128)(2,1)} %refs_0_.1, bf16[1024,1024]{1,0:T(8,128)(2,1)} %refs_1_, bf16[4,256,1024]{2,1,0:T(8,128)(2,1)} %refs_2_, bf16[4,256,1024]{2,1,0:T(8,128)(2,1)} %refs_3_, ...), custom_call_target="tpu_custom_call" | custom-call | tf_op jit(solution)/shard_map/attend/pallas_call | solution.py:248
  52.4 4.7 %all-to-all-start.1 = ((bf16[64,40,128]{2,1,0:T(8,128)(2,1)}), bf16[64,40,128]{2,1,0:T(8,128)(2,1)S(1)}, u32[]{:S(2)}, u32[]{:S(2)}) async-start(bf16[64,40,128]{2,1,0:T(8,128)(2,1)} %bitcast.1), calls=%async_computation.1 | async-start | bytes 1310720 | tf_op jit(solution)/shard_map/all_to_all | solution.py:343
  57.1 0.0 copy-done
  57.1 0.0 copy-done.1
  57.1 0.1 new_tokens.1
  57.2 13.6 %all-to-all-done.1.parts_ref = bf16[64,40,128]{2,1,0:T(8,128)(2,1)S(1)} async-done(((bf16[64,40,128]{2,1,0:T(8,128)(2,1)}), bf16[64,40,128]{2,1,0:T(8,128)(2,1)S(1)}, u32[]{:S(2)}, u32[]{:S(2)}) %all-to-all-start.1) | async-done | bytes 655392 | tf_op jit(solution)/shard_map/all_to_all | solution.py:343
  70.8 1.2 %merge.1 = bf16[4,2,512]{2,1,0:T(2,128)(2,1)} custom-call(bf16[64,40,128]{2,1,0:T(8,128)(2,1)S(1)} %all-to-all-done.1.parts_ref, f32[2,4,8,128]{3,2,1,0:T(8,128)S(1)} %get-tuple-element.31.score_ref, f32[2,4,8,128]{3,2,1,0:T(8,128)S(1)} %get-tuple-element.32.value_ref), custom_call_target="tpu_custom_call" | custom-call | tf_op jit(solution)/shard_map/merge/pallas_call | solution.py:331
Async XLA Ops:
  1.5 26.1 %collective-permute-start.1 = (bf16[1024,1024]{1,0:T(8,128)(2,1)}, bf16[1024,1024]{1,0:T(8,128)(2,1)S(1)}, u32[]{:S(2)}, u32[]{:S(2)}) collective-permute-start(bf16[1024,1024]{1,0:T(8,128)(2,1)} %refs_0_.1), channel_id=1, source_target_pairs={{0,16},{16,0},{1,17},{17,1},{2,18},{18,2},{3,19},{19,3},{4,20},{20... | collective-permute-start | bytes 6291464 | tf_op jit(solution)/shard_map/ppermute | solution.py:366
  1.5 26.1 %collective-permute-start.2 = (bf16[1024,1024]{1,0:T(8,128)(2,1)}, bf16[1024,1024]{1,0:T(8,128)(2,1)}, u32[]{:S(2)}, u32[]{:S(2)}) collective-permute-start(bf16[1024,1024]{1,0:T(8,128)(2,1)} %refs_1_), channel_id=1, source_target_pairs={{0,16},{16,0},{1,17},{17,1},{2,18},{18,2},{3,19},{19,3},{4,20},{20... | collective-permute-start | bytes 6291464 | tf_op jit(solution)/shard_map/ppermute | solution.py:366
  2.0 25.6 %collective-permute-start.3 = (bf16[4,256,1024]{2,1,0:T(8,128)(2,1)}, bf16[4,256,1024]{2,1,0:T(8,128)(2,1)}, u32[]{:S(2)}, u32[]{:S(2)}) collective-permute-start(bf16[4,256,1024]{2,1,0:T(8,128)(2,1)} %refs_2_), channel_id=1, source_target_pairs={{0,16},{16,0},{1,17},{17,1},{2,18},{18,2},{3,19},{19,3},{4,20},{20... | collective-permute-start | bytes 6291464 | tf_op jit(solution)/shard_map/ppermute | solution.py:366
  2.1 25.6 %collective-permute-start.4 = (bf16[4,256,1024]{2,1,0:T(8,128)(2,1)}, bf16[4,256,1024]{2,1,0:T(8,128)(2,1)}, u32[]{:S(2)}, u32[]{:S(2)}) collective-permute-start(bf16[4,256,1024]{2,1,0:T(8,128)(2,1)} %refs_3_), channel_id=1, source_target_pairs={{0,16},{16,0},{1,17},{17,1},{2,18},{18,2},{3,19},{19,3},{4,20},{20... | collective-permute-start | bytes 6291464 | tf_op jit(solution)/shard_map/ppermute | solution.py:366
  2.6 25.1 %all-to-all-start = ((bf16[64,32,128]{2,1,0:T(8,128)(2,1)}), bf16[64,32,128]{2,1,0:T(8,128)(2,1)S(1)}, u32[]{:S(2)}, u32[]{:S(2)}) async-start(bf16[64,32,128]{2,1,0:T(8,128)(2,1)} %spread.1), calls=%async_computation | async-start | bytes 1048576 | tf_op jit(solution)/shard_map/all_to_all | solution.py:343
  14.1 1.3 %collective-permute-start = (s32[4]{0:T(128)}, s32[4]{0:T(128)S(1)}, u32[]{:S(2)}, u32[]{:S(2)}) collective-permute-start(s32[4]{0:T(128)} %refs_0_), channel_id=1, source_target_pairs={{0,16},{16,0},{1,17},{17,1},{2,18},{18,2},{3,19},{19,3},{4,20},{20... | collective-permute-start | bytes 56 | tf_op jit(solution)/shard_map/ppermute | solution.py:367
  15.4 0.7 copy-start.2
  16.1 0.7 copy-start.3
  27.7 29.4 %copy-start = (bf16[4,2,512]{2,1,0:T(2,128)(2,1)S(1)}, bf16[4,2,512]{2,1,0:T(2,128)(2,1)}, u32[]{:S(2)}) copy-start(bf16[4,2,512]{2,1,0:T(2,128)(2,1)} %q_ref.2) | copy-start | bytes 24580
  27.7 29.4 %copy-start.1 = (bf16[4,2,2,1024]{3,2,1,0:T(2,128)(2,1)S(1)}, bf16[4,2,2,1024]{3,2,1,0:T(2,128)(2,1)}, u32[]{:S(2)}) copy-start(bf16[4,2,2,1024]{3,2,1,0:T(2,128)(2,1)} %new_ref) | copy-start | bytes 98308
  52.4 18.4 %all-to-all-start.1 = ((bf16[64,40,128]{2,1,0:T(8,128)(2,1)}), bf16[64,40,128]{2,1,0:T(8,128)(2,1)S(1)}, u32[]{:S(2)}, u32[]{:S(2)}) async-start(bf16[64,40,128]{2,1,0:T(8,128)(2,1)} %bitcast.1), calls=%async_computation.1 | async-start | bytes 1310720 | tf_op jit(solution)/shard_map/all_to_all | solution.py:343

commit v10 on v6

--- a/solution.py
+++ b/solution.py
@@ -149,7 +149,7 @@
 
     own_top[...] = jnp.full(own_top.shape, LOWEST, jnp.float32)
     own_acc[...] = jnp.zeros(own_acc.shape, jnp.float32)
-    position = iota((halves * 8, span), 1)
+    position = iota((heads * halves * 8, span), 1)
 
     def cut(i):
         return slice(i * HEAD, (i + 1) * HEAD)
@@ -173,24 +173,31 @@
             q_ref[:, i] = x.reshape((layers,) + q_ref.shape[2:])
         found = []
         total = sides * slots
+        size = halves * 8
+        none = jnp.zeros((size, HEAD), jnp.float32)
         for j in range(total):
             layer, row, live = info[j], info[total + j], info[2 * total + j]
             sk_ref, sv_ref = held[4 * (j // slots) + 2 : 4 * (j // slots) + 4]
+            stacked = []
             for i in range(heads):
-                q = q_ref[jnp.minimum(layer, layers - 1), i, :, row]
-                q = q.reshape(halves * 8, HEAD).astype(jnp.bfloat16)
-                own = dot(q, sk_ref[pair, j % slots, :, cut(i)], NT) * SCALE
-                own = jnp.where(position < live, own, LOWEST)
-                peak = jnp.max(own, axis=1, keepdims=True)
-                peak = jnp.broadcast_to(as_bf16(peak), (halves * 8, HEAD))
-                shift = jnp.concatenate([peak] * (span // HEAD), axis=1)
-                weights = jnp.exp2(own - shift).astype(jnp.bfloat16)
-                values = sv_ref[pair, j % slots, :, cut(i)]
-                values = jnp.concatenate([values, ones[:span]], axis=1)
-                found.append((layer, i, row, peak, dot(weights, values, NN)))
-        for layer, i, row, peak, summed in found:
-            own_top[layer, i, :, row] = peak.reshape(halves, 8, HEAD)
-            own_acc[layer, i, :, row] = summed.reshape(halves, 8, 2 * HEAD)
+                q = q_ref[jnp.minimum(layer, layers - 1), i, :, row].reshape(size, HEAD)
+                stacked.append(jnp.concatenate([q if n == i else none for n in range(heads)], axis=1))
+            q = jnp.concatenate(stacked, axis=0).astype(jnp.bfloat16)
+            own = dot(q, sk_ref[pair, j % slots], NT) * SCALE
+            own = jnp.where(position < live, own, LOWEST)
+            peak = jnp.max(own, axis=1, keepdims=True)
+            peak = jnp.broadcast_to(as_bf16(peak), (heads * size, HEAD))
+            shift = jnp.concatenate([peak] * (span // HEAD), axis=1)
+            weights = jnp.exp2(own - shift).astype(jnp.bfloat16)
+            found.append((layer, row, peak, weights, dot(weights, sv_ref[pair, j % slots], NN)))
+        sums = dot(jnp.concatenate([x[3] for x in found], axis=0), ones[:span], NN)
+        for j, (layer, row, peak, _, summed) in enumerate(found):
+            for i in range(heads):
+                at = slice(i * size, (i + 1) * size)
+                total_at = slice((j * heads + i) * size, (j * heads + i + 1) * size)
+                state = jnp.concatenate([summed[at, cut(i)], sums[total_at]], axis=1)
+                own_top[layer, i, :, row] = peak[at].reshape(halves, 8, HEAD)
+                own_acc[layer, i, :, row] = state.reshape(halves, 8, 2 * HEAD)
 
         for number, (i, c) in enumerate(items):
             later = scored(*items[number + 1]) if number + 1 < len(items) else None

time: 60.4 us -> 65.6 us (1.086)
  Pallas kernels: 17 us -> 22.2 us
    pallas_call x1, Pallas kernels: 12.7 us -> 17.9 us  [attend(): pl.pallas_call(functools.partial(attend_kernel, sides=len(caches), heads=...]
where the time goes in v10:
time: 65.6 us; the launch traced here: 65.3 us
  waiting for transfers between devices  24.4 us (37%)
  Pallas kernels  22.2 us (34%)
  starting transfers between devices  17.3 us (26%)
  local copies, waits for them, and re-layouts  1.32 us (2%)
    all_to_all x2, waiting for transfers between devices, exchange(): return lax.all_to_all(x, axes, split_axis=0, concat_axis=0, tiled=True)  23.2 us
    pallas_call x1, Pallas kernels, attend(): pl.pallas_call(functools.partial(attend_kernel, sides=len(caches), heads=...  17.9 us
    all_to_all x2, starting transfers between devices, exchange(): return lax.all_to_all(x, axes, split_axis=0, concat_axis=0, tiled=True)  16.2 us
    pallas_call x1, Pallas kernels, spread(): pl.pallas_call(spread_kernel, out_shape=jax.ShapeDtypeStruct((copies, que...  1.54 us
    pallas_call x1, Pallas kernels, locate(): pl.pallas_call(functools.partial(locate_kernel, span=span), in_specs=[sme...  1.4 us
    unnamed x8, local copies, waits for them, and re-layouts  1.32 us
  transfers between devices with their start and end apart: 7, of which 3 were waited for; matrix products, arithmetic and copies ran while one was open for 0% of the time, Pallas kernels for 5%

profile of v10, /device:TPU:0, one launch (start us, length us, event | category | flops | bytes accessed | tf_op | source)
XLA Modules:
  0.0 65.3 jit_solution(11504142849004808309)
XLA Ops:
  0.0 0.0 collective-permute-start.1
  0.0 0.5 collective-permute-start.2
  0.5 0.0 collective-permute-start.3
  0.5 0.5 collective-permute-start.4
  1.0 1.5 %spread.1 = bf16[64,32,128]{2,1,0:T(8,128)(2,1)} custom-call(bf16[4,2,512]{2,1,0:T(2,128)(2,1)} %q_ref.2), custom_call_target="tpu_custom_call" | custom-call | tf_op jit(solution)/shard_map/spread/pallas_call | solution.py:79
  2.6 11.5 %all-to-all-start = ((bf16[64,32,128]{2,1,0:T(8,128)(2,1)}), bf16[64,32,128]{2,1,0:T(8,128)(2,1)S(1)}, u32[]{:S(2)}, u32[]{:S(2)}) async-start(bf16[64,32,128]{2,1,0:T(8,128)(2,1)} %spread.1), calls=%async_computation | async-start | bytes 1048576 | tf_op jit(solution)/shard_map/all_to_all | solution.py:341
  14.1 0.1 collective-permute-start
  14.2 1.2 %collective-permute-done.refs_1_ = s32[4]{0:T(128)S(1)} collective-permute-done((s32[4]{0:T(128)}, s32[4]{0:T(128)S(1)}, u32[]{:S(2)}, u32[]{:S(2)}) %collective-permute-start) | collective-permute-done | bytes 48 | tf_op jit(solution)/shard_map/ppermute | solution.py:363
  15.4 0.0 copy-start.2
  15.4 0.7 %copy-done.2 = s32[32]{0:T(128)S(1)} copy-done((s32[32]{0:T(128)S(1)}, s32[32]{0:T(128)}, u32[]{:S(2)}) %copy-start.2) | copy-done | bytes 152
  16.1 0.0 copy-start.3
  16.1 0.7 %copy-done.3 = s32[4]{0:T(128)S(1)} copy-done((s32[4]{0:T(128)S(1)}, s32[4]{0:T(128)}, u32[]{:S(2)}) %copy-start.3) | copy-done | bytes 40
  16.7 1.4 %locate.1.info = s32[24]{0:T(128)S(1)} custom-call(s32[32]{0:T(128)S(1)} %copy-done.2, s32[4]{0:T(128)S(1)} %copy-done.3, s32[4]{0:T(128)S(1)} %collective-permute-done.refs_1_), custom_call_target="tpu_custom_call" | custom-call | tf_op jit(solution)/shard_map/locate/pallas_call | solution.py:112
  18.1 9.6 %all-to-all-done = bf16[64,32,128]{2,1,0:T(8,128)(2,1)S(1)} async-done(((bf16[64,32,128]{2,1,0:T(8,128)(2,1)}), bf16[64,32,128]{2,1,0:T(8,128)(2,1)S(1)}, u32[]{:S(2)}, u32[]{:S(2)}) %all-to-all-start) | async-done | bytes 524320 | tf_op jit(solution)/shard_map/all_to_all | solution.py:341
  27.7 0.0 collective-permute-done.1.refs_4_
  27.7 0.0 collective-permute-done.2.refs_5_
  27.7 0.0 collective-permute-done.3.refs_6_
  27.7 0.0 collective-permute-done.4.refs_7_
  27.7 0.0 copy-start
  27.7 0.0 copy-start.1
  27.7 17.9 %attend.1 = bf16[4,16,40,128]{3,2,1,0:T(8,128)(2,1)} custom-call(s32[24]{0:T(128)S(1)} %locate.1.info, bf16[4,8,64,128]{3,2,1,0:T(8,128)(2,1)S(1)} %bitcast.2, bf16[1024,1024]{1,0:T(8,128)(2,1)} %refs_0_.3, bf16[1024,1024]{1,0:T(8,128)(2,1)} %refs_1_.1, bf16[4,256,1024]{2,1,0:T(8,128)(2,1)} %refs_2_.1, bf16[4,256,1024]{2,1,0:T(8,128)(2,1)} %refs_3_.1, ...), custom_call_target="tpu_custom_call" | custom-call | tf_op jit(solution)/shard_map/attend/pallas_call | solution.py:246
  45.7 4.7 %all-to-all-start.1 = ((bf16[64,40,128]{2,1,0:T(8,128)(2,1)}), bf16[64,40,128]{2,1,0:T(8,128)(2,1)S(1)}, u32[]{:S(2)}, u32[]{:S(2)}) async-start(bf16[64,40,128]{2,1,0:T(8,128)(2,1)} %bitcast.1), calls=%async_computation.1 | async-start | bytes 1310720 | tf_op jit(solution)/shard_map/all_to_all | solution.py:341
  50.3 0.0 copy-done
  50.3 0.0 copy-done.1
  50.3 0.1 new_tokens.1
  50.5 13.6 %all-to-all-done.1.parts_ref = bf16[64,40,128]{2,1,0:T(8,128)(2,1)S(1)} async-done(((bf16[64,40,128]{2,1,0:T(8,128)(2,1)}), bf16[64,40,128]{2,1,0:T(8,128)(2,1)S(1)}, u32[]{:S(2)}, u32[]{:S(2)}) %all-to-all-start.1) | async-done | bytes 655392 | tf_op jit(solution)/shard_map/all_to_all | solution.py:341
  64.1 1.2 %merge.1 = bf16[4,2,512]{2,1,0:T(2,128)(2,1)} custom-call(bf16[64,40,128]{2,1,0:T(8,128)(2,1)S(1)} %all-to-all-done.1.parts_ref, f32[2,4,8,128]{3,2,1,0:T(8,128)S(1)} %get-tuple-element.21.score_ref, f32[2,4,8,128]{3,2,1,0:T(8,128)S(1)} %get-tuple-element.22.value_ref), custom_call_target="tpu_custom_call" | custom-call | tf_op jit(solution)/shard_map/merge/pallas_call | solution.py:329
Async XLA Ops:
  0.0 27.7 %collective-permute-start.1 = (bf16[1024,1024]{1,0:T(8,128)(2,1)}, bf16[1024,1024]{1,0:T(8,128)(2,1)S(1)}, u32[]{:S(2)}, u32[]{:S(2)}) collective-permute-start(bf16[1024,1024]{1,0:T(8,128)(2,1)} %refs_0_.3), channel_id=1, source_target_pairs={{0,16},{16,0},{1,17},{17,1},{2,18},{18,2},{3,19},{19,3},{4,20},{20... | collective-permute-start | bytes 6291464 | tf_op jit(solution)/shard_map/ppermute | solution.py:361
  0.0 27.7 %collective-permute-start.2 = (bf16[1024,1024]{1,0:T(8,128)(2,1)}, bf16[1024,1024]{1,0:T(8,128)(2,1)}, u32[]{:S(2)}, u32[]{:S(2)}) collective-permute-start(bf16[1024,1024]{1,0:T(8,128)(2,1)} %refs_1_.1), channel_id=1, source_target_pairs={{0,16},{16,0},{1,17},{17,1},{2,18},{18,2},{3,19},{19,3},{4,20},{20... | collective-permute-start | bytes 6291464 | tf_op jit(solution)/shard_map/ppermute | solution.py:361
  0.5 27.2 %collective-permute-start.3 = (bf16[4,256,1024]{2,1,0:T(8,128)(2,1)}, bf16[4,256,1024]{2,1,0:T(8,128)(2,1)}, u32[]{:S(2)}, u32[]{:S(2)}) collective-permute-start(bf16[4,256,1024]{2,1,0:T(8,128)(2,1)} %refs_2_.1), channel_id=1, source_target_pairs={{0,16},{16,0},{1,17},{17,1},{2,18},{18,2},{3,19},{19,3},{4,20},{20... | collective-permute-start | bytes 6291464 | tf_op jit(solution)/shard_map/ppermute | solution.py:361
  0.5 27.2 %collective-permute-start.4 = (bf16[4,256,1024]{2,1,0:T(8,128)(2,1)}, bf16[4,256,1024]{2,1,0:T(8,128)(2,1)}, u32[]{:S(2)}, u32[]{:S(2)}) collective-permute-start(bf16[4,256,1024]{2,1,0:T(8,128)(2,1)} %refs_3_.1), channel_id=1, source_target_pairs={{0,16},{16,0},{1,17},{17,1},{2,18},{18,2},{3,19},{19,3},{4,20},{20... | collective-permute-start | bytes 6291464 | tf_op jit(solution)/shard_map/ppermute | solution.py:361
  2.6 25.1 %all-to-all-start = ((bf16[64,32,128]{2,1,0:T(8,128)(2,1)}), bf16[64,32,128]{2,1,0:T(8,128)(2,1)S(1)}, u32[]{:S(2)}, u32[]{:S(2)}) async-start(bf16[64,32,128]{2,1,0:T(8,128)(2,1)} %spread.1), calls=%async_computation | async-start | bytes 1048576 | tf_op jit(solution)/shard_map/all_to_all | solution.py:341
  14.1 1.3 %collective-permute-start = (s32[4]{0:T(128)}, s32[4]{0:T(128)S(1)}, u32[]{:S(2)}, u32[]{:S(2)}) collective-permute-start(s32[4]{0:T(128)} %refs_0_.2), channel_id=1, source_target_pairs={{0,16},{16,0},{1,17},{17,1},{2,18},{18,2},{3,19},{19,3},{4,20},{20... | collective-permute-start | bytes 56 | tf_op jit(solution)/shard_map/ppermute | solution.py:363
  15.4 0.7 %copy-start.2 = (s32[32]{0:T(128)S(1)}, s32[32]{0:T(128)}, u32[]{:S(2)}) copy-start(s32[32]{0:T(128)} %slot_ref) | copy-start | bytes 388
  16.1 0.7 %copy-start.3 = (s32[4]{0:T(128)S(1)}, s32[4]{0:T(128)}, u32[]{:S(2)}) copy-start(s32[4]{0:T(128)} %refs_0_.2) | copy-start | bytes 52
  27.7 22.6 %copy-start = (bf16[4,2,512]{2,1,0:T(2,128)(2,1)S(1)}, bf16[4,2,512]{2,1,0:T(2,128)(2,1)}, u32[]{:S(2)}) copy-start(bf16[4,2,512]{2,1,0:T(2,128)(2,1)} %q_ref.2) | copy-start | bytes 24580
  27.7 22.6 %copy-start.1 = (bf16[4,2,2,1024]{3,2,1,0:T(2,128)(2,1)S(1)}, bf16[4,2,2,1024]{3,2,1,0:T(2,128)(2,1)}, u32[]{:S(2)}) copy-start(bf16[4,2,2,1024]{3,2,1,0:T(2,128)(2,1)} %new_ref) | copy-start | bytes 98308
  45.7 18.4 %all-to-all-start.1 = ((bf16[64,40,128]{2,1,0:T(8,128)(2,1)}), bf16[64,40,128]{2,1,0:T(8,128)(2,1)S(1)}, u32[]{:S(2)}, u32[]{:S(2)}) async-start(bf16[64,40,128]{2,1,0:T(8,128)(2,1)} %bitcast.1), calls=%async_computation.1 | async-start | bytes 1310720 | tf_op jit(solution)/shard_map/all_to_all | solution.py:341

commit v11 on v10

--- a/solution.py
+++ b/solution.py
@@ -189,15 +189,14 @@
             peak = jnp.broadcast_to(as_bf16(peak), (heads * size, HEAD))
             shift = jnp.concatenate([peak] * (span // HEAD), axis=1)
             weights = jnp.exp2(own - shift).astype(jnp.bfloat16)
-            found.append((layer, row, peak, weights, dot(weights, sv_ref[pair, j % slots], NN)))
-        sums = dot(jnp.concatenate([x[3] for x in found], axis=0), ones[:span], NN)
-        for j, (layer, row, peak, _, summed) in enumerate(found):
             for i in range(heads):
                 at = slice(i * size, (i + 1) * size)
-                total_at = slice((j * heads + i) * size, (j * heads + i + 1) * size)
-                state = jnp.concatenate([summed[at, cut(i)], sums[total_at]], axis=1)
-                own_top[layer, i, :, row] = peak[at].reshape(halves, 8, HEAD)
-                own_acc[layer, i, :, row] = state.reshape(halves, 8, 2 * HEAD)
+                values = sv_ref[pair, j % slots, :, cut(i)]
+                values = jnp.concatenate([values, ones[:span]], axis=1)
+                found.append((layer, i, row, peak[at], dot(weights[at], values, NN)))
+        for layer, i, row, peak, summed in found:
+            own_top[layer, i, :, row] = peak.reshape(halves, 8, HEAD)
+            own_acc[layer, i, :, row] = summed.reshape(halves, 8, 2 * HEAD)
 
         for number, (i, c) in enumerate(items):
             later = scored(*items[number + 1]) if number + 1 < len(items) else None
@@ -357,10 +356,13 @@
     chips = layers * members
     swap = [(i, (i + 1) % cores) for i in range(cores)]
 
+    far_lengths = lax.ppermute(suffix_lengths, "core", swap)
+    far_lengths, suffix_keys, suffix_values = lax.optimization_barrier(
+        (far_lengths, suffix_keys, suffix_values)
+    )
     own = (prefix_keys, prefix_values, suffix_keys, suffix_values)
     far = tuple(lax.ppermute(x, "core", swap) for x in own)
     own = tuple(pltpu.with_memory_space_constraint(x, pltpu.HBM) for x in own)
-    far_lengths = lax.ppermute(suffix_lengths, "core", swap)
 
     blocks, row_slot = lax.optimization_barrier((spread(queries, chips), row_slot))
     near = exchange(blocks, CHIPS)

time: 65.6 us -> 61.7 us (0.941)
  Pallas kernels: 22.2 us -> 17.1 us
  waiting for transfers between devices: 24.4 us -> 25.7 us
    pallas_call x1, Pallas kernels: 17.9 us -> 12.8 us  [attend(): pl.pallas_call(functools.partial(attend_kernel, sides=len(caches), heads=...]
    all_to_all x2, waiting for transfers between devices: 23.2 us -> 24.9 us  [exchange(): return lax.all_to_all(x, axes, split_axis=0, concat_axis=0, tiled=True)]
where the time goes in v11:
time: 61.7 us; the launch traced here: 61.3 us
  waiting for transfers between devices  25.7 us (42%)
  starting transfers between devices  17.2 us (28%)
  Pallas kernels  17.1 us (28%)
  local copies, waits for them, and re-layouts  1.32 us (2%)
    all_to_all x2, waiting for transfers between devices, exchange(): return lax.all_to_all(x, axes, split_axis=0, concat_axis=0, tiled=True)  24.9 us
    all_to_all x2, starting transfers between devices, exchange(): return lax.all_to_all(x, axes, split_axis=0, concat_axis=0, tiled=True)  16.2 us
    pallas_call x1, Pallas kernels, attend(): pl.pallas_call(functools.partial(attend_kernel, sides=len(caches), heads=...  12.8 us
    pallas_call x1, Pallas kernels, spread(): pl.pallas_call(spread_kernel, out_shape=jax.ShapeDtypeStruct((copies, que...  1.54 us
    pallas_call x1, Pallas kernels, locate(): pl.pallas_call(functools.partial(locate_kernel, span=span), in_specs=[sme...  1.4 us
    unnamed x8, local copies, waits for them, and re-layouts  1.32 us
  transfers between devices with their start and end apart: 7, of which 3 were waited for; matrix products, arithmetic and copies ran while one was open for 0% of the time, Pallas kernels for 5%

profile of v11, /device:TPU:0, one launch (start us, length us, event | category | flops | bytes accessed | tf_op | source)
XLA Modules:
  0.0 61.3 jit_solution(10366425229170621143)
XLA Ops:
  0.0 0.0 collective-permute-start
  0.0 0.5 collective-permute-start.1
  0.5 0.0 collective-permute-start.2
  0.5 0.7 %collective-permute-done.refs_1_ = s32[4]{0:T(128)S(1)} collective-permute-done((s32[4]{0:T(128)}, s32[4]{0:T(128)S(1)}, u32[]{:S(2)}, u32[]{:S(2)}) %collective-permute-start) | collective-permute-done | bytes 48 | tf_op jit(solution)/shard_map/ppermute | solution.py:359
  1.3 0.2 collective-permute-start.3
  1.5 0.3 collective-permute-start.4
  1.8 1.5 %spread.1 = bf16[64,32,128]{2,1,0:T(8,128)(2,1)} custom-call(bf16[4,2,512]{2,1,0:T(2,128)(2,1)} %q_ref.2), custom_call_target="tpu_custom_call" | custom-call | tf_op jit(solution)/shard_map/spread/pallas_call | solution.py:79
  3.3 11.5 %all-to-all-start = ((bf16[64,32,128]{2,1,0:T(8,128)(2,1)}), bf16[64,32,128]{2,1,0:T(8,128)(2,1)S(1)}, u32[]{:S(2)}, u32[]{:S(2)}) async-start(bf16[64,32,128]{2,1,0:T(8,128)(2,1)} %spread.1), calls=%async_computation | async-start | bytes 1048576 | tf_op jit(solution)/shard_map/all_to_all | solution.py:340
  14.8 0.0 copy-start.2
  14.8 0.6 %copy-done.2 = s32[32]{0:T(128)S(1)} copy-done((s32[32]{0:T(128)S(1)}, s32[32]{0:T(128)}, u32[]{:S(2)}) %copy-start.2) | copy-done | bytes 152
  15.5 0.0 copy-start.3
  15.5 0.7 %copy-done.3 = s32[4]{0:T(128)S(1)} copy-done((s32[4]{0:T(128)S(1)}, s32[4]{0:T(128)}, u32[]{:S(2)}) %copy-start.3) | copy-done | bytes 40
  16.1 1.4 %locate.1.info = s32[24]{0:T(128)S(1)} custom-call(s32[32]{0:T(128)S(1)} %copy-done.2, s32[4]{0:T(128)S(1)} %copy-done.3, s32[4]{0:T(128)S(1)} %collective-permute-done.refs_1_), custom_call_target="tpu_custom_call" | custom-call | tf_op jit(solution)/shard_map/locate/pallas_call | solution.py:112
  17.5 11.1 %all-to-all-done = bf16[64,32,128]{2,1,0:T(8,128)(2,1)S(1)} async-done(((bf16[64,32,128]{2,1,0:T(8,128)(2,1)}), bf16[64,32,128]{2,1,0:T(8,128)(2,1)S(1)}, u32[]{:S(2)}, u32[]{:S(2)}) %all-to-all-start) | async-done | bytes 524320 | tf_op jit(solution)/shard_map/all_to_all | solution.py:340
  28.6 0.0 collective-permute-done.1.refs_4_
  28.6 0.0 collective-permute-done.2.refs_5_
  28.6 0.0 collective-permute-done.3.refs_6_
  28.6 0.0 collective-permute-done.4.refs_7_
  28.7 0.0 copy-start
  28.7 0.0 copy-start.1
  28.7 12.8 %attend.1 = bf16[4,16,40,128]{3,2,1,0:T(8,128)(2,1)} custom-call(s32[24]{0:T(128)S(1)} %locate.1.info, bf16[4,8,64,128]{3,2,1,0:T(8,128)(2,1)S(1)} %bitcast.2, bf16[1024,1024]{1,0:T(8,128)(2,1)} %refs_0_.3, bf16[1024,1024]{1,0:T(8,128)(2,1)} %refs_1_.1, bf16[4,256,1024]{2,1,0:T(8,128)(2,1)} %refs_2_, bf16[4,256,1024]{2,1,0:T(8,128)(2,1)} %refs_3_, ...), custom_call_target="tpu_custom_call" | custom-call | tf_op jit(solution)/shard_map/attend/pallas_call | solution.py:245
  41.5 4.7 %all-to-all-start.1 = ((bf16[64,40,128]{2,1,0:T(8,128)(2,1)}), bf16[64,40,128]{2,1,0:T(8,128)(2,1)S(1)}, u32[]{:S(2)}, u32[]{:S(2)}) async-start(bf16[64,40,128]{2,1,0:T(8,128)(2,1)} %bitcast.1), calls=%async_computation.1 | async-start | bytes 1310720 | tf_op jit(solution)/shard_map/all_to_all | solution.py:340
  46.1 0.0 copy-done
  46.2 0.0 copy-done.1
  46.2 0.1 new_tokens.1
  46.3 13.8 %all-to-all-done.1.parts_ref = bf16[64,40,128]{2,1,0:T(8,128)(2,1)S(1)} async-done(((bf16[64,40,128]{2,1,0:T(8,128)(2,1)}), bf16[64,40,128]{2,1,0:T(8,128)(2,1)S(1)}, u32[]{:S(2)}, u32[]{:S(2)}) %all-to-all-start.1) | async-done | bytes 655392 | tf_op jit(solution)/shard_map/all_to_all | solution.py:340
  60.1 1.2 %merge.1 = bf16[4,2,512]{2,1,0:T(2,128)(2,1)} custom-call(bf16[64,40,128]{2,1,0:T(8,128)(2,1)S(1)} %all-to-all-done.1.parts_ref, f32[2,4,8,128]{3,2,1,0:T(8,128)S(1)} %get-tuple-element.27.score_ref, f32[2,4,8,128]{3,2,1,0:T(8,128)S(1)} %get-tuple-element.28.value_ref), custom_call_target="tpu_custom_call" | custom-call | tf_op jit(solution)/shard_map/merge/pallas_call | solution.py:328
Async XLA Ops:
  0.0 1.3 %collective-permute-start = (s32[4]{0:T(128)}, s32[4]{0:T(128)S(1)}, u32[]{:S(2)}, u32[]{:S(2)}) collective-permute-start(s32[4]{0:T(128)} %refs_0_.2), channel_id=1, source_target_pairs={{0,16},{16,0},{1,17},{17,1},{2,18},{18,2},{3,19},{19,3},{4,20},{20... | collective-permute-start | bytes 56 | tf_op jit(solution)/shard_map/ppermute | solution.py:359
  0.0 28.6 %collective-permute-start.1 = (bf16[1024,1024]{1,0:T(8,128)(2,1)}, bf16[1024,1024]{1,0:T(8,128)(2,1)S(1)}, u32[]{:S(2)}, u32[]{:S(2)}) collective-permute-start(bf16[1024,1024]{1,0:T(8,128)(2,1)} %refs_0_.3), channel_id=1, source_target_pairs={{0,16},{16,0},{1,17},{17,1},{2,18},{18,2},{3,19},{19,3},{4,20},{20... | collective-permute-start | bytes 6291464 | tf_op jit(solution)/shard_map/ppermute | solution.py:364
  0.5 28.1 %collective-permute-start.2 = (bf16[1024,1024]{1,0:T(8,128)(2,1)}, bf16[1024,1024]{1,0:T(8,128)(2,1)}, u32[]{:S(2)}, u32[]{:S(2)}) collective-permute-start(bf16[1024,1024]{1,0:T(8,128)(2,1)} %refs_1_.1), channel_id=1, source_target_pairs={{0,16},{16,0},{1,17},{17,1},{2,18},{18,2},{3,19},{19,3},{4,20},{20... | collective-permute-start | bytes 6291464 | tf_op jit(solution)/shard_map/ppermute | solution.py:364
  1.3 27.4 %collective-permute-start.3 = (bf16[4,256,1024]{2,1,0:T(8,128)(2,1)}, bf16[4,256,1024]{2,1,0:T(8,128)(2,1)}, u32[]{:S(2)}, u32[]{:S(2)}) collective-permute-start(bf16[4,256,1024]{2,1,0:T(8,128)(2,1)} %refs_2_), channel_id=1, source_target_pairs={{0,16},{16,0},{1,17},{17,1},{2,18},{18,2},{3,19},{19,3},{4,20},{20... | collective-permute-start | bytes 6291464 | tf_op jit(solution)/shard_map/ppermute | solution.py:364
  1.5 27.2 %collective-permute-start.4 = (bf16[4,256,1024]{2,1,0:T(8,128)(2,1)}, bf16[4,256,1024]{2,1,0:T(8,128)(2,1)}, u32[]{:S(2)}, u32[]{:S(2)}) collective-permute-start(bf16[4,256,1024]{2,1,0:T(8,128)(2,1)} %refs_3_), channel_id=1, source_target_pairs={{0,16},{16,0},{1,17},{17,1},{2,18},{18,2},{3,19},{19,3},{4,20},{20... | collective-permute-start | bytes 6291464 | tf_op jit(solution)/shard_map/ppermute | solution.py:364
  3.3 25.3 %all-to-all-start = ((bf16[64,32,128]{2,1,0:T(8,128)(2,1)}), bf16[64,32,128]{2,1,0:T(8,128)(2,1)S(1)}, u32[]{:S(2)}, u32[]{:S(2)}) async-start(bf16[64,32,128]{2,1,0:T(8,128)(2,1)} %spread.1), calls=%async_computation | async-start | bytes 1048576 | tf_op jit(solution)/shard_map/all_to_all | solution.py:340
  14.8 0.7 %copy-start.2 = (s32[32]{0:T(128)S(1)}, s32[32]{0:T(128)}, u32[]{:S(2)}) copy-start(s32[32]{0:T(128)} %slot_ref) | copy-start | bytes 388
  15.5 0.7 %copy-start.3 = (s32[4]{0:T(128)S(1)}, s32[4]{0:T(128)}, u32[]{:S(2)}) copy-start(s32[4]{0:T(128)} %refs_0_.2) | copy-start | bytes 52
  28.7 17.5 %copy-start = (bf16[4,2,512]{2,1,0:T(2,128)(2,1)S(1)}, bf16[4,2,512]{2,1,0:T(2,128)(2,1)}, u32[]{:S(2)}) copy-start(bf16[4,2,512]{2,1,0:T(2,128)(2,1)} %q_ref.2) | copy-start | bytes 24580
  28.7 17.5 %copy-start.1 = (bf16[4,2,2,1024]{3,2,1,0:T(2,128)(2,1)S(1)}, bf16[4,2,2,1024]{3,2,1,0:T(2,128)(2,1)}, u32[]{:S(2)}) copy-start(bf16[4,2,2,1024]{3,2,1,0:T(2,128)(2,1)} %new_ref) | copy-start | bytes 98308
  41.5 18.6 %all-to-all-start.1 = ((bf16[64,40,128]{2,1,0:T(8,128)(2,1)}), bf16[64,40,128]{2,1,0:T(8,128)(2,1)S(1)}, u32[]{:S(2)}, u32[]{:S(2)}) async-start(bf16[64,40,128]{2,1,0:T(8,128)(2,1)} %bitcast.1), calls=%async_computation.1 | async-start | bytes 1310720 | tf_op jit(solution)/shard_map/all_to_all | solution.py:340

commit v12 on v6

--- a/solution.py
+++ b/solution.py
@@ -154,6 +154,9 @@
     def cut(i):
         return slice(i * HEAD, (i + 1) * HEAD)
 
+    def padded(x):
+        return jnp.concatenate([x, jnp.zeros_like(x)], axis=1)
+
     @pl.loop(0, pairs)
     def _(pair):
         for n in range(count):
@@ -162,8 +165,8 @@
 
         def scored(i, c):
             at = slice(c * per_chunk, (c + 1) * per_chunk)
-            q = near_ref[at, first + i].reshape(chunk, HEAD)
-            return [dot(q, held[4 * side][pair, :, cut(i)], NT) for side in range(sides)]
+            q = padded(near_ref[at, first + i].reshape(chunk, HEAD))
+            return [dot(q, padded(held[4 * side][pair, :, cut(i)]), NT) for side in range(sides)]
 
         items = [(i, c) for i in range(heads) for c in range(layers // per_chunk)]
         scores = scored(*items[0])
@@ -179,7 +182,7 @@
             for i in range(heads):
                 q = q_ref[jnp.minimum(layer, layers - 1), i, :, row]
                 q = q.reshape(halves * 8, HEAD).astype(jnp.bfloat16)
-                own = dot(q, sk_ref[pair, j % slots, :, cut(i)], NT) * SCALE
+                own = dot(padded(q), padded(sk_ref[pair, j % slots, :, cut(i)]), NT) * SCALE
                 own = jnp.where(position < live, own, LOWEST)
                 peak = jnp.max(own, axis=1, keepdims=True)
                 peak = jnp.broadcast_to(as_bf16(peak), (halves * 8, HEAD))

time: 60.4 us -> 60.4 us (level)
  no operation moved by 1% of the time
where the time goes in v12:
time: 60.4 us; the launch traced here: 60 us
  waiting for transfers between devices  24.4 us (40%)
  starting transfers between devices  17.3 us (29%)
  Pallas kernels  16.9 us (28%)
  local copies, waits for them, and re-layouts  1.32 us (2%)
    all_to_all x2, waiting for transfers between devices, exchange(): return lax.all_to_all(x, axes, split_axis=0, concat_axis=0, tiled=True)  23.2 us
    all_to_all x2, starting transfers between devices, exchange(): return lax.all_to_all(x, axes, split_axis=0, concat_axis=0, tiled=True)  16.2 us
    pallas_call x1, Pallas kernels, attend(): pl.pallas_call(functools.partial(attend_kernel, sides=len(caches), heads=...  12.7 us
    pallas_call x1, Pallas kernels, spread(): pl.pallas_call(spread_kernel, out_shape=jax.ShapeDtypeStruct((copies, que...  1.54 us
    pallas_call x1, Pallas kernels, locate(): pl.pallas_call(functools.partial(locate_kernel, span=span), in_specs=[sme...  1.4 us
    unnamed x8, local copies, waits for them, and re-layouts  1.32 us
    ppermute x1, waiting for transfers between devices, per_device(): far_lengths = lax.ppermute(suffix_lengths, 'core', swap)  1.24 us
    pallas_call x1, Pallas kernels, merge(): pl.pallas_call(merge_kernel, out_shape=jax.ShapeDtypeStruct(shape, jnp.bf...  1.22 us
  transfers between devices with their start and end apart: 7, of which 3 were waited for; matrix products, arithmetic and copies ran while one was open for 0% of the time, Pallas kernels for 5%

profile of v12, /device:TPU:0, one launch (start us, length us, event | category | flops | bytes accessed | tf_op | source)
XLA Modules:
  0.0 60.0 jit_solution(4241675441226684815)
XLA Ops:
  0.0 0.0 collective-permute-start.1
  0.0 0.5 collective-permute-start.2
  0.5 0.0 collective-permute-start.3
  0.5 0.5 collective-permute-start.4
  1.0 1.5 %spread.1 = bf16[64,32,128]{2,1,0:T(8,128)(2,1)} custom-call(bf16[4,2,512]{2,1,0:T(2,128)(2,1)} %q_ref.2), custom_call_target="tpu_custom_call" | custom-call | tf_op jit(solution)/shard_map/spread/pallas_call | solution.py:79
  2.6 11.5 %all-to-all-start = ((bf16[64,32,128]{2,1,0:T(8,128)(2,1)}), bf16[64,32,128]{2,1,0:T(8,128)(2,1)S(1)}, u32[]{:S(2)}, u32[]{:S(2)}) async-start(bf16[64,32,128]{2,1,0:T(8,128)(2,1)} %spread.1), calls=%async_computation | async-start | bytes 1048576 | tf_op jit(solution)/shard_map/all_to_all | solution.py:337
  14.1 0.1 collective-permute-start
  14.2 1.2 %collective-permute-done.refs_1_ = s32[4]{0:T(128)S(1)} collective-permute-done((s32[4]{0:T(128)}, s32[4]{0:T(128)S(1)}, u32[]{:S(2)}, u32[]{:S(2)}) %collective-permute-start) | collective-permute-done | bytes 48 | tf_op jit(solution)/shard_map/ppermute | solution.py:359
  15.4 0.0 copy-start.2
  15.4 0.7 %copy-done.2 = s32[32]{0:T(128)S(1)} copy-done((s32[32]{0:T(128)S(1)}, s32[32]{0:T(128)}, u32[]{:S(2)}) %copy-start.2) | copy-done | bytes 152
  16.1 0.0 copy-start.3
  16.1 0.7 %copy-done.3 = s32[4]{0:T(128)S(1)} copy-done((s32[4]{0:T(128)S(1)}, s32[4]{0:T(128)}, u32[]{:S(2)}) %copy-start.3) | copy-done | bytes 40
  16.7 1.4 %locate.1.info = s32[24]{0:T(128)S(1)} custom-call(s32[32]{0:T(128)S(1)} %copy-done.2, s32[4]{0:T(128)S(1)} %copy-done.3, s32[4]{0:T(128)S(1)} %collective-permute-done.refs_1_), custom_call_target="tpu_custom_call" | custom-call | tf_op jit(solution)/shard_map/locate/pallas_call | solution.py:112
  18.1 9.6 %all-to-all-done = bf16[64,32,128]{2,1,0:T(8,128)(2,1)S(1)} async-done(((bf16[64,32,128]{2,1,0:T(8,128)(2,1)}), bf16[64,32,128]{2,1,0:T(8,128)(2,1)S(1)}, u32[]{:S(2)}, u32[]{:S(2)}) %all-to-all-start) | async-done | bytes 524320 | tf_op jit(solution)/shard_map/all_to_all | solution.py:337
  27.7 0.0 collective-permute-done.1.refs_4_
  27.7 0.0 collective-permute-done.2.refs_5_
  27.7 0.0 collective-permute-done.3.refs_6_
  27.7 0.0 collective-permute-done.4.refs_7_
  27.7 0.0 copy-start
  27.7 0.0 copy-start.1
  27.7 12.7 %attend.1 = bf16[4,16,40,128]{3,2,1,0:T(8,128)(2,1)} custom-call(s32[24]{0:T(128)S(1)} %locate.1.info, bf16[4,8,64,128]{3,2,1,0:T(8,128)(2,1)S(1)} %bitcast.2, bf16[1024,1024]{1,0:T(8,128)(2,1)} %refs_0_.3, bf16[1024,1024]{1,0:T(8,128)(2,1)} %refs_1_.1, bf16[4,256,1024]{2,1,0:T(8,128)(2,1)} %refs_2_.1, bf16[4,256,1024]{2,1,0:T(8,128)(2,1)} %refs_3_.1, ...), custom_call_target="tpu_custom_call" | custom-call | tf_op jit(solution)/shard_map/attend/pallas_call | solution.py:242
  40.4 4.7 %all-to-all-start.1 = ((bf16[64,40,128]{2,1,0:T(8,128)(2,1)}), bf16[64,40,128]{2,1,0:T(8,128)(2,1)S(1)}, u32[]{:S(2)}, u32[]{:S(2)}) async-start(bf16[64,40,128]{2,1,0:T(8,128)(2,1)} %bitcast.1), calls=%async_computation.1 | async-start | bytes 1310720 | tf_op jit(solution)/shard_map/all_to_all | solution.py:337
  45.1 0.0 copy-done
  45.1 0.0 copy-done.1
  45.1 0.1 new_tokens.1
  45.2 13.6 %all-to-all-done.1.parts_ref = bf16[64,40,128]{2,1,0:T(8,128)(2,1)S(1)} async-done(((bf16[64,40,128]{2,1,0:T(8,128)(2,1)}), bf16[64,40,128]{2,1,0:T(8,128)(2,1)S(1)}, u32[]{:S(2)}, u32[]{:S(2)}) %all-to-all-start.1) | async-done | bytes 655392 | tf_op jit(solution)/shard_map/all_to_all | solution.py:337
  58.8 1.2 %merge.1 = bf16[4,2,512]{2,1,0:T(2,128)(2,1)} custom-call(bf16[64,40,128]{2,1,0:T(8,128)(2,1)S(1)} %all-to-all-done.1.parts_ref, f32[2,4,8,128]{3,2,1,0:T(8,128)S(1)} %get-tuple-element.21.score_ref, f32[2,4,8,128]{3,2,1,0:T(8,128)S(1)} %get-tuple-element.22.value_ref), custom_call_target="tpu_custom_call" | custom-call | tf_op jit(solution)/shard_map/merge/pallas_call | solution.py:325
Async XLA Ops:
  0.0 27.7 %collective-permute-start.1 = (bf16[1024,1024]{1,0:T(8,128)(2,1)}, bf16[1024,1024]{1,0:T(8,128)(2,1)S(1)}, u32[]{:S(2)}, u32[]{:S(2)}) collective-permute-start(bf16[1024,1024]{1,0:T(8,128)(2,1)} %refs_0_.3), channel_id=1, source_target_pairs={{0,16},{16,0},{1,17},{17,1},{2,18},{18,2},{3,19},{19,3},{4,20},{20... | collective-permute-start | bytes 6291464 | tf_op jit(solution)/shard_map/ppermute | solution.py:357
  0.0 27.7 %collective-permute-start.2 = (bf16[1024,1024]{1,0:T(8,128)(2,1)}, bf16[1024,1024]{1,0:T(8,128)(2,1)}, u32[]{:S(2)}, u32[]{:S(2)}) collective-permute-start(bf16[1024,1024]{1,0:T(8,128)(2,1)} %refs_1_.1), channel_id=1, source_target_pairs={{0,16},{16,0},{1,17},{17,1},{2,18},{18,2},{3,19},{19,3},{4,20},{20... | collective-permute-start | bytes 6291464 | tf_op jit(solution)/shard_map/ppermute | solution.py:357
  0.5 27.2 %collective-permute-start.3 = (bf16[4,256,1024]{2,1,0:T(8,128)(2,1)}, bf16[4,256,1024]{2,1,0:T(8,128)(2,1)}, u32[]{:S(2)}, u32[]{:S(2)}) collective-permute-start(bf16[4,256,1024]{2,1,0:T(8,128)(2,1)} %refs_2_.1), channel_id=1, source_target_pairs={{0,16},{16,0},{1,17},{17,1},{2,18},{18,2},{3,19},{19,3},{4,20},{20... | collective-permute-start | bytes 6291464 | tf_op jit(solution)/shard_map/ppermute | solution.py:357
  0.5 27.2 %collective-permute-start.4 = (bf16[4,256,1024]{2,1,0:T(8,128)(2,1)}, bf16[4,256,1024]{2,1,0:T(8,128)(2,1)}, u32[]{:S(2)}, u32[]{:S(2)}) collective-permute-start(bf16[4,256,1024]{2,1,0:T(8,128)(2,1)} %refs_3_.1), channel_id=1, source_target_pairs={{0,16},{16,0},{1,17},{17,1},{2,18},{18,2},{3,19},{19,3},{4,20},{20... | collective-permute-start | bytes 6291464 | tf_op jit(solution)/shard_map/ppermute | solution.py:357
  2.6 25.1 %all-to-all-start = ((bf16[64,32,128]{2,1,0:T(8,128)(2,1)}), bf16[64,32,128]{2,1,0:T(8,128)(2,1)S(1)}, u32[]{:S(2)}, u32[]{:S(2)}) async-start(bf16[64,32,128]{2,1,0:T(8,128)(2,1)} %spread.1), calls=%async_computation | async-start | bytes 1048576 | tf_op jit(solution)/shard_map/all_to_all | solution.py:337
  14.1 1.3 %collective-permute-start = (s32[4]{0:T(128)}, s32[4]{0:T(128)S(1)}, u32[]{:S(2)}, u32[]{:S(2)}) collective-permute-start(s32[4]{0:T(128)} %refs_0_.2), channel_id=1, source_target_pairs={{0,16},{16,0},{1,17},{17,1},{2,18},{18,2},{3,19},{19,3},{4,20},{20... | collective-permute-start | bytes 56 | tf_op jit(solution)/shard_map/ppermute | solution.py:359
  15.4 0.7 %copy-start.2 = (s32[32]{0:T(128)S(1)}, s32[32]{0:T(128)}, u32[]{:S(2)}) copy-start(s32[32]{0:T(128)} %slot_ref) | copy-start | bytes 388
  16.1 0.7 %copy-start.3 = (s32[4]{0:T(128)S(1)}, s32[4]{0:T(128)}, u32[]{:S(2)}) copy-start(s32[4]{0:T(128)} %refs_0_.2) | copy-start | bytes 52
  27.7 17.4 %copy-start = (bf16[4,2,512]{2,1,0:T(2,128)(2,1)S(1)}, bf16[4,2,512]{2,1,0:T(2,128)(2,1)}, u32[]{:S(2)}) copy-start(bf16[4,2,512]{2,1,0:T(2,128)(2,1)} %q_ref.2) | copy-start | bytes 24580
  27.7 17.4 %copy-start.1 = (bf16[4,2,2,1024]{3,2,1,0:T(2,128)(2,1)S(1)}, bf16[4,2,2,1024]{3,2,1,0:T(2,128)(2,1)}, u32[]{:S(2)}) copy-start(bf16[4,2,2,1024]{3,2,1,0:T(2,128)(2,1)} %new_ref) | copy-start | bytes 98308
  40.4 18.4 %all-to-all-start.1 = ((bf16[64,40,128]{2,1,0:T(8,128)(2,1)}), bf16[64,40,128]{2,1,0:T(8,128)(2,1)S(1)}, u32[]{:S(2)}, u32[]{:S(2)}) async-start(bf16[64,40,128]{2,1,0:T(8,128)(2,1)} %bitcast.1), calls=%async_computation.1 | async-start | bytes 1310720 | tf_op jit(solution)/shard_map/all_to_all | solution.py:337

commit v13 on v6

--- a/solution.py
+++ b/solution.py
@@ -181,7 +181,8 @@
                 q = q.reshape(halves * 8, HEAD).astype(jnp.bfloat16)
                 own = dot(q, sk_ref[pair, j % slots, :, cut(i)], NT) * SCALE
                 own = jnp.where(position < live, own, LOWEST)
-                peak = jnp.max(own, axis=1, keepdims=True)
+                peak = functools.reduce(jnp.maximum, columns(own))
+                peak = jnp.max(peak, axis=1, keepdims=True)
                 peak = jnp.broadcast_to(as_bf16(peak), (halves * 8, HEAD))
                 shift = jnp.concatenate([peak] * (span // HEAD), axis=1)
                 weights = jnp.exp2(own - shift).astype(jnp.bfloat16)
@@ -194,7 +195,8 @@
 
         for number, (i, c) in enumerate(items):
             later = scored(*items[number + 1]) if number + 1 < len(items) else None
-            peak = functools.reduce(jnp.maximum, [jnp.max(x, axis=1, keepdims=True) for x in scores])
+            peak = functools.reduce(jnp.maximum, [y for x in scores for y in columns(x)])
+            peak = jnp.max(peak, axis=1, keepdims=True)
             peak = jnp.broadcast_to(as_bf16(peak * SCALE), (chunk, HEAD))
             shift = jnp.concatenate([peak] * (length // HEAD), axis=1)
             summed = None

time: 60.4 us -> 60.5 us (level)
  no operation moved by 1% of the time
where the time goes in v13:
time: 60.5 us; the launch traced here: 60.1 us
  waiting for transfers between devices  24.4 us (40%)
  starting transfers between devices  17.3 us (29%)
  Pallas kernels  17.1 us (28%)
  local copies, waits for them, and re-layouts  1.32 us (2%)
    all_to_all x2, waiting for transfers between devices, exchange(): return lax.all_to_all(x, axes, split_axis=0, concat_axis=0, tiled=True)  23.2 us
    all_to_all x2, starting transfers between devices, exchange(): return lax.all_to_all(x, axes, split_axis=0, concat_axis=0, tiled=True)  16.2 us
    pallas_call x1, Pallas kernels, attend(): pl.pallas_call(functools.partial(attend_kernel, sides=len(caches), heads=...  12.8 us
    pallas_call x1, Pallas kernels, spread(): pl.pallas_call(spread_kernel, out_shape=jax.ShapeDtypeStruct((copies, que...  1.54 us
    pallas_call x1, Pallas kernels, locate(): pl.pallas_call(functools.partial(locate_kernel, span=span), in_specs=[sme...  1.4 us
    unnamed x8, local copies, waits for them, and re-layouts  1.32 us
    ppermute x1, waiting for transfers between devices, per_device(): far_lengths = lax.ppermute(suffix_lengths, 'core', swap)  1.24 us
    pallas_call x1, Pallas kernels, merge(): pl.pallas_call(merge_kernel, out_shape=jax.ShapeDtypeStruct(shape, jnp.bf...  1.22 us
  transfers between devices with their start and end apart: 7, of which 3 were waited for; matrix products, arithmetic and copies ran while one was open for 0% of the time, Pallas kernels for 5%

profile of v13, /device:TPU:0, one launch (start us, length us, event | category | flops | bytes accessed | tf_op | source)
XLA Modules:
  0.0 60.1 jit_solution(16173067804527713139)
XLA Ops:
  0.0 0.0 collective-permute-start.1
  0.0 0.5 collective-permute-start.2
  0.5 0.0 collective-permute-start.3
  0.5 0.5 collective-permute-start.4
  1.0 1.5 %spread.1 = bf16[64,32,128]{2,1,0:T(8,128)(2,1)} custom-call(bf16[4,2,512]{2,1,0:T(2,128)(2,1)} %q_ref.2), custom_call_target="tpu_custom_call" | custom-call | tf_op jit(solution)/shard_map/spread/pallas_call | solution.py:79
  2.6 11.5 %all-to-all-start = ((bf16[64,32,128]{2,1,0:T(8,128)(2,1)}), bf16[64,32,128]{2,1,0:T(8,128)(2,1)S(1)}, u32[]{:S(2)}, u32[]{:S(2)}) async-start(bf16[64,32,128]{2,1,0:T(8,128)(2,1)} %spread.1), calls=%async_computation | async-start | bytes 1048576 | tf_op jit(solution)/shard_map/all_to_all | solution.py:336
  14.1 0.1 collective-permute-start
  14.2 1.2 %collective-permute-done.refs_1_ = s32[4]{0:T(128)S(1)} collective-permute-done((s32[4]{0:T(128)}, s32[4]{0:T(128)S(1)}, u32[]{:S(2)}, u32[]{:S(2)}) %collective-permute-start) | collective-permute-done | bytes 48 | tf_op jit(solution)/shard_map/ppermute | solution.py:358
  15.4 0.0 copy-start.2
  15.4 0.7 %copy-done.2 = s32[32]{0:T(128)S(1)} copy-done((s32[32]{0:T(128)S(1)}, s32[32]{0:T(128)}, u32[]{:S(2)}) %copy-start.2) | copy-done | bytes 152
  16.1 0.0 copy-start.3
  16.1 0.7 %copy-done.3 = s32[4]{0:T(128)S(1)} copy-done((s32[4]{0:T(128)S(1)}, s32[4]{0:T(128)}, u32[]{:S(2)}) %copy-start.3) | copy-done | bytes 40
  16.7 1.4 %locate.1.info = s32[24]{0:T(128)S(1)} custom-call(s32[32]{0:T(128)S(1)} %copy-done.2, s32[4]{0:T(128)S(1)} %copy-done.3, s32[4]{0:T(128)S(1)} %collective-permute-done.refs_1_), custom_call_target="tpu_custom_call" | custom-call | tf_op jit(solution)/shard_map/locate/pallas_call | solution.py:112
  18.1 9.6 %all-to-all-done = bf16[64,32,128]{2,1,0:T(8,128)(2,1)S(1)} async-done(((bf16[64,32,128]{2,1,0:T(8,128)(2,1)}), bf16[64,32,128]{2,1,0:T(8,128)(2,1)S(1)}, u32[]{:S(2)}, u32[]{:S(2)}) %all-to-all-start) | async-done | bytes 524320 | tf_op jit(solution)/shard_map/all_to_all | solution.py:336
  27.7 0.0 collective-permute-done.1.refs_4_
  27.7 0.0 collective-permute-done.2.refs_5_
  27.7 0.0 collective-permute-done.3.refs_6_
  27.7 0.0 collective-permute-done.4.refs_7_
  27.7 0.0 copy-start
  27.7 0.0 copy-start.1
  27.7 12.8 %attend.1 = bf16[4,16,40,128]{3,2,1,0:T(8,128)(2,1)} custom-call(s32[24]{0:T(128)S(1)} %locate.1.info, bf16[4,8,64,128]{3,2,1,0:T(8,128)(2,1)S(1)} %bitcast.2, bf16[1024,1024]{1,0:T(8,128)(2,1)} %refs_0_.3, bf16[1024,1024]{1,0:T(8,128)(2,1)} %refs_1_.1, bf16[4,256,1024]{2,1,0:T(8,128)(2,1)} %refs_2_.1, bf16[4,256,1024]{2,1,0:T(8,128)(2,1)} %refs_3_.1, ...), custom_call_target="tpu_custom_call" | custom-call | tf_op jit(solution)/shard_map/attend/pallas_call | solution.py:241
  40.5 4.7 %all-to-all-start.1 = ((bf16[64,40,128]{2,1,0:T(8,128)(2,1)}), bf16[64,40,128]{2,1,0:T(8,128)(2,1)S(1)}, u32[]{:S(2)}, u32[]{:S(2)}) async-start(bf16[64,40,128]{2,1,0:T(8,128)(2,1)} %bitcast.1), calls=%async_computation.1 | async-start | bytes 1310720 | tf_op jit(solution)/shard_map/all_to_all | solution.py:336
  45.2 0.0 copy-done
  45.2 0.0 copy-done.1
  45.2 0.1 new_tokens.1
  45.3 13.6 %all-to-all-done.1.parts_ref = bf16[64,40,128]{2,1,0:T(8,128)(2,1)S(1)} async-done(((bf16[64,40,128]{2,1,0:T(8,128)(2,1)}), bf16[64,40,128]{2,1,0:T(8,128)(2,1)S(1)}, u32[]{:S(2)}, u32[]{:S(2)}) %all-to-all-start.1) | async-done | bytes 655392 | tf_op jit(solution)/shard_map/all_to_all | solution.py:336
  58.9 1.2 %merge.1 = bf16[4,2,512]{2,1,0:T(2,128)(2,1)} custom-call(bf16[64,40,128]{2,1,0:T(8,128)(2,1)S(1)} %all-to-all-done.1.parts_ref, f32[2,4,8,128]{3,2,1,0:T(8,128)S(1)} %get-tuple-element.21.score_ref, f32[2,4,8,128]{3,2,1,0:T(8,128)S(1)} %get-tuple-element.22.value_ref), custom_call_target="tpu_custom_call" | custom-call | tf_op jit(solution)/shard_map/merge/pallas_call | solution.py:324
Async XLA Ops:
  0.0 27.7 %collective-permute-start.1 = (bf16[1024,1024]{1,0:T(8,128)(2,1)}, bf16[1024,1024]{1,0:T(8,128)(2,1)S(1)}, u32[]{:S(2)}, u32[]{:S(2)}) collective-permute-start(bf16[1024,1024]{1,0:T(8,128)(2,1)} %refs_0_.3), channel_id=1, source_target_pairs={{0,16},{16,0},{1,17},{17,1},{2,18},{18,2},{3,19},{19,3},{4,20},{20... | collective-permute-start | bytes 6291464 | tf_op jit(solution)/shard_map/ppermute | solution.py:356
  0.0 27.7 %collective-permute-start.2 = (bf16[1024,1024]{1,0:T(8,128)(2,1)}, bf16[1024,1024]{1,0:T(8,128)(2,1)}, u32[]{:S(2)}, u32[]{:S(2)}) collective-permute-start(bf16[1024,1024]{1,0:T(8,128)(2,1)} %refs_1_.1), channel_id=1, source_target_pairs={{0,16},{16,0},{1,17},{17,1},{2,18},{18,2},{3,19},{19,3},{4,20},{20... | collective-permute-start | bytes 6291464 | tf_op jit(solution)/shard_map/ppermute | solution.py:356
  0.5 27.2 %collective-permute-start.3 = (bf16[4,256,1024]{2,1,0:T(8,128)(2,1)}, bf16[4,256,1024]{2,1,0:T(8,128)(2,1)}, u32[]{:S(2)}, u32[]{:S(2)}) collective-permute-start(bf16[4,256,1024]{2,1,0:T(8,128)(2,1)} %refs_2_.1), channel_id=1, source_target_pairs={{0,16},{16,0},{1,17},{17,1},{2,18},{18,2},{3,19},{19,3},{4,20},{20... | collective-permute-start | bytes 6291464 | tf_op jit(solution)/shard_map/ppermute | solution.py:356
  0.5 27.2 %collective-permute-start.4 = (bf16[4,256,1024]{2,1,0:T(8,128)(2,1)}, bf16[4,256,1024]{2,1,0:T(8,128)(2,1)}, u32[]{:S(2)}, u32[]{:S(2)}) collective-permute-start(bf16[4,256,1024]{2,1,0:T(8,128)(2,1)} %refs_3_.1), channel_id=1, source_target_pairs={{0,16},{16,0},{1,17},{17,1},{2,18},{18,2},{3,19},{19,3},{4,20},{20... | collective-permute-start | bytes 6291464 | tf_op jit(solution)/shard_map/ppermute | solution.py:356
  2.6 25.1 %all-to-all-start = ((bf16[64,32,128]{2,1,0:T(8,128)(2,1)}), bf16[64,32,128]{2,1,0:T(8,128)(2,1)S(1)}, u32[]{:S(2)}, u32[]{:S(2)}) async-start(bf16[64,32,128]{2,1,0:T(8,128)(2,1)} %spread.1), calls=%async_computation | async-start | bytes 1048576 | tf_op jit(solution)/shard_map/all_to_all | solution.py:336
  14.1 1.3 %collective-permute-start = (s32[4]{0:T(128)}, s32[4]{0:T(128)S(1)}, u32[]{:S(2)}, u32[]{:S(2)}) collective-permute-start(s32[4]{0:T(128)} %refs_0_.2), channel_id=1, source_target_pairs={{0,16},{16,0},{1,17},{17,1},{2,18},{18,2},{3,19},{19,3},{4,20},{20... | collective-permute-start | bytes 56 | tf_op jit(solution)/shard_map/ppermute | solution.py:358
  15.4 0.7 %copy-start.2 = (s32[32]{0:T(128)S(1)}, s32[32]{0:T(128)}, u32[]{:S(2)}) copy-start(s32[32]{0:T(128)} %slot_ref) | copy-start | bytes 388
  16.1 0.7 %copy-start.3 = (s32[4]{0:T(128)S(1)}, s32[4]{0:T(128)}, u32[]{:S(2)}) copy-start(s32[4]{0:T(128)} %refs_0_.2) | copy-start | bytes 52
  27.7 17.5 %copy-start = (bf16[4,2,512]{2,1,0:T(2,128)(2,1)S(1)}, bf16[4,2,512]{2,1,0:T(2,128)(2,1)}, u32[]{:S(2)}) copy-start(bf16[4,2,512]{2,1,0:T(2,128)(2,1)} %q_ref.2) | copy-start | bytes 24580
  27.7 17.5 %copy-start.1 = (bf16[4,2,2,1024]{3,2,1,0:T(2,128)(2,1)S(1)}, bf16[4,2,2,1024]{3,2,1,0:T(2,128)(2,1)}, u32[]{:S(2)}) copy-start(bf16[4,2,2,1024]{3,2,1,0:T(2,128)(2,1)} %new_ref) | copy-start | bytes 98308
  40.5 18.4 %all-to-all-start.1 = ((bf16[64,40,128]{2,1,0:T(8,128)(2,1)}), bf16[64,40,128]{2,1,0:T(8,128)(2,1)S(1)}, u32[]{:S(2)}, u32[]{:S(2)}) async-start(bf16[64,40,128]{2,1,0:T(8,128)(2,1)} %bitcast.1), calls=%async_computation.1 | async-start | bytes 1310720 | tf_op jit(solution)/shard_map/all_to_all | solution.py:336

commit v14 on v6

--- a/solution.py
+++ b/solution.py
@@ -163,7 +163,8 @@
         def scored(i, c):
             at = slice(c * per_chunk, (c + 1) * per_chunk)
             q = near_ref[at, first + i].reshape(chunk, HEAD)
-            return [dot(q, held[4 * side][pair, :, cut(i)], NT) for side in range(sides)]
+            keys = [held[4 * side][pair, :, cut(i)] for side in range(sides)]
+            return dot(q, jnp.concatenate(keys, axis=0), NT)
 
         items = [(i, c) for i in range(heads) for c in range(layers // per_chunk)]
         scores = scored(*items[0])
@@ -194,15 +195,15 @@
 
         for number, (i, c) in enumerate(items):
             later = scored(*items[number + 1]) if number + 1 < len(items) else None
-            peak = functools.reduce(jnp.maximum, [jnp.max(x, axis=1, keepdims=True) for x in scores])
+            peak = jnp.max(scores, axis=1, keepdims=True)
             peak = jnp.broadcast_to(as_bf16(peak * SCALE), (chunk, HEAD))
-            shift = jnp.concatenate([peak] * (length // HEAD), axis=1)
-            summed = None
-            for side, x in enumerate(scores):
-                weights = jnp.exp2(x * SCALE - shift).astype(jnp.bfloat16)
-                values = held[4 * side + 1][pair, :, cut(i)]
-                part = dot(weights, jnp.concatenate([values, ones], axis=1), NN)
-                summed = part if summed is None else summed + part
+            shift = jnp.concatenate([peak] * (sides * length // HEAD), axis=1)
+            weights = jnp.exp2(scores * SCALE - shift).astype(jnp.bfloat16)
+            values = [
+                jnp.concatenate([held[4 * side + 1][pair, :, cut(i)], ones], axis=1)
+                for side in range(sides)
+            ]
+            summed = dot(weights, jnp.concatenate(values, axis=0), NN)
             at = slice(c * per_chunk, (c + 1) * per_chunk)
             own = own_top[at, i].reshape(chunk, HEAD)
             carried = own_acc[at, i].reshape(chunk, 2 * HEAD)

time: 60.4 us -> 60.5 us (level)
  no operation moved by 1% of the time
where the time goes in v14:
time: 60.5 us; the launch traced here: 60.1 us
  waiting for transfers between devices  24.4 us (40%)
  starting transfers between devices  17.3 us (29%)
  Pallas kernels  17.1 us (28%)
  local copies, waits for them, and re-layouts  1.32 us (2%)
    all_to_all x2, waiting for transfers between devices, exchange(): return lax.all_to_all(x, axes, split_axis=0, concat_axis=0, tiled=True)  23.2 us
    all_to_all x2, starting transfers between devices, exchange(): return lax.all_to_all(x, axes, split_axis=0, concat_axis=0, tiled=True)  16.2 us
    pallas_call x1, Pallas kernels, attend(): pl.pallas_call(functools.partial(attend_kernel, sides=len(caches), heads=...  12.8 us
    pallas_call x1, Pallas kernels, spread(): pl.pallas_call(spread_kernel, out_shape=jax.ShapeDtypeStruct((copies, que...  1.54 us
    pallas_call x1, Pallas kernels, locate(): pl.pallas_call(functools.partial(locate_kernel, span=span), in_specs=[sme...  1.4 us
    unnamed x8, local copies, waits for them, and re-layouts  1.32 us
    ppermute x1, waiting for transfers between devices, per_device(): far_lengths = lax.ppermute(suffix_lengths, 'core', swap)  1.24 us
    pallas_call x1, Pallas kernels, merge(): pl.pallas_call(merge_kernel, out_shape=jax.ShapeDtypeStruct(shape, jnp.bf...  1.22 us
  transfers between devices with their start and end apart: 7, of which 3 were waited for; matrix products, arithmetic and copies ran while one was open for 0% of the time, Pallas kernels for 5%

profile of v14, /device:TPU:0, one launch (start us, length us, event | category | flops | bytes accessed | tf_op | source)
XLA Modules:
  0.0 60.1 jit_solution(4172654231061475140)
XLA Ops:
  0.0 0.0 collective-permute-start.1
  0.0 0.5 collective-permute-start.2
  0.5 0.0 collective-permute-start.3
  0.5 0.5 collective-permute-start.4
  1.0 1.5 %spread.1 = bf16[64,32,128]{2,1,0:T(8,128)(2,1)} custom-call(bf16[4,2,512]{2,1,0:T(2,128)(2,1)} %q_ref.2), custom_call_target="tpu_custom_call" | custom-call | tf_op jit(solution)/shard_map/spread/pallas_call | solution.py:79
  2.6 11.5 %all-to-all-start = ((bf16[64,32,128]{2,1,0:T(8,128)(2,1)}), bf16[64,32,128]{2,1,0:T(8,128)(2,1)S(1)}, u32[]{:S(2)}, u32[]{:S(2)}) async-start(bf16[64,32,128]{2,1,0:T(8,128)(2,1)} %spread.1), calls=%async_computation | async-start | bytes 1048576 | tf_op jit(solution)/shard_map/all_to_all | solution.py:335
  14.1 0.1 collective-permute-start
  14.2 1.2 %collective-permute-done.refs_1_ = s32[4]{0:T(128)S(1)} collective-permute-done((s32[4]{0:T(128)}, s32[4]{0:T(128)S(1)}, u32[]{:S(2)}, u32[]{:S(2)}) %collective-permute-start) | collective-permute-done | bytes 48 | tf_op jit(solution)/shard_map/ppermute | solution.py:357
  15.4 0.0 copy-start.2
  15.4 0.7 %copy-done.2 = s32[32]{0:T(128)S(1)} copy-done((s32[32]{0:T(128)S(1)}, s32[32]{0:T(128)}, u32[]{:S(2)}) %copy-start.2) | copy-done | bytes 152
  16.1 0.0 copy-start.3
  16.1 0.7 %copy-done.3 = s32[4]{0:T(128)S(1)} copy-done((s32[4]{0:T(128)S(1)}, s32[4]{0:T(128)}, u32[]{:S(2)}) %copy-start.3) | copy-done | bytes 40
  16.7 1.4 %locate.1.info = s32[24]{0:T(128)S(1)} custom-call(s32[32]{0:T(128)S(1)} %copy-done.2, s32[4]{0:T(128)S(1)} %copy-done.3, s32[4]{0:T(128)S(1)} %collective-permute-done.refs_1_), custom_call_target="tpu_custom_call" | custom-call | tf_op jit(solution)/shard_map/locate/pallas_call | solution.py:112
  18.1 9.6 %all-to-all-done = bf16[64,32,128]{2,1,0:T(8,128)(2,1)S(1)} async-done(((bf16[64,32,128]{2,1,0:T(8,128)(2,1)}), bf16[64,32,128]{2,1,0:T(8,128)(2,1)S(1)}, u32[]{:S(2)}, u32[]{:S(2)}) %all-to-all-start) | async-done | bytes 524320 | tf_op jit(solution)/shard_map/all_to_all | solution.py:335
  27.7 0.0 collective-permute-done.1.refs_4_
  27.7 0.0 collective-permute-done.2.refs_5_
  27.7 0.0 collective-permute-done.3.refs_6_
  27.7 0.0 collective-permute-done.4.refs_7_
  27.7 0.0 copy-start
  27.7 0.0 copy-start.1
  27.7 12.8 %attend.1 = bf16[4,16,40,128]{3,2,1,0:T(8,128)(2,1)} custom-call(s32[24]{0:T(128)S(1)} %locate.1.info, bf16[4,8,64,128]{3,2,1,0:T(8,128)(2,1)S(1)} %bitcast.2, bf16[1024,1024]{1,0:T(8,128)(2,1)} %refs_0_.3, bf16[1024,1024]{1,0:T(8,128)(2,1)} %refs_1_.1, bf16[4,256,1024]{2,1,0:T(8,128)(2,1)} %refs_2_.1, bf16[4,256,1024]{2,1,0:T(8,128)(2,1)} %refs_3_.1, ...), custom_call_target="tpu_custom_call" | custom-call | tf_op jit(solution)/shard_map/attend/pallas_call | solution.py:240
  40.5 4.7 %all-to-all-start.1 = ((bf16[64,40,128]{2,1,0:T(8,128)(2,1)}), bf16[64,40,128]{2,1,0:T(8,128)(2,1)S(1)}, u32[]{:S(2)}, u32[]{:S(2)}) async-start(bf16[64,40,128]{2,1,0:T(8,128)(2,1)} %bitcast.1), calls=%async_computation.1 | async-start | bytes 1310720 | tf_op jit(solution)/shard_map/all_to_all | solution.py:335
  45.2 0.0 copy-done
  45.2 0.0 copy-done.1
  45.2 0.1 new_tokens.1
  45.3 13.6 %all-to-all-done.1.parts_ref = bf16[64,40,128]{2,1,0:T(8,128)(2,1)S(1)} async-done(((bf16[64,40,128]{2,1,0:T(8,128)(2,1)}), bf16[64,40,128]{2,1,0:T(8,128)(2,1)S(1)}, u32[]{:S(2)}, u32[]{:S(2)}) %all-to-all-start.1) | async-done | bytes 655392 | tf_op jit(solution)/shard_map/all_to_all | solution.py:335
  58.9 1.2 %merge.1 = bf16[4,2,512]{2,1,0:T(2,128)(2,1)} custom-call(bf16[64,40,128]{2,1,0:T(8,128)(2,1)S(1)} %all-to-all-done.1.parts_ref, f32[2,4,8,128]{3,2,1,0:T(8,128)S(1)} %get-tuple-element.21.score_ref, f32[2,4,8,128]{3,2,1,0:T(8,128)S(1)} %get-tuple-element.22.value_ref), custom_call_target="tpu_custom_call" | custom-call | tf_op jit(solution)/shard_map/merge/pallas_call | solution.py:323
Async XLA Ops:
  0.0 27.7 %collective-permute-start.1 = (bf16[1024,1024]{1,0:T(8,128)(2,1)}, bf16[1024,1024]{1,0:T(8,128)(2,1)S(1)}, u32[]{:S(2)}, u32[]{:S(2)}) collective-permute-start(bf16[1024,1024]{1,0:T(8,128)(2,1)} %refs_0_.3), channel_id=1, source_target_pairs={{0,16},{16,0},{1,17},{17,1},{2,18},{18,2},{3,19},{19,3},{4,20},{20... | collective-permute-start | bytes 6291464 | tf_op jit(solution)/shard_map/ppermute | solution.py:355
  0.0 27.7 %collective-permute-start.2 = (bf16[1024,1024]{1,0:T(8,128)(2,1)}, bf16[1024,1024]{1,0:T(8,128)(2,1)}, u32[]{:S(2)}, u32[]{:S(2)}) collective-permute-start(bf16[1024,1024]{1,0:T(8,128)(2,1)} %refs_1_.1), channel_id=1, source_target_pairs={{0,16},{16,0},{1,17},{17,1},{2,18},{18,2},{3,19},{19,3},{4,20},{20... | collective-permute-start | bytes 6291464 | tf_op jit(solution)/shard_map/ppermute | solution.py:355
  0.5 27.2 %collective-permute-start.3 = (bf16[4,256,1024]{2,1,0:T(8,128)(2,1)}, bf16[4,256,1024]{2,1,0:T(8,128)(2,1)}, u32[]{:S(2)}, u32[]{:S(2)}) collective-permute-start(bf16[4,256,1024]{2,1,0:T(8,128)(2,1)} %refs_2_.1), channel_id=1, source_target_pairs={{0,16},{16,0},{1,17},{17,1},{2,18},{18,2},{3,19},{19,3},{4,20},{20... | collective-permute-start | bytes 6291464 | tf_op jit(solution)/shard_map/ppermute | solution.py:355
  0.5 27.2 %collective-permute-start.4 = (bf16[4,256,1024]{2,1,0:T(8,128)(2,1)}, bf16[4,256,1024]{2,1,0:T(8,128)(2,1)}, u32[]{:S(2)}, u32[]{:S(2)}) collective-permute-start(bf16[4,256,1024]{2,1,0:T(8,128)(2,1)} %refs_3_.1), channel_id=1, source_target_pairs={{0,16},{16,0},{1,17},{17,1},{2,18},{18,2},{3,19},{19,3},{4,20},{20... | collective-permute-start | bytes 6291464 | tf_op jit(solution)/shard_map/ppermute | solution.py:355
  2.6 25.1 %all-to-all-start = ((bf16[64,32,128]{2,1,0:T(8,128)(2,1)}), bf16[64,32,128]{2,1,0:T(8,128)(2,1)S(1)}, u32[]{:S(2)}, u32[]{:S(2)}) async-start(bf16[64,32,128]{2,1,0:T(8,128)(2,1)} %spread.1), calls=%async_computation | async-start | bytes 1048576 | tf_op jit(solution)/shard_map/all_to_all | solution.py:335
  14.1 1.3 %collective-permute-start = (s32[4]{0:T(128)}, s32[4]{0:T(128)S(1)}, u32[]{:S(2)}, u32[]{:S(2)}) collective-permute-start(s32[4]{0:T(128)} %refs_0_.2), channel_id=1, source_target_pairs={{0,16},{16,0},{1,17},{17,1},{2,18},{18,2},{3,19},{19,3},{4,20},{20... | collective-permute-start | bytes 56 | tf_op jit(solution)/shard_map/ppermute | solution.py:357
  15.4 0.7 %copy-start.2 = (s32[32]{0:T(128)S(1)}, s32[32]{0:T(128)}, u32[]{:S(2)}) copy-start(s32[32]{0:T(128)} %slot_ref) | copy-start | bytes 388
  16.1 0.7 %copy-start.3 = (s32[4]{0:T(128)S(1)}, s32[4]{0:T(128)}, u32[]{:S(2)}) copy-start(s32[4]{0:T(128)} %refs_0_.2) | copy-start | bytes 52
  27.7 17.5 %copy-start = (bf16[4,2,512]{2,1,0:T(2,128)(2,1)S(1)}, bf16[4,2,512]{2,1,0:T(2,128)(2,1)}, u32[]{:S(2)}) copy-start(bf16[4,2,512]{2,1,0:T(2,128)(2,1)} %q_ref.2) | copy-start | bytes 24580
  27.7 17.5 %copy-start.1 = (bf16[4,2,2,1024]{3,2,1,0:T(2,128)(2,1)S(1)}, bf16[4,2,2,1024]{3,2,1,0:T(2,128)(2,1)}, u32[]{:S(2)}) copy-start(bf16[4,2,2,1024]{3,2,1,0:T(2,128)(2,1)} %new_ref) | copy-start | bytes 98308
  40.5 18.4 %all-to-all-start.1 = ((bf16[64,40,128]{2,1,0:T(8,128)(2,1)}), bf16[64,40,128]{2,1,0:T(8,128)(2,1)S(1)}, u32[]{:S(2)}, u32[]{:S(2)}) async-start(bf16[64,40,128]{2,1,0:T(8,128)(2,1)} %bitcast.1), calls=%async_computation.1 | async-start | bytes 1310720 | tf_op jit(solution)/shard_map/all_to_all | solution.py:335

commit v15 on v14

--- a/solution.py
+++ b/solution.py
@@ -361,7 +361,7 @@
     info = locate(row_slot, (suffix_lengths, far_lengths), suffix_keys.shape[1])
     near, info = lax.optimization_barrier((near, info))
     near = near.reshape((layers, members) + near.shape[1:])
-    parts = attend(info, near, (own, far), 2, 128)
+    parts = attend(info, near, (own, far), 2, 256)
     parts, queries, new_kv = lax.optimization_barrier((parts, queries, new_kv))
     received = exchange(parts.reshape((chips,) + parts.shape[2:]), CHIPS)
     scores, values = new_tokens(queries, new_kv)

time: 60.5 us -> 60.2 us (level)
  no operation moved by 1% of the time
where the time goes in v15:
time: 60.2 us; the launch traced here: 59.8 us
  waiting for transfers between devices  24.4 us (41%)
  starting transfers between devices  17.3 us (29%)
  Pallas kernels  16.8 us (28%)
  local copies, waits for them, and re-layouts  1.32 us (2%)
    all_to_all x2, waiting for transfers between devices, exchange(): return lax.all_to_all(x, axes, split_axis=0, concat_axis=0, tiled=True)  23.2 us
    all_to_all x2, starting transfers between devices, exchange(): return lax.all_to_all(x, axes, split_axis=0, concat_axis=0, tiled=True)  16.2 us
    pallas_call x1, Pallas kernels, attend(): pl.pallas_call(functools.partial(attend_kernel, sides=len(caches), heads=...  12.5 us
    pallas_call x1, Pallas kernels, spread(): pl.pallas_call(spread_kernel, out_shape=jax.ShapeDtypeStruct((copies, que...  1.54 us
    pallas_call x1, Pallas kernels, locate(): pl.pallas_call(functools.partial(locate_kernel, span=span), in_specs=[sme...  1.4 us
    unnamed x8, local copies, waits for them, and re-layouts  1.32 us
    ppermute x1, waiting for transfers between devices, per_device(): far_lengths = lax.ppermute(suffix_lengths, 'core', swap)  1.24 us
    pallas_call x1, Pallas kernels, merge(): pl.pallas_call(merge_kernel, out_shape=jax.ShapeDtypeStruct(shape, jnp.bf...  1.22 us
  transfers between devices with their start and end apart: 7, of which 3 were waited for; matrix products, arithmetic and copies ran while one was open for 0% of the time, Pallas kernels for 5%

profile of v15, /device:TPU:0, one launch (start us, length us, event | category | flops | bytes accessed | tf_op | source)
XLA Modules:
  0.0 59.8 jit_solution(6416594780780044199)
XLA Ops:
  0.0 0.0 collective-permute-start.1
  0.0 0.5 collective-permute-start.2
  0.5 0.0 collective-permute-start.3
  0.5 0.5 collective-permute-start.4
  1.0 1.5 %spread.1 = bf16[64,32,128]{2,1,0:T(8,128)(2,1)} custom-call(bf16[4,2,512]{2,1,0:T(2,128)(2,1)} %q_ref.2), custom_call_target="tpu_custom_call" | custom-call | tf_op jit(solution)/shard_map/spread/pallas_call | solution.py:79
  2.6 11.5 %all-to-all-start = ((bf16[64,32,128]{2,1,0:T(8,128)(2,1)}), bf16[64,32,128]{2,1,0:T(8,128)(2,1)S(1)}, u32[]{:S(2)}, u32[]{:S(2)}) async-start(bf16[64,32,128]{2,1,0:T(8,128)(2,1)} %spread.1), calls=%async_computation | async-start | bytes 1048576 | tf_op jit(solution)/shard_map/all_to_all | solution.py:335
  14.1 0.1 collective-permute-start
  14.2 1.2 %collective-permute-done.refs_1_ = s32[4]{0:T(128)S(1)} collective-permute-done((s32[4]{0:T(128)}, s32[4]{0:T(128)S(1)}, u32[]{:S(2)}, u32[]{:S(2)}) %collective-permute-start) | collective-permute-done | bytes 48 | tf_op jit(solution)/shard_map/ppermute | solution.py:357
  15.4 0.0 copy-start.2
  15.4 0.7 %copy-done.2 = s32[32]{0:T(128)S(1)} copy-done((s32[32]{0:T(128)S(1)}, s32[32]{0:T(128)}, u32[]{:S(2)}) %copy-start.2) | copy-done | bytes 152
  16.1 0.0 copy-start.3
  16.1 0.7 %copy-done.3 = s32[4]{0:T(128)S(1)} copy-done((s32[4]{0:T(128)S(1)}, s32[4]{0:T(128)}, u32[]{:S(2)}) %copy-start.3) | copy-done | bytes 40
  16.7 1.4 %locate.1.info = s32[24]{0:T(128)S(1)} custom-call(s32[32]{0:T(128)S(1)} %copy-done.2, s32[4]{0:T(128)S(1)} %copy-done.3, s32[4]{0:T(128)S(1)} %collective-permute-done.refs_1_), custom_call_target="tpu_custom_call" | custom-call | tf_op jit(solution)/shard_map/locate/pallas_call | solution.py:112
  18.1 9.6 %all-to-all-done = bf16[64,32,128]{2,1,0:T(8,128)(2,1)S(1)} async-done(((bf16[64,32,128]{2,1,0:T(8,128)(2,1)}), bf16[64,32,128]{2,1,0:T(8,128)(2,1)S(1)}, u32[]{:S(2)}, u32[]{:S(2)}) %all-to-all-start) | async-done | bytes 524320 | tf_op jit(solution)/shard_map/all_to_all | solution.py:335
  27.7 0.0 collective-permute-done.1.refs_4_
  27.7 0.0 collective-permute-done.2.refs_5_
  27.7 0.0 collective-permute-done.3.refs_6_
  27.7 0.0 collective-permute-done.4.refs_7_
  27.7 0.0 copy-start
  27.7 0.0 copy-start.1
  27.7 12.5 %attend.1 = bf16[4,16,40,128]{3,2,1,0:T(8,128)(2,1)} custom-call(s32[24]{0:T(128)S(1)} %locate.1.info, bf16[4,8,64,128]{3,2,1,0:T(8,128)(2,1)S(1)} %bitcast.2, bf16[1024,1024]{1,0:T(8,128)(2,1)} %refs_0_.3, bf16[1024,1024]{1,0:T(8,128)(2,1)} %refs_1_.1, bf16[4,256,1024]{2,1,0:T(8,128)(2,1)} %refs_2_.1, bf16[4,256,1024]{2,1,0:T(8,128)(2,1)} %refs_3_.1, ...), custom_call_target="tpu_custom_call" | custom-call | tf_op jit(solution)/shard_map/attend/pallas_call | solution.py:240
  40.2 4.7 %all-to-all-start.1 = ((bf16[64,40,128]{2,1,0:T(8,128)(2,1)}), bf16[64,40,128]{2,1,0:T(8,128)(2,1)S(1)}, u32[]{:S(2)}, u32[]{:S(2)}) async-start(bf16[64,40,128]{2,1,0:T(8,128)(2,1)} %bitcast.1), calls=%async_computation.1 | async-start | bytes 1310720 | tf_op jit(solution)/shard_map/all_to_all | solution.py:335
  44.9 0.0 copy-done
  44.9 0.0 copy-done.1
  44.9 0.1 new_tokens.1
  45.0 13.6 %all-to-all-done.1.parts_ref = bf16[64,40,128]{2,1,0:T(8,128)(2,1)S(1)} async-done(((bf16[64,40,128]{2,1,0:T(8,128)(2,1)}), bf16[64,40,128]{2,1,0:T(8,128)(2,1)S(1)}, u32[]{:S(2)}, u32[]{:S(2)}) %all-to-all-start.1) | async-done | bytes 655392 | tf_op jit(solution)/shard_map/all_to_all | solution.py:335
  58.6 1.2 %merge.1 = bf16[4,2,512]{2,1,0:T(2,128)(2,1)} custom-call(bf16[64,40,128]{2,1,0:T(8,128)(2,1)S(1)} %all-to-all-done.1.parts_ref, f32[2,4,8,128]{3,2,1,0:T(8,128)S(1)} %get-tuple-element.21.score_ref, f32[2,4,8,128]{3,2,1,0:T(8,128)S(1)} %get-tuple-element.22.value_ref), custom_call_target="tpu_custom_call" | custom-call | tf_op jit(solution)/shard_map/merge/pallas_call | solution.py:323
Async XLA Ops:
  0.0 27.7 %collective-permute-start.1 = (bf16[1024,1024]{1,0:T(8,128)(2,1)}, bf16[1024,1024]{1,0:T(8,128)(2,1)S(1)}, u32[]{:S(2)}, u32[]{:S(2)}) collective-permute-start(bf16[1024,1024]{1,0:T(8,128)(2,1)} %refs_0_.3), channel_id=1, source_target_pairs={{0,16},{16,0},{1,17},{17,1},{2,18},{18,2},{3,19},{19,3},{4,20},{20... | collective-permute-start | bytes 6291464 | tf_op jit(solution)/shard_map/ppermute | solution.py:355
  0.0 27.7 %collective-permute-start.2 = (bf16[1024,1024]{1,0:T(8,128)(2,1)}, bf16[1024,1024]{1,0:T(8,128)(2,1)}, u32[]{:S(2)}, u32[]{:S(2)}) collective-permute-start(bf16[1024,1024]{1,0:T(8,128)(2,1)} %refs_1_.1), channel_id=1, source_target_pairs={{0,16},{16,0},{1,17},{17,1},{2,18},{18,2},{3,19},{19,3},{4,20},{20... | collective-permute-start | bytes 6291464 | tf_op jit(solution)/shard_map/ppermute | solution.py:355
  0.5 27.2 %collective-permute-start.3 = (bf16[4,256,1024]{2,1,0:T(8,128)(2,1)}, bf16[4,256,1024]{2,1,0:T(8,128)(2,1)}, u32[]{:S(2)}, u32[]{:S(2)}) collective-permute-start(bf16[4,256,1024]{2,1,0:T(8,128)(2,1)} %refs_2_.1), channel_id=1, source_target_pairs={{0,16},{16,0},{1,17},{17,1},{2,18},{18,2},{3,19},{19,3},{4,20},{20... | collective-permute-start | bytes 6291464 | tf_op jit(solution)/shard_map/ppermute | solution.py:355
  0.5 27.2 %collective-permute-start.4 = (bf16[4,256,1024]{2,1,0:T(8,128)(2,1)}, bf16[4,256,1024]{2,1,0:T(8,128)(2,1)}, u32[]{:S(2)}, u32[]{:S(2)}) collective-permute-start(bf16[4,256,1024]{2,1,0:T(8,128)(2,1)} %refs_3_.1), channel_id=1, source_target_pairs={{0,16},{16,0},{1,17},{17,1},{2,18},{18,2},{3,19},{19,3},{4,20},{20... | collective-permute-start | bytes 6291464 | tf_op jit(solution)/shard_map/ppermute | solution.py:355
  2.6 25.1 %all-to-all-start = ((bf16[64,32,128]{2,1,0:T(8,128)(2,1)}), bf16[64,32,128]{2,1,0:T(8,128)(2,1)S(1)}, u32[]{:S(2)}, u32[]{:S(2)}) async-start(bf16[64,32,128]{2,1,0:T(8,128)(2,1)} %spread.1), calls=%async_computation | async-start | bytes 1048576 | tf_op jit(solution)/shard_map/all_to_all | solution.py:335
  14.1 1.3 %collective-permute-start = (s32[4]{0:T(128)}, s32[4]{0:T(128)S(1)}, u32[]{:S(2)}, u32[]{:S(2)}) collective-permute-start(s32[4]{0:T(128)} %refs_0_.2), channel_id=1, source_target_pairs={{0,16},{16,0},{1,17},{17,1},{2,18},{18,2},{3,19},{19,3},{4,20},{20... | collective-permute-start | bytes 56 | tf_op jit(solution)/shard_map/ppermute | solution.py:357
  15.4 0.7 %copy-start.2 = (s32[32]{0:T(128)S(1)}, s32[32]{0:T(128)}, u32[]{:S(2)}) copy-start(s32[32]{0:T(128)} %slot_ref) | copy-start | bytes 388
  16.1 0.7 %copy-start.3 = (s32[4]{0:T(128)S(1)}, s32[4]{0:T(128)}, u32[]{:S(2)}) copy-start(s32[4]{0:T(128)} %refs_0_.2) | copy-start | bytes 52
  27.7 17.2 %copy-start = (bf16[4,2,512]{2,1,0:T(2,128)(2,1)S(1)}, bf16[4,2,512]{2,1,0:T(2,128)(2,1)}, u32[]{:S(2)}) copy-start(bf16[4,2,512]{2,1,0:T(2,128)(2,1)} %q_ref.2) | copy-start | bytes 24580
  27.7 17.2 %copy-start.1 = (bf16[4,2,2,1024]{3,2,1,0:T(2,128)(2,1)S(1)}, bf16[4,2,2,1024]{3,2,1,0:T(2,128)(2,1)}, u32[]{:S(2)}) copy-start(bf16[4,2,2,1024]{3,2,1,0:T(2,128)(2,1)} %new_ref) | copy-start | bytes 98308
  40.2 18.4 %all-to-all-start.1 = ((bf16[64,40,128]{2,1,0:T(8,128)(2,1)}), bf16[64,40,128]{2,1,0:T(8,128)(2,1)S(1)}, u32[]{:S(2)}, u32[]{:S(2)}) async-start(bf16[64,40,128]{2,1,0:T(8,128)(2,1)} %bitcast.1), calls=%async_computation.1 | async-start | bytes 1310720 | tf_op jit(solution)/shard_map/all_to_all | solution.py:335
